TPU v7x, 32 devices: a whole 2x2x4 slice. The times are simulated.
32 devices in a mesh: segment: 4 (over y, core), ha: 4 (over z), wa: 2 (over x).
Axes of the slice: x: 2, y: 2, z: 4, core: 2. Of those that a mesh axis runs over, the one named last changes fastest.
Arguments:
- latent: bfloat16 [4, 8, 1536], P(None, 'ha', 'wa'), may hold values from -6 to 6
- cache_a: bfloat16 [2, 8, 1536], P(None, 'ha', 'wa'), may hold values from -6 to 6
- cache_b: bfloat16 [2, 16, 1536], P(None, 'ha', 'wa'), may hold values from -4 to 4
- cache_c: bfloat16 [2, 32, 3072], P(None, 'ha', 'wa'), may hold values from -4 to 4
- cache_d: bfloat16 [2, 64, 3072], P(None, 'ha', 'wa'), may hold values from -4 to 4
- conv_pack: bfloat16 [4, 10368, 384], P('segment', 'ha', 'wa'), as said below
- up_pack: bfloat16 [4, 384, 1728], P('segment', 'wa', 'ha'), as said below
Outputs:
- decoded: bfloat16 [4, 128, 6144], P('segment', 'ha', 'wa')
Inputs may be any that keep to these rules, and one draw needn't show every extreme that they name: `conv_pack`: rows past 27 cin and columns other than multiples of 384 / cm in a section's row are not read. `up_pack`: rows other than multiples of 384 / cm and columns past 9 co in a section's row are not read.
All inputs are finite; a program needn't handle non-finite values.
Results may differ from a plain program's by a relative error of at most 0.018.
Values may be sent and summed in bfloat16 or wider, within the bound.
No kernel may reach another device: no remote copies, remote signals or barrier semaphores. Data moves between devices by JAX's collectives and lax.ppermute only.
A program may use at most 192 MiB of HBM per device.

v0:
```python
from functools import partial

import jax
import jax.numpy as jnp
from jax import lax
from jax.experimental import pallas as pl
from jax.experimental.pallas import tpu as pltpu
from jax.sharding import PartitionSpec as P

WIDE = 384
MID = 192
NARROW = 96


EPSILON = 1e-06


def shortened(array):

    def short(part):
        return part.astype(jnp.bfloat16) if part.dtype == jnp.float32 else part

    return jax.tree.map(short, array)


def passed_along(value, axis, steps):
    count = lax.axis_size(axis)
    initial, last = (max(0, -steps), min(count, count - steps))
    return lax.ppermute(value, axis, [(source, source + steps) for source in range(initial, last)])


def layer_table():
    return ((WIDE, WIDE, MID), (MID, WIDE, MID), (MID, MID, NARROW), (NARROW, NARROW, NARROW))


def round_up(amount):
    return -(-amount // 128) * 128


def volume(target):
    amount = 1
    for extent in target:
        amount = amount * extent
    return amount


def flat_pad(tensor, length):
    leading = tensor.shape[0]
    packed = tensor.reshape(leading, -1)
    return jnp.pad(packed, ((0, 0), (0, length - packed.shape[1])))


def reshaped(packed, target):
    return packed[:, : volume(target)].reshape((packed.shape[0],) + tuple(target))


def add_rows(tensor, from_above, from_below):
    leading, height, width, channels = tensor.shape
    upper = reshaped(from_above, (1, width, channels))
    lower = reshaped(from_below, (1, width, channels))
    return jnp.concatenate([upper, tensor, lower], axis=1)


def add_cols(tensor, from_left, from_right):
    leading, height, width, channels = tensor.shape
    before = reshaped(from_left, (height, 1, channels))
    after = reshaped(from_right, (height, 1, channels))
    return jnp.concatenate([before, tensor, after], axis=2)


def trade_rows(upper_rim, bottom):
    return (
        jax.tree.map(
            lambda part, own: part.astype(own.dtype),
            passed_along(shortened(bottom), "ha", 1),
            bottom,
        ),
        jax.tree.map(
            lambda part, own: part.astype(own.dtype),
            passed_along(shortened(upper_rim), "ha", -1),
            upper_rim,
        ),
    )


def trade_cols(left_rim, right_rim):
    return (
        jax.tree.map(
            lambda part, own: part.astype(own.dtype),
            passed_along(shortened(right_rim), "wa", 1),
            right_rim,
        ),
        jax.tree.map(
            lambda part, own: part.astype(own.dtype),
            passed_along(shortened(left_rim), "wa", -1),
            left_rim,
        ),
    )


def causal_conv(stacked, kernel):
    result = lax.conv_general_dilated(
        stacked[None],
        kernel,
        (1, 1, 1),
        "VALID",
        dimension_numbers=("NDHWC", "DHWIO", "NDHWC"),
        preferred_element_type=jnp.float32,
    )
    return result[0, 0]


def activate(conv_sum):
    inverse = lax.rsqrt(jnp.mean(conv_sum * conv_sum, axis=-1, keepdims=True) + EPSILON)
    return jax.nn.silu(conv_sum * inverse).astype(jnp.bfloat16)


def upsample_conv(hidden_ext, kernel):
    expanded = jnp.repeat(jnp.repeat(hidden_ext, 2, axis=0), 2, axis=1)[1:-1, 1:-1]
    result = lax.conv_general_dilated(
        expanded[None],
        kernel,
        (1, 1),
        "VALID",
        dimension_numbers=("NHWC", "HWIO", "NHWC"),
        preferred_element_type=jnp.float32,
    )
    return result[0].astype(jnp.bfloat16)


def per_device(latent, cache_a, cache_b, cache_c, cache_d, conv_pack, up_pack):
    frames = latent.shape[0]
    tile_rows = latent.shape[1]
    tile_cols = latent.shape[2] // WIDE
    layers = layer_table()
    section = lax.axis_index("segment")
    segments = lax.axis_size("segment")
    final_segment = segments - 1
    input_shapes = [
        (tile_rows << level, tile_cols << level, layers[level][0]) for level in range(4)
    ]
    mid_shapes = [(tile_rows << level, tile_cols << level, layers[level][1]) for level in range(4)]
    out_shapes = [
        (tile_rows << level + 1, tile_cols << level + 1, layers[level][2]) for level in range(4)
    ]
    ext_shapes = [(target[0] + 2, target[1] + 2, target[2]) for target in input_shapes]
    all_shapes = input_shapes + mid_shapes
    row_length = round_up(max((target[1] * target[2] for target in all_shapes)))
    column_length = round_up(max(((target[0] + 2) * target[2] for target in all_shapes)))
    size_input = round_up(max((volume(target) for target in input_shapes)))
    size_middle = round_up(max((volume(target) for target in mid_shapes)))
    size_extended = round_up(max((volume(target) for target in ext_shapes)))
    size_output = round_up(max((volume(target) for target in out_shapes)))
    final_shape = out_shapes[3]
    final_count = volume(final_shape)
    conv_rows, up_rows = (
        lax.all_gather(conv_pack, "ha", axis=1, tiled=True),
        lax.all_gather(up_pack, "ha", axis=2, tiled=True),
    )
    conv_all, up_all = (
        lax.all_gather(conv_rows, "wa", axis=2, tiled=True),
        lax.all_gather(up_rows, "wa", axis=1, tiled=True),
    )

    def conv_kernel(level):
        width_in, width_mid, width_out = layers[level]
        columns = conv_all[0, : 27 * width_in, :: WIDE // width_mid]
        return columns.reshape(3, 3, 3, width_in, columns.shape[1])

    def up_kernel(level):
        width_in, width_mid, width_out = layers[level]
        rows_used = up_all[0, :: WIDE // width_mid, : 9 * width_out]
        return rows_used.reshape(width_mid, 3, 3, width_out).transpose(1, 2, 0, 3)

    conv_kernels = [conv_kernel(level) for level in range(4)]
    up_kernels = [up_kernel(level) for level in range(4)]

    def row_rims(packed, shapes):

        def rows_branch(level, packed):
            tensor = reshaped(packed, shapes[level])
            return (flat_pad(tensor[:, :1], row_length), flat_pad(tensor[:, -1:], row_length))

        upper_rim, bottom = lax.switch(
            section, [partial(rows_branch, level) for level in range(4)], packed
        )
        return trade_rows(upper_rim, bottom)

    def extend(packed, shapes):
        from_above, from_below = row_rims(packed, shapes)

        def cols_branch(level, packed, from_above, from_below):
            tensor = add_rows(reshaped(packed, shapes[level]), from_above, from_below)
            return (
                flat_pad(tensor[:, :, :1], column_length),
                flat_pad(tensor[:, :, -1:], column_length),
            )

        left_rim, right_rim = lax.switch(
            section,
            [partial(cols_branch, level) for level in range(4)],
            packed,
            from_above,
            from_below,
        )
        from_left, from_right = trade_cols(left_rim, right_rim)
        return (from_above, from_below, from_left, from_right)

    def assemble(packed, target, rims):
        tensor = add_rows(reshaped(packed, target), rims[0], rims[1])
        return add_cols(tensor, rims[2], rims[3])

    caches = (cache_a, cache_b, cache_c, cache_d)

    def cache_branch(level):
        return flat_pad(caches[level], size_input)

    cached = lax.switch(section, [partial(cache_branch, level) for level in range(4)])
    cache_rims = extend(cached, input_shapes)

    def store_branch(level, packed, rims):
        return flat_pad(assemble(packed, input_shapes[level], rims), size_extended)

    history = lax.switch(
        section, [partial(store_branch, level) for level in range(4)], cached, cache_rims
    )
    finished = jnp.zeros((frames, final_shape[0], final_shape[1] * final_shape[2]), jnp.bfloat16)
    stream = jnp.zeros((1, size_input), jnp.bfloat16)
    for moment in range(frames + segments - 1):
        if moment == 0:
            incoming = stream
        else:
            incoming = jax.tree.map(
                lambda part, own: part.astype(own.dtype),
                passed_along(shortened(stream), "segment", 1),
                stream,
            )
        frame_id = moment - section
        active = (frame_id >= 0) & (frame_id < frames)
        chosen = jnp.clip(frame_id, 0, frames - 1)
        picked = lax.dynamic_index_in_dim(latent, chosen, 0, keepdims=True)
        current = jnp.where(section == 0, flat_pad(picked, size_input), incoming)
        branch_id = jnp.where(active, section, 4)
        rims = extend(current, input_shapes)

        def conv_branch(level, current, history, rims):
            window = assemble(current, input_shapes[level], rims)
            earlier = reshaped(history, ext_shapes[level])
            hidden = activate(
                causal_conv(jnp.concatenate([earlier, window], axis=0), conv_kernels[level])
            )
            return (flat_pad(hidden[None], size_middle), flat_pad(window, size_extended))

        def spare_conv(current, history, rims):
            return (
                jnp.zeros((1, size_middle), jnp.bfloat16),
                jnp.zeros((1, size_extended), jnp.bfloat16),
            )

        hidden, window = lax.switch(
            branch_id,
            [partial(conv_branch, level) for level in range(4)] + [spare_conv],
            current,
            history,
            rims,
        )
        hidden_rims = extend(hidden, mid_shapes)

        def up_branch(level, hidden, hidden_rims):
            expanded = assemble(hidden, mid_shapes[level], hidden_rims)[0]
            return flat_pad(upsample_conv(expanded, up_kernels[level])[None], size_output)

        def spare_up(hidden, hidden_rims):
            return jnp.zeros((1, size_output), jnp.bfloat16)

        produced = lax.switch(
            branch_id,
            [partial(up_branch, level) for level in range(4)] + [spare_up],
            hidden,
            hidden_rims,
        )
        shifted = jnp.concatenate([history[1:], window], axis=0)
        history = jnp.where(active, shifted, history)
        stream = produced[:, :size_input]
        if moment >= final_segment:
            finished_id = moment - final_segment
            picture = produced[:, :final_count].reshape(
                1, final_shape[0], final_shape[1] * final_shape[2]
            )
            finished = finished.at[finished_id].set(picture[0])
    collected = lax.all_to_all(finished, "segment", split_axis=0, concat_axis=0, tiled=True)
    per_segment = frames // segments
    own_frame = collected[final_segment * per_segment : (final_segment + 1) * per_segment]
    return own_frame


AXES = ("segment", "ha", "wa")
VMEM = 60 * 1024 * 1024


def place(s, h, w):
    return (s * 4 + h) * 2 + w


def send(value, pairs):
    return lax.ppermute(value, AXES, [(place(*a), place(*b)) for a, b in pairs])


def square(segments, dh, dw):
    return [
        ((s, h, w), (s, h ^ dh, w ^ dw)) for s in segments for h in range(2) for w in range(2)
    ]


def kernel_call(body, out_shape, scratch, *args, copies=0, flops=10**9):
    return pl.pallas_call(
        body,
        out_shape=out_shape,
        in_specs=[pl.BlockSpec(memory_space=pltpu.SMEM)] + [pl.BlockSpec(memory_space=pl.ANY)] * (len(args) - 1),
        out_specs=jax.tree.map(lambda _: pl.BlockSpec(memory_space=pl.ANY), out_shape),
        scratch_shapes=scratch + [pltpu.SemaphoreType.DMA((copies,))],
        compiler_params=pltpu.CompilerParams(vmem_limit_bytes=VMEM),
        cost_estimate=pl.CostEstimate(flops=flops, bytes_accessed=4 * 10**6, transcendentals=0),
    )(*args)


def start_all(pairs, sems, first=0):
    copies = [pltpu.make_async_copy(a, b, sems.at[first + n]) for n, (a, b) in enumerate(pairs)]
    for copy in copies:
        copy.start()
    return copies


def wait_all(copies):
    for copy in copies:
        copy.wait()


def dot(a, b):
    return jnp.dot(a, b, preferred_element_type=jnp.float32)


def index_of(shape):
    return lax.broadcasted_iota(jnp.int32, shape, 0)


def silu(v):
    return v / (1.0 + jnp.exp(-v))


def shifts(base, pitch, width):
    n = base.shape[0]
    left, right = pltpu.roll(base, 1, 0), pltpu.roll(base, n - 1, 0)
    if pitch == width:
        column = index_of(base.shape) % pitch
        left = jnp.where(column == 0, 0.0, left)
        right = jnp.where(column == width - 1, 0.0, right)
    return left, base, right


def upsample(p_ref, t_ref, pitch, width, lanes):
    n = p_ref.shape[0]
    blocks = lanes // 128
    column = index_of((n, 128)) % pitch
    for block in range(blocks):

        def tap(dy, dx):
            at = (dy * 3 + dx) * lanes + block * 128
            return p_ref[:, at : at + 128]

        for b in range(2):
            rows = []
            for dy in range(3):
                middle = tap(dy, 1)
                if b == 0:
                    far = pltpu.roll(tap(dy, 0), 1, 0)
                    if pitch == width:
                        far = jnp.where(column == 0, 0.0, far)
                    rows.append(far + middle + tap(dy, 2))
                else:
                    far = pltpu.roll(tap(dy, 2), n - 1, 0)
                    if pitch == width:
                        far = jnp.where(column == width - 1, 0.0, far)
                    rows.append(tap(dy, 0) + middle + far)
            t_ref[block, pl.ds(b, n, stride=2), :] = pltpu.roll(rows[0], pitch, 0) + rows[1] + rows[2]
            t_ref[blocks + block, pl.ds(b, n, stride=2), :] = (
                rows[0] + rows[1] + pltpu.roll(rows[2], n - pitch, 0)
            )


def conv0_body(ids, g_any, k_any, out_any, g_ref, k_ref, gf, base, xx, acc, buf, out_ref, sems):
    s, h = ids[0], ids[1]

    @pl.when(s == 0)
    def _():
        coming = start_all([(g_any, g_ref), (k_any, k_ref)], sems)
        base[...] = jnp.zeros_like(base)
        coming[0].wait()
        gf[...] = g_ref[...].astype(jnp.float32)
        for frame in range(6):
            for hh in range(4):
                for ww in range(2):
                    for r in range(2):
                        row = 8 + frame * 2 + r if frame < 2 else (frame - 2) * 2 + r
                        for c in range(2):
                            at = frame * 160 + (1 + 2 * hh + r) * 16 + 2 * ww + c
                            base[at : at + 1, :] = gf[hh * 2 + ww, row : row + 1, c * 384 : (c + 1) * 384]
        for dx, moved in enumerate(shifts(base[...], 16, 4)):
            xx[dx] = moved.astype(jnp.bfloat16)
        coming[1].wait()
        for part in range(4):

            @pl.when(h == part)
            def _():
                total = None
                at, end = part * 2592, part * 2592 + 2592
                while at < end:
                    tap, c0 = divmod(at, 384)
                    c1 = min(384, c0 + end - at)
                    dt, dy, dx = tap // 9, tap // 3 % 3, tap % 3
                    start = dt * 160 + dy * 16
                    k0 = at - part * 2592
                    term = dot(xx[dx, start : start + 608, c0:c1], k_ref[k0 : k0 + c1 - c0, :])
                    total = term if total is None else total + term
                    at += c1 - c0
                acc[...] = total

        for frame in range(4):
            for r in range(8):
                to, at = (frame * 8 + r) * 4, frame * 160 + r * 16
                buf[to : to + 4, :] = acc[at : at + 4, :]
        out_ref[...] = buf[...].astype(jnp.bfloat16)
        wait_all(start_all([(out_ref, out_any)], sems))


def conv0(ids, gathered, k):
    f32, bf16 = jnp.float32, jnp.bfloat16
    return kernel_call(
        conv0_body,
        jax.ShapeDtypeStruct((128, 192), bf16),
        [
            pltpu.VMEM((8, 20, 768), bf16),
            pltpu.VMEM((2592, 192), bf16),
            pltpu.VMEM((8, 20, 768), f32),
            pltpu.VMEM((960, 384), f32),
            pltpu.VMEM((3, 960, 384), bf16),
            pltpu.VMEM((608, 192), f32),
            pltpu.VMEM((128, 192), f32),
            pltpu.VMEM((128, 192), bf16),
        ],
        ids, gathered, k,
        copies=2,
    )


def join_taps(h, pieces_own, pieces_z, cat_ref, taps_ref, width, lanes):
    for z in range(2):

        @pl.when(h == z)
        def _():
            for mine, pieces in ((z, pieces_own), (1 - z, pieces_z)):
                for number, piece in enumerate(pieces):
                    at = (mine + 2 * number) * 432
                    cat_ref[:, at : at + 432] = piece

    for tap in range(9):
        taps_ref[:, tap * lanes : tap * lanes + width] = cat_ref[:, tap * width : (tap + 1) * width]


def up0_body(ids, y_any, own_any, z_any, x_any, d_any, out_any, y_ref, own, nz, nx, nd, cat, taps, hbuf, hs, p, t,
             out_ref, sems):
    s, h, w = ids[0], ids[1], ids[2]

    @pl.when((s == 0) & (h < 2))
    def _():
        coming = start_all([(y_any, y_ref), (own_any, own), (z_any, nz), (x_any, nx), (d_any, nd)], sems)
        coming[0].wait()
        halves = []
        for ww in range(2):
            total = y_ref[ww].astype(jnp.float32)
            for hh in range(1, 4):
                total = total + y_ref[hh * 2 + ww].astype(jnp.float32)
            halves.append(total)
        squares = sum(jnp.sum(half * half, axis=1, keepdims=True) for half in halves)
        inverse = lax.rsqrt(squares / 384.0 + EPSILON)
        active = [silu(half * inverse) for half in halves]
        hs[...] = jnp.zeros_like(hs)
        for k in range(2):
            hbuf[...] = jnp.where(w == k, active[0], active[1])
            for frame in range(4):
                for r in range(8):
                    to, at = frame * 72 + r * 8, (frame * 8 + r) * 4
                    hs[k, to : to + 4, :] = hbuf[at : at + 4, :]
        wait_all(coming[1:])
        for k, (mine, other) in enumerate(((own, nz), (nx, nd))):
            join_taps(h, (mine[0:192], mine[192:384]), (other[0:192], other[192:384]), cat, taps, 192, 256)
            term = dot(hs[k].astype(jnp.bfloat16), taps[...])
            if k == 0:
                p[...] = term
            else:
                p[...] = p[...] + term
        upsample(p, t, 8, 4, 256)
        column = index_of((16, 192))
        out_ref[...] = jnp.zeros_like(out_ref)
        for z in range(2):

            @pl.when(h == z)
            def _():
                for frame in range(4):
                    for r in range(11):
                        y = r + 5 * z
                        at = frame * 144 + (y // 2) * 16
                        to = frame * 192 + (r + 1 - z) * 16
                        for lane, count in ((0, 128), (128, 64)):
                            row = t[y % 2 * 2 + lane // 128, at : at + 16, 0:count]
                            row = jnp.where(column[:, 0:count] < 8, row, 0.0)
                            out_ref[to : to + 16, lane : lane + count] = row.astype(jnp.bfloat16)

        wait_all(start_all([(out_ref, out_any)], sems))


def up0(ids, partials, ups):
    f32, bf16 = jnp.float32, jnp.bfloat16
    return kernel_call(
        up0_body,
        jax.ShapeDtypeStruct((768, 192), bf16),
        [
            pltpu.VMEM((8, 128, 192), bf16),
            *[pltpu.VMEM((384, 432), bf16)] * 4,
            pltpu.VMEM((192, 1728), bf16),
            pltpu.VMEM((192, 2304), bf16),
            pltpu.VMEM((128, 192), f32),
            pltpu.VMEM((2, 288, 192), f32),
            pltpu.VMEM((288, 2304), f32),
            pltpu.VMEM((4, 576, 128), f32),
            pltpu.VMEM((768, 192), bf16),
        ],
        ids, partials, *ups,
        copies=5,
    )


def group_rows(first, second, group):
    parts, at, end = [], group * 576, group * 576 + 576
    while at < end:
        quarter, row = divmod(at, 1296)
        count = min(1296 - row, end - at)
        source = (first, second)[quarter // 2]
        lane = quarter % 2 * 192
        parts.append(source[row : row + count, lane : lane + 192])
        at += count
    return parts[0] if len(parts) == 1 else jnp.concatenate(parts, axis=0)


def section1_body(ids, x_any, g_any, *refs):
    kernels_any, ups_any, out_any = refs[0:8], refs[8:12], refs[12]
    x_ref, g_ref = refs[13:15]
    k_own, k_z, k_x, k_d, own, nz, nx, nd = refs[15:23]
    gf, full, base, xx, acc, hs, cat, taps, p, t, out_ref, sems = refs[23:]
    s, h, w = ids[0], ids[1], ids[2]

    @pl.when((s == 1) & (h < 2))
    def _():
        coming = start_all([(x_any, x_ref), (g_any, g_ref)], sems)
        pairs = []
        for number, piece in enumerate((k_own, k_z, k_x, k_d)):
            pairs.append((kernels_any[2 * number], piece.at[0:640]))
            pairs.append((kernels_any[2 * number + 1], piece.at[640:1296]))
        arriving = start_all(pairs, sems, 2)
        rising = start_all(list(zip(ups_any, (own, nz, nx, nd))), sems, 10)
        wait_all(coming)

        @pl.when(w == 0)
        def _():
            gf[...] = g_ref[...].astype(jnp.float32)
            full[...] = jnp.zeros_like(full)
            for frame in range(2):
                for hh in range(4):
                    for ww in range(2):
                        for r in range(4):
                            for c in range(4):
                                row = 12 + frame * 4 + r
                                at = frame * 288 + (1 + hh * 4 + r) * 16 + ww * 4 + c
                                full[at : at + 1, :] = gf[hh * 2 + ww, row : row + 1, c * 192 : (c + 1) * 192]
            for frame in range(2):
                start = pl.multiple_of(frame * 288 + h * 96, 32)
                base[frame * 192 : (frame + 1) * 192] = full[pl.ds(start, 192), :]
            base[384:768] = x_ref[0:384].astype(jnp.float32)

        @pl.when(w == 1)
        def _():
            base[...] = x_ref[...].astype(jnp.float32)

        for dx, moved in enumerate(shifts(base[...], 16, 8)):
            xx[:, dx * 192 : (dx + 1) * 192] = moved.astype(jnp.bfloat16)
        wait_all(arriving)
        for z in range(2):

            @pl.when(h == z)
            def _():
                for k, (mine, other) in enumerate(((k_own, k_z), (k_x, k_d))):
                    first, second = (mine, other) if z == 0 else (other, mine)
                    total = None
                    for group in range(9):
                        start = group // 3 * 192 + group % 3 * 16
                        term = dot(xx[start : start + 352, :], group_rows(first, second, group))
                        total = term if total is None else total + term
                    acc[k] = total

        squares = sum(jnp.sum(acc[k] * acc[k], axis=1, keepdims=True) for k in range(2))
        inverse = lax.rsqrt(squares / 384.0 + EPSILON)
        index = index_of((352, 192))
        keep = (index % 192 < 160) & (index % 16 < 8)
        for k in range(2):
            hs[k, 0:352] = jnp.where(keep, silu(acc[k] * inverse), 0.0).astype(jnp.bfloat16)
            hs[k, 352:384] = jnp.zeros((32, 192), jnp.bfloat16)
        wait_all(rising)
        for k, (mine, other) in enumerate(((own, nz), (nx, nd))):
            join_taps(h, (mine[0:192], mine[192:384]), (other[0:192], other[192:384]), cat, taps, 192, 256)
            term = dot(hs[k], taps[...])
            if k == 0:
                p[...] = term
            else:
                p[...] = p[...] + term
        upsample(p, t, 16, 8, 256)
        out_ref[...] = jnp.zeros_like(out_ref)
        for z in range(2):

            @pl.when(h == z)
            def _():
                for frame in range(2):
                    for r in range(19):
                        y = r + z
                        at = frame * 384 + (y // 2) * 32
                        to = (r + 1 - z) * 16
                        for lane, count in ((0, 128), (128, 64)):
                            row = t[y % 2 * 2 + lane // 128, at : at + 16, 0:count].astype(jnp.bfloat16)
                            lane0 = frame * 192 + lane
                            out_ref[to : to + 16, lane0 : lane0 + count] = row

        wait_all(start_all([(out_ref, out_any)], sems))


def section1(ids, frames, gathered, kernels, ups):
    f32, bf16 = jnp.float32, jnp.bfloat16
    return kernel_call(
        section1_body,
        jax.ShapeDtypeStruct((320, 384), bf16),
        [
            pltpu.VMEM((768, 192), bf16),
            pltpu.VMEM((8, 20, 768), bf16),
            *[pltpu.VMEM((1296, 384), bf16)] * 4,
            *[pltpu.VMEM((384, 432), bf16)] * 4,
            pltpu.VMEM((8, 20, 768), f32),
            pltpu.VMEM((576, 192), f32),
            pltpu.VMEM((768, 192), f32),
            pltpu.VMEM((768, 576), bf16),
            pltpu.VMEM((2, 352, 192), f32),
            pltpu.VMEM((2, 384, 192), bf16),
            pltpu.VMEM((192, 1728), bf16),
            pltpu.VMEM((192, 2304), bf16),
            pltpu.VMEM((384, 2304), f32),
            pltpu.VMEM((4, 768, 128), f32),
            pltpu.VMEM((320, 384), bf16),
        ],
        ids, frames, gathered, *kernels, *ups,
        copies=14,
    )


def pick(across, step, count, at):
    source = lax.broadcasted_iota(jnp.int32, (192, 192), 1 if across else 0)
    target = lax.broadcasted_iota(jnp.int32, (192, 192), 0 if across else 1) - at
    return ((source == target * step) & (target >= 0) & (target < count)).astype(jnp.bfloat16)


def pack_body(ids, k_any, u_any, upper_any, lower_any, up_any, k, u, upper, lower, up, sems):
    s, w = ids[0], ids[2]
    bf16 = jnp.bfloat16
    coming = start_all([(k_any, k), (u_any, u)], sems)
    wait_all(coming)

    @pl.when(s < 2)
    def _():
        for half in range(2):
            lane = half * 192
            upper[:, lane : lane + 192] = k[half * 1296 : half * 1296 + 640]
            lower[:, lane : lane + 192] = k[half * 1296 + 640 : half * 1296 + 1296]
        up[...] = u[...]

    for level, step, count in ((2, 2, 96), (3, 4, 48)):

        @pl.when(s == level)
        def _():
            columns = pick(False, step, count, w * count)
            for half in range(2):
                lane = half * 192
                upper[:, lane : lane + 192] = dot(k[half * 1296 : half * 1296 + 640], columns).astype(bf16)
                lower[:, lane : lane + 192] = dot(k[half * 1296 + 640 : half * 1296 + 1296], columns).astype(bf16)
            up[...] = dot(pick(True, step, count, w * count), u[...]).astype(bf16)

    wait_all(start_all([(upper, upper_any), (lower, lower_any), (up, up_any)], sems))


def pack(ids, k, u):
    bf16 = jnp.bfloat16
    shapes = ((640, 384), (656, 384), (192, 432))
    return kernel_call(
        pack_body,
        tuple(jax.ShapeDtypeStruct(shape, bf16) for shape in shapes),
        [pltpu.VMEM((2592, 192), bf16), pltpu.VMEM((192, 432), bf16)] + [pltpu.VMEM(shape, bf16) for shape in shapes],
        ids, k, u,
        copies=3,
    )


def merge_body(ids, *refs):
    kernels_any, ups_any, (k2_any, k3_any, up_any) = refs[0:8], refs[8:12], refs[12:15]
    pieces, ups = refs[15:19], refs[19:23]
    k2, wide, k3, cat, up, sems = refs[23:]
    s, h = ids[0], ids[1]

    @pl.when((s >= 2) & (h < 2))
    def _():
        pairs = []
        for number, piece in enumerate(pieces):
            pairs.append((kernels_any[2 * number], piece.at[0:640]))
            pairs.append((kernels_any[2 * number + 1], piece.at[640:1296]))
        coming = start_all(pairs, sems)
        rising = start_all([(a.at[0:192], b) for a, b in zip(ups_any, ups)], sems, 8)
        wait_all(rising)
        for z in range(2):

            @pl.when(h == z)
            def _():
                cat[:, z * 432 : z * 432 + 432] = ups[0][...] + ups[2][...]
                cat[:, (1 - z) * 432 : (1 - z) * 432 + 432] = ups[1][...] + ups[3][...]

        up[...] = jnp.zeros_like(up)
        for tap in range(9):
            up[:, tap * 128 : tap * 128 + 96] = cat[:, tap * 96 : (tap + 1) * 96]
        wait_all(coming)
        own, nz, nx, nd = pieces

        @pl.when(s == 2)
        def _():
            for z in range(2):

                @pl.when(h == z)
                def _():
                    for part, (a, b) in enumerate(((own, nx), (nz, nd))):
                        part = part ^ z
                        for half in range(2):
                            at, lane = (part * 2 + half) * 1296, half * 192
                            k2[at : at + 1296, :] = a[:, lane : lane + 192] + b[:, lane : lane + 192]

            wait_all(start_all([(k2, k2_any)], sems))

        @pl.when(s == 3)
        def _():
            for z in range(2):

                @pl.when(h == z)
                def _():
                    a, b = ((own, nx), (nz, nd))[z]
                    for half in range(2):
                        lane = half * 192
                        rows = a[:, lane : lane + 128] + b[:, lane : lane + 128]
                        wide[half * 1296 : half * 1296 + 1296, :] = rows

            k3[...] = jnp.zeros_like(k3)
            for tap in range(27):
                k3[tap * 128 : tap * 128 + 96, :] = wide[tap * 96 : tap * 96 + 96, :]
            wait_all(start_all([(k3, k3_any)], sems))

        wait_all(start_all([(up, up_any)], sems))


def merge(ids, kernels, ups):
    bf16 = jnp.bfloat16
    shapes = ((5184, 192), (3456, 128), (192, 1152))
    return kernel_call(
        merge_body,
        tuple(jax.ShapeDtypeStruct(shape, bf16) for shape in shapes),
        [
            *[pltpu.VMEM((1296, 384), bf16)] * 4,
            *[pltpu.VMEM((192, 432), bf16)] * 4,
            pltpu.VMEM((5184, 192), bf16),
            pltpu.VMEM((2592, 128), bf16),
            pltpu.VMEM((3456, 128), bf16),
            pltpu.VMEM((192, 864), bf16),
            pltpu.VMEM((192, 1152), bf16),
        ],
        ids, *kernels, *ups,
        copies=12,
    )


def caches_body(ids, b0_any, b1_any, b2_any, c_any, d_any, bands, wide, c_full, d_full, c, d, sems):
    s, h, w = ids[0], ids[1], ids[2]
    f32, bf16 = jnp.float32, jnp.bfloat16

    @pl.when((s >= 2) & (h < 2))
    def _():
        wait_all(start_all([(a, bands.at[n]) for n, a in enumerate((b0_any, b1_any, b2_any))], sems))
        c_full[...] = jnp.zeros_like(c_full)
        d_full[...] = jnp.zeros_like(d_full)
        for band in range(3):
            wide[...] = bands[band].astype(f32)
            for side in range(2):
                swapped = (w + side) % 2
                for frame in range(2):
                    row = side * 48 + frame * 8
                    for column in range(8):
                        at = (frame * 26 + 1 + band * 8) * 16 + swapped * 8 + column
                        lane = column * 192
                        c_full[0, pl.ds(at, 8, stride=16), :] = wide[row : row + 8, lane : lane + 128]
                        tail = jnp.concatenate([wide[row : row + 8, lane + 128 : lane + 192]] * 2, axis=1)
                        c_full[1, pl.ds(at, 8, stride=16), :] = tail
                    row = side * 48 + 16 + frame * 16
                    for column in range(16):
                        at = (frame * 50 + 1 + band * 16) * 32 + swapped * 16 + column
                        lane = column * 96
                        part = wide[row : row + 16, lane : lane + 96]
                        part = jnp.concatenate([part, part[:, 0:32]], axis=1)
                        d_full[pl.ds(at, 16, stride=32), :] = part
        for frame in range(2):
            at = pl.multiple_of((frame * 26 + h * 6) * 16, 32)
            c[frame * 320 : frame * 320 + 320, 0:128] = c_full[0, pl.ds(at, 320), :].astype(bf16)
            c[frame * 320 : frame * 320 + 320, 128:192] = c_full[1, pl.ds(at, 320), 0:64].astype(bf16)
            at = pl.multiple_of((frame * 50 + h * 15) * 32, 32)
            d[frame * 1120 : frame * 1120 + 1120, :] = d_full[pl.ds(at, 1120), 0:96].astype(bf16)
        wait_all(start_all([(c, c_any), (d, d_any)], sems))


def caches(ids, bands):
    f32, bf16 = jnp.float32, jnp.bfloat16
    return kernel_call(
        caches_body,
        (jax.ShapeDtypeStruct((640, 192), bf16), jax.ShapeDtypeStruct((2240, 96), bf16)),
        [
            pltpu.VMEM((3, 96, 1536), bf16),
            pltpu.VMEM((96, 1536), f32),
            pltpu.VMEM((2, 832, 128), f32),
            pltpu.VMEM((3200, 128), f32),
            pltpu.VMEM((640, 192), bf16),
            pltpu.VMEM((2240, 96), bf16),
        ],
        ids, *bands,
        copies=3,
    )


def sections23_body(ids, same2, same3, other2, other3, c_any, d_any, k2_own, k2_sent, k3_own, k3_sent, u_own, u_sent,
                    out0, out1, out2, out3, pairs, d_ref, k2, k3, u2, u3, line, base, xx, hs, p, t, base3, xx3, hs3, p3, t3, out_ref,
                    sems):
    s, h, w = ids[0], ids[1], ids[2]
    f32, bf16 = jnp.float32, jnp.bfloat16

    @pl.when((s >= 2) & (h < 2))
    def _():
        frame = (s - 2) * 2 + w
        line[0:640] = jnp.zeros((640, 192), bf16)
        for segment, same, other in ((2, same2, other2), (3, same3, other3)):

            @pl.when(s == segment)
            def _():
                held2, held3 = (k2_own, k3_sent) if segment == 2 else (k2_sent, k3_own)
                up2, up3 = (u_own, u_sent) if segment == 2 else (u_sent, u_own)
                start_all(
                    [
                        (same, pairs.at[w]),
                        (other, pairs.at[1 - w]),
                        (c_any, line.at[640:1280]),
                        (held2, k2),
                        (up2, u2),
                        (d_any, d_ref),
                        (held3, k3),
                        (up3.at[0:96], u3),
                    ],
                    sems,
                )

        coming = [
            pltpu.make_async_copy(a, b, sems.at[n])
            for n, (a, b) in enumerate(
                [
                    (same2, pairs.at[0]),
                    (other2, pairs.at[1]),
                    (c_any, line.at[640:1280]),
                    (k2_own, k2),
                    (u_own, u2),
                    (d_any, d_ref),
                    (k3_own, k3),
                    (u_own.at[0:96], u3),
                ]
            )
        ]
        wait_all(coming[0:3])
        for number in range(2):
            for k in range(2):
                at = 1280 + (2 * number + k) * 320
                line[at : at + 320] = pairs[number, :, k * 192 : (k + 1) * 192]

        base[...] = line[pl.ds(pl.multiple_of(frame * 320, 320), 1600), :].astype(f32)
        for dx, moved in enumerate(shifts(base[...], 16, 16)):
            xx[:, dx * 192 : (dx + 1) * 192] = moved.astype(bf16)
        coming[3].wait()
        total = None
        for group in range(9):
            start = group // 3 * 320 + group % 3 * 16
            term = dot(xx[start : start + 928, :], k2[group * 576 : (group + 1) * 576, :])
            total = term if total is None else total + term
        inverse = lax.rsqrt(jnp.sum(total * total, axis=1, keepdims=True) / 192.0 + EPSILON)
        keep = index_of((928, 192)) % 320 < 288
        hs[0:928] = jnp.where(keep, silu(total * inverse), 0.0).astype(bf16)
        hs[928:960] = jnp.zeros((32, 192), bf16)
        coming[4].wait()
        p[...] = dot(hs[...], u2[...])
        upsample(p, t, 16, 16, 128)

        for z in range(2):

            @pl.when(h == z)
            def _():
                blank = 0 if z == 0 else 34
                for moment in range(3):
                    to = moment * 1120 + blank * 32
                    base3[to : to + 32] = jnp.zeros((32, 96), f32)
                    for r in range(34):
                        y = r + 2 * z
                        at = moment * 640 + (y // 2) * 32
                        to = moment * 1120 + (r + 1 - z) * 32
                        base3[to : to + 32] = t[y % 2, at : at + 32, 0:96].astype(bf16).astype(f32)

        wait_all(coming[5:8])

        @pl.when(frame == 0)
        def _():
            base3[0:2240] = d_ref[...].astype(f32)

        @pl.when(frame == 1)
        def _():
            base3[0:1120] = d_ref[1120:2240].astype(f32)

        xx3[...] = jnp.zeros_like(xx3)
        for dx, moved in enumerate(shifts(base3[...], 32, 32)):
            xx3[:, dx * 128 : dx * 128 + 96] = moved.astype(bf16)
        total = None
        for group in range(9):
            start = group // 3 * 1120 + group % 3 * 32
            term = dot(xx3[start : start + 1056, :], k3[group * 384 : (group + 1) * 384, 0:96])
            total = term if total is None else total + term
        inverse = lax.rsqrt(jnp.sum(total * total, axis=1, keepdims=True) / 96.0 + EPSILON)
        hs3[0:1056] = silu(total * inverse).astype(bf16)
        hs3[1056:1120] = jnp.zeros((64, 96), bf16)
        p3[...] = dot(hs3[...], u3[...])
        upsample(p3, t3, 32, 32, 128)
        for z in range(2):

            @pl.when(h == z)
            def _():
                for r in range(64):
                    y = r + 2 * z
                    row = t3[y % 2, (y // 2) * 64 : (y // 2) * 64 + 64, 0:96].astype(bf16)
                    for half in range(2):
                        at = r % 32 * 32
                        out_ref[r // 32 * 2 + half, at : at + 32, :] = row[half * 32 : half * 32 + 32]

        wait_all(start_all([(out_ref.at[n], target) for n, target in enumerate((out0, out1, out2, out3))], sems))


def sections23(ids, received, c, d, kernels):
    f32, bf16 = jnp.float32, jnp.bfloat16
    return kernel_call(
        sections23_body,
        tuple([jax.ShapeDtypeStruct((1024, 96), bf16)] * 4),
        [
            pltpu.VMEM((2, 320, 384), bf16),
            pltpu.VMEM((2240, 96), bf16),
            pltpu.VMEM((5184, 192), bf16),
            pltpu.VMEM((3456, 128), bf16),
            pltpu.VMEM((192, 1152), bf16),
            pltpu.VMEM((96, 1152), bf16),
            pltpu.VMEM((2560, 192), bf16),
            pltpu.VMEM((1600, 192), f32),
            pltpu.VMEM((1600, 576), bf16),
            pltpu.VMEM((960, 192), bf16),
            pltpu.VMEM((960, 1152), f32),
            pltpu.VMEM((2, 1920, 128), f32),
            pltpu.VMEM((3360, 96), f32),
            pltpu.VMEM((3360, 384), bf16),
            pltpu.VMEM((1120, 96), bf16),
            pltpu.VMEM((1120, 1152), f32),
            pltpu.VMEM((2, 2240, 128), f32),
            pltpu.VMEM((4, 1024, 96), bf16),
        ],
        ids, *received, c, d, *kernels,
        copies=8,
    )


def relay(latent, cache_a, cache_b, cache_c, cache_d, conv_pack, up_pack):
    s, h, w = (lax.axis_index(axis) for axis in AXES)
    ids = jnp.stack([s, h, w]).astype(jnp.int32)
    k = conv_pack[0]

    upper, lower, u = pack(ids, k, up_pack[0])
    later = (1, 2, 3)
    u_far = send(u, [((s_, h_ + 2, w_), (s_, h_, w_)) for s_ in (0, 1) for h_ in range(2) for w_ in range(2)])
    upper_z, lower_z = (send(part, square(later, 1, 0)) for part in (upper, lower))
    upper_x, lower_x = (send(part, square(later, 0, 1)) for part in (upper, lower))
    ups = jnp.concatenate([u, u_far], axis=0)
    u_z = send(ups, square(range(4), 1, 0))
    u_x = send(ups, square(range(4), 0, 1))
    u_d = send(u_z, square(range(4), 0, 1))
    upper_d = send(upper_z, square(later, 0, 1))
    lower_d = send(lower_x, square(later, 1, 0))
    kernels = (upper, lower, upper_z, lower_z, upper_x, lower_x, upper_d, lower_d)
    risers = (ups, u_z, u_x, u_d)

    tiles = jnp.concatenate([latent.reshape(8, 768), cache_a.reshape(4, 768), cache_b.reshape(8, 768)], axis=0)
    gathered = lax.all_to_all(
        jnp.broadcast_to(tiles[None], (8, 20, 768)), ("ha", "wa"), split_axis=0, concat_axis=0, tiled=True
    )
    partial_sums = conv0(ids, gathered, k)
    partials = lax.all_to_all(
        jnp.broadcast_to(partial_sums[None], (8, 128, 192)), ("ha", "wa"), split_axis=0, concat_axis=0, tiled=True
    )
    risen = up0(ids, partials, risers)
    given = send(risen, [((0, h_, w_), (1, h_, w_)) for h_ in range(2) for w_ in range(2)])

    out1 = section1(ids, given, gathered, kernels, risers)
    received = [
        send(out1, [((1, h_, w_), (s_, h_, w_ ^ dw)) for h_ in range(2) for w_ in range(2)])
        for dw in range(2)
        for s_ in (2, 3)
    ]

    k2, k3, u23 = merge(ids, kernels, risers)
    pairs = [((s_, h_, w_), (s_ ^ 1, h_, w_)) for s_ in (2, 3) for h_ in range(2) for w_ in range(2)]
    k2_sent = send(k2, [pair for pair in pairs if pair[0][0] == 2])
    k3_sent = send(k3, [pair for pair in pairs if pair[0][0] == 3])
    u_sent = send(u23, pairs)
    own = jnp.concatenate([cache_c.reshape(16, 1536), cache_d.reshape(32, 1536)], axis=0)
    beside = send(own, [((s_, h_, w_), (s_, h_, w_ ^ 1)) for s_ in (2, 3) for h_ in range(4) for w_ in range(2)])
    both = jnp.concatenate([own, beside], axis=0)
    bands = [both] + [
        send(both, [((s_, h_ + n, w_), (s_, h_, w_)) for s_ in (2, 3) for h_ in range(2) for w_ in range(2)])
        for n in (1, 2)
    ]
    c, d = caches(ids, bands)
    blocks = sections23(ids, received, c, d, (k2, k2_sent, k3, k3_sent, u23, u_sent))

    arrived = [
        send(
            blocks[2 * n + half],
            [((2 + c_, z, x), (2 * c_ + x, 2 * z + n, half)) for c_ in range(2) for z in range(2) for x in range(2)],
        )
        for n in range(2)
        for half in range(2)
    ]
    lower_half = jnp.where(w == 0, arrived[2], arrived[3])
    upper_half = jnp.where(w == 0, arrived[0], arrived[1])
    return jnp.where(h % 2 == 0, upper_half, lower_half).reshape(1, 32, 3072)


def solution(mesh):
    in_specs = (
        P(None, "ha", "wa"),
        P(None, "ha", "wa"),
        P(None, "ha", "wa"),
        P(None, "ha", "wa"),
        P(None, "ha", "wa"),
        P("segment", "ha", "wa"),
        P("segment", "wa", "ha"),
    )
    out_specs = P("segment", "ha", "wa")
    sizes = tuple(mesh.shape[axis] for axis in AXES)
    program = relay if sizes == (4, 4, 2) else per_device
    return jax.shard_map(
        program, mesh=mesh, in_specs=in_specs, out_specs=out_specs, check_vma=False
    )
```

profile of v0, /device:TPU:22, one launch (start us, length us, event | category | flops | bytes accessed | tf_op | source)
XLA Modules:
  0.0 185.2 jit_solution(6461251281728064046)
XLA Ops:
  0.0 2.5 %copy.10 = bf16[1,2592,192]{2,1,0:T(8,128)(2,1)} copy(bf16[1,2592,192]{1,2,0:T(8,128)(2,1)} %param.12) | data formatting | bytes 1990656 | tf_op args[5]
  3.1 3.7 %shard_map.74 = (bf16[640,384]{1,0:T(8,128)(2,1)}, bf16[656,384]{1,0:T(8,128)(2,1)}, bf16[192,432]{1,0:T(8,128)(2,1)}) custom-call(s32[3]{0:T(128)} %pad_add_fusion.ids, bf16[2592,192]{1,0:T(8,128)(2,1)} %bitcast.7, bf16[192,432]{1,0:T(8,128)(2,1)} %bitcast.13), custom_call_target="tpu_custom_call" | custom-call | flops 1000000000 | bytes 4000000 | tf_op jit(solution)/shard_map/pallas_call | solution.py:316
  6.8 0.7 collective-permute-start.8
  7.5 0.7 collective-permute-start.5
  8.2 0.7 collective-permute-start
  8.9 0.7 collective-permute-start.7
  9.6 0.9 constant_dynamic-update-slice_fusion.1
  10.6 1.4 collective-permute-start.1
  12.0 0.7 collective-permute-start.6
  12.7 0.7 collective-permute-start.10
  13.5 0.7 collective-permute-start.9
  14.2 1.4 collective-permute-start.2
  15.6 1.4 collective-permute-start.3
  17.2 0.7 copy-done.2
  18.1 0.8 copy-done.3
  18.9 0.8 shard_map.78
  19.7 4.4 %copy.13 = bf16[5184,192]{0,1:T(8,128)(2,1)} copy(bf16[5184,192]{1,0:T(8,128)(2,1)} %get-tuple-element.22.k2_own) | data formatting | bytes 3981312 | tf_op jit(solution)/shard_map/pallas_call | solution.py:316
  24.0 0.8 collective-permute-start.18
  24.9 58.4 %all_to_all.10.g_any = bf16[8,20,768]{2,1,0:T(8,128)(2,1)} all-to-all(bf16[8,20,768]{2,1,0:T(8,128)(2,1)S(1)} %broadcast_in_dim.4), channel_id=1, replica_groups=mesh['segment'=4,'ha'=4,'wa'=2] {'ha','wa'}, dimensions={0} | all-to-all | bytes 491520 | tf_op jit(solution)/shard_map/all_to_all | solution.py:1023
  83.3 0.8 shard_map.73
  84.1 0.9 copy.11
  85.1 0.8 broadcast_in_dim.5
  85.9 6.6 %all-to-all-start.1 = ((bf16[8,128,192]{1,2,0:T(8,128)(2,1)}), bf16[8,128,192]{1,2,0:T(8,128)(2,1)S(1)}, u32[]{:S(2)}, u32[]{:S(2)}) async-start(bf16[8,128,192]{1,2,0:T(8,128)(2,1)} %broadcast_in_dim.5), calls=%async_computation.1 | async-start | bytes 786432 | tf_op jit(solution)/shard_map/all_to_all | solution.py:1027
  92.5 0.7 pad_maximum_fusion.1
  93.2 2.5 %collective-permute-start.15 = (bf16[48,1536]{1,0:T(8,128)(2,1)}, bf16[48,1536]{1,0:T(8,128)(2,1)}, u32[]{:S(2)}, u32[]{:S(2)}) collective-permute-start(bf16[48,1536]{1,0:T(8,128)(2,1)} %pad_maximum_fusion.1), channel_id=1, source_target_pairs={{16,17},{17,16},{18,19},{19,18},{20,21},{21,20},{22,23},{23,22},{2... | collective-permute-start | bytes 442376 | tf_op jit(solution)/shard_map/ppermute | solution.py:306
  95.7 1.6 collective-permute-start.19
  97.3 0.9 all-to-all-done.1
  98.2 1.0 copy.12.y_any
  99.2 1.0 shard_map.75
  100.3 0.7 collective-permute-start.4
  101.0 1.4 collective-permute-start.20
  102.4 1.6 pad_maximum_fusion.b0_any
  104.0 5.4 %collective-permute-start.16 = (bf16[96,1536]{1,0:T(8,128)(2,1)}, bf16[96,1536]{1,0:T(8,128)(2,1)}, u32[]{:S(2)}, u32[]{:S(2)}) collective-permute-start(bf16[96,1536]{1,0:T(8,128)(2,1)} %pad_maximum_fusion.b0_any), channel_id=1, source_target_pairs={{18,16},{19,17},{20,18},{21,19},{26,24},{27,25},{28,26},{29,27}} | collective-permute-start | bytes 884744 | tf_op jit(solution)/shard_map/ppermute | solution.py:306
  109.5 2.4 %collective-permute-start.17 = (bf16[96,1536]{1,0:T(8,128)(2,1)}, bf16[96,1536]{1,0:T(8,128)(2,1)}, u32[]{:S(2)}, u32[]{:S(2)}) collective-permute-start(bf16[96,1536]{1,0:T(8,128)(2,1)} %pad_maximum_fusion.b0_any), channel_id=1, source_target_pairs={{20,16},{21,17},{22,18},{23,19},{28,24},{29,25},{30,26},{31,27}} | collective-permute-start | bytes 884744 | tf_op jit(solution)/shard_map/ppermute | solution.py:306
  111.8 0.8 shard_map.76
  112.6 10.1 %collective-permute-done.16.b1_any = bf16[96,1536]{1,0:T(8,128)(2,1)} collective-permute-done((bf16[96,1536]{1,0:T(8,128)(2,1)}, bf16[96,1536]{1,0:T(8,128)(2,1)}, u32[]{:S(2)}, u32[]{:S(2)}) %collective-permute-start.16) | collective-permute-done | bytes 294944 | tf_op jit(solution)/shard_map/ppermute | solution.py:306
  123.4 5.3 %collective-permute-done.17.b2_any = bf16[96,1536]{1,0:T(8,128)(2,1)} collective-permute-done((bf16[96,1536]{1,0:T(8,128)(2,1)}, bf16[96,1536]{1,0:T(8,128)(2,1)}, u32[]{:S(2)}, u32[]{:S(2)}) %collective-permute-start.17) | collective-permute-done | bytes 294944 | tf_op jit(solution)/shard_map/ppermute | solution.py:306
  129.3 1.4 collective-permute-start.13
  130.7 1.4 collective-permute-start.14
  132.1 0.7 shard_map.77
  132.8 3.5 %copy.14.k2_sent = bf16[5184,192]{1,0:T(8,128)(2,1)} copy(bf16[5184,192]{0,1:T(8,128)(2,1)S(1)} %collective-permute-done.18) | data formatting | bytes 3981312 | tf_op jit(solution)/shard_map/ppermute | solution.py:306
  137.1 1.0 shard_map.79
  138.1 0.7 collective-permute-start.23
  138.8 0.7 collective-permute-start.24
  139.4 0.7 collective-permute-start.21
  140.1 1.3 collective-permute-start.22
  141.5 42.7 %collective-permute-done.22 = bf16[1024,96]{1,0:T(8,128)(2,1)S(1)} collective-permute-done((bf16[1024,96]{1,0:T(8,128)(2,1)}, bf16[1024,96]{1,0:T(8,128)(2,1)S(1)}, u32[]{:S(2)}, u32[]{:S(2)}) %collective-permute-start.22) | collective-permute-done | bytes 196640 | tf_op jit(solution)/shard_map/ppermute | solution.py:306
  184.2 1.0 reshape.25
  (64 shorter events, 3.0 us)
Async XLA Ops:
  3.1 14.0 %copy-start.14 = (bf16[2,4,768]{2,1,0:T(4,128)(2,1)S(1)}, bf16[2,4,768]{2,1,0:T(4,128)(2,1)}, u32[]{:S(2)}) copy-start(bf16[2,4,768]{2,1,0:T(4,128)(2,1)} %param.9) | copy-start | bytes 36868
  3.1 14.0 %copy-start.16 = (bf16[2,2,768]{2,1,0:T(2,128)(2,1)S(1)}, bf16[2,2,768]{2,1,0:T(2,128)(2,1)}, u32[]{:S(2)}) copy-start(bf16[2,2,768]{2,1,0:T(2,128)(2,1)} %param.8) | copy-start | bytes 18436
  3.1 14.0 %copy-start.15 = (bf16[4,2,768]{2,1,0:T(2,128)(2,1)S(1)}, bf16[4,2,768]{2,1,0:T(2,128)(2,1)}, u32[]{:S(2)}) copy-start(bf16[4,2,768]{2,1,0:T(2,128)(2,1)} %param.7) | copy-start | bytes 36868
  6.8 5.9 %collective-permute-start.8 = (bf16[656,384]{1,0:T(8,128)(2,1)}, bf16[656,384]{1,0:T(8,128)(2,1)S(1)}, u32[]{:S(2)}, u32[]{:S(2)}) collective-permute-start(bf16[656,384]{1,0:T(8,128)(2,1)} %get-tuple-element.19.refs_1_), channel_id=1, source_target_pairs={{8,9},{9,8},{10,11},{11,10},{16,17},{17,16},{18,19},{19,18},{24,25... | collective-permute-start | bytes 1511432 | tf_op jit(solution)/shard_map/ppermute | solution.py:306
  7.5 5.9 %collective-permute-start.5 = (bf16[640,384]{1,0:T(8,128)(2,1)}, bf16[640,384]{1,0:T(8,128)(2,1)S(1)}, u32[]{:S(2)}, u32[]{:S(2)}) collective-permute-start(bf16[640,384]{1,0:T(8,128)(2,1)} %get-tuple-element.18.refs_0_), channel_id=1, source_target_pairs={{8,10},{9,11},{10,8},{11,9},{16,18},{17,19},{18,16},{19,17},{24,26... | collective-permute-start | bytes 1474568 | tf_op jit(solution)/shard_map/ppermute | solution.py:306
  8.2 2.3 %collective-permute-start = (bf16[192,432]{1,0:T(8,128)(2,1)}, bf16[192,432]{1,0:T(8,128)(2,1)S(1)}, u32[]{:S(2)}, u32[]{:S(2)}) collective-permute-start(bf16[192,432]{1,0:T(8,128)(2,1)} %get-tuple-element.17), channel_id=1, source_target_pairs={{4,0},{5,1},{6,2},{7,3},{12,8},{13,9},{14,10},{15,11}} | collective-permute-start | bytes 497672 | tf_op jit(solution)/shard_map/ppermute | solution.py:306
  8.9 5.3 %collective-permute-start.7 = (bf16[640,384]{1,0:T(8,128)(2,1)}, bf16[640,384]{1,0:T(8,128)(2,1)S(1)}, u32[]{:S(2)}, u32[]{:S(2)}) collective-permute-start(bf16[640,384]{1,0:T(8,128)(2,1)} %get-tuple-element.18.refs_0_), channel_id=1, source_target_pairs={{8,9},{9,8},{10,11},{11,10},{16,17},{17,16},{18,19},{19,18},{24,25... | collective-permute-start | bytes 1474568 | tf_op jit(solution)/shard_map/ppermute | solution.py:306
  10.6 6.6 %copy-start = (bf16[384,432]{1,0:T(8,128)(2,1)}, bf16[384,432]{1,0:T(8,128)(2,1)S(1)}, u32[]{:S(2)}) copy-start(bf16[384,432]{1,0:T(8,128)(2,1)S(1)} %constant_dynamic-update-slice_fusion.own_any.refs_8_) | copy-start | bytes 995332
  10.6 5.0 %collective-permute-start.1 = (bf16[384,432]{1,0:T(8,128)(2,1)S(1)}, bf16[384,432]{1,0:T(8,128)(2,1)}, u32[]{:S(2)}, u32[]{:S(2)}) collective-permute-start(bf16[384,432]{1,0:T(8,128)(2,1)S(1)} %constant_dynamic-update-slice_fusion.own_any.refs_8_), channel_id=1, source_target_pairs={{0,2},{1,3},{2,0},{3,1},{8,10},{9,11},{10,8},{11,9},{16,18},{17,19... | collective-permute-start | bytes 995336 | tf_op jit(solution)/shard_map/ppermute | solution.py:306
  12.0 5.1 %collective-permute-start.6 = (bf16[656,384]{1,0:T(8,128)(2,1)}, bf16[656,384]{1,0:T(8,128)(2,1)S(1)}, u32[]{:S(2)}, u32[]{:S(2)}) collective-permute-start(bf16[656,384]{1,0:T(8,128)(2,1)} %get-tuple-element.19.refs_1_), channel_id=1, source_target_pairs={{8,10},{9,11},{10,8},{11,9},{16,18},{17,19},{18,16},{19,17},{24,26... | collective-permute-start | bytes 1511432 | tf_op jit(solution)/shard_map/ppermute | solution.py:306
  12.7 4.5 %copy-start.1 = (bf16[656,384]{1,0:T(8,128)(2,1)}, bf16[656,384]{1,0:T(8,128)(2,1)S(1)}, u32[]{:S(2)}) copy-start(bf16[656,384]{1,0:T(8,128)(2,1)S(1)} %collective-permute-done.8.refs_5_) | copy-start | bytes 1511428
  12.7 4.4 %collective-permute-start.10 = (bf16[656,384]{1,0:T(8,128)(2,1)S(1)}, bf16[656,384]{1,0:T(8,128)(2,1)S(1)}, u32[]{:S(2)}, u32[]{:S(2)}) collective-permute-start(bf16[656,384]{1,0:T(8,128)(2,1)S(1)} %collective-permute-done.8.refs_5_), channel_id=1, source_target_pairs={{8,10},{9,11},{10,8},{11,9},{16,18},{17,19},{18,16},{19,17},{24,26... | collective-permute-start | bytes 1511432 | tf_op jit(solution)/shard_map/ppermute | solution.py:306
  13.4 3.8 %copy-start.4 = (bf16[640,384]{1,0:T(8,128)(2,1)}, bf16[640,384]{1,0:T(8,128)(2,1)S(1)}, u32[]{:S(2)}) copy-start(bf16[640,384]{1,0:T(8,128)(2,1)S(1)} %collective-permute-done.5.refs_2_) | copy-start | bytes 1474564
  13.5 3.7 %collective-permute-start.9 = (bf16[640,384]{1,0:T(8,128)(2,1)S(1)}, bf16[640,384]{1,0:T(8,128)(2,1)S(1)}, u32[]{:S(2)}, u32[]{:S(2)}) collective-permute-start(bf16[640,384]{1,0:T(8,128)(2,1)S(1)} %collective-permute-done.5.refs_2_), channel_id=1, source_target_pairs={{8,9},{9,8},{10,11},{11,10},{16,17},{17,16},{18,19},{19,18},{24,25... | collective-permute-start | bytes 1474568 | tf_op jit(solution)/shard_map/ppermute | solution.py:306
  14.2 3.0 %copy-start.5 = (bf16[640,384]{1,0:T(8,128)(2,1)}, bf16[640,384]{1,0:T(8,128)(2,1)S(1)}, u32[]{:S(2)}) copy-start(bf16[640,384]{1,0:T(8,128)(2,1)S(1)} %collective-permute-done.7.refs_4_) | copy-start | bytes 1474564
  14.2 2.9 %collective-permute-start.2 = (bf16[384,432]{1,0:T(8,128)(2,1)S(1)}, bf16[384,432]{1,0:T(8,128)(2,1)}, u32[]{:S(2)}, u32[]{:S(2)}) collective-permute-start(bf16[384,432]{1,0:T(8,128)(2,1)S(1)} %constant_dynamic-update-slice_fusion.own_any.refs_8_), channel_id=1, source_target_pairs={{0,1},{1,0},{2,3},{3,2},{8,9},{9,8},{10,11},{11,10},{16,17},{17,16... | collective-permute-start | bytes 995336 | tf_op jit(solution)/shard_map/ppermute | solution.py:306
  15.6 1.5 collective-permute-start.3
  17.1 0.8 copy-start.2
  17.2 0.9 copy-start.6
  18.1 0.8 copy-start.3
  24.0 106.7 %collective-permute-start.18 = (bf16[5184,192]{0,1:T(8,128)(2,1)}, bf16[5184,192]{0,1:T(8,128)(2,1)S(1)}, u32[]{:S(2)}, u32[]{:S(2)}) collective-permute-start(bf16[5184,192]{0,1:T(8,128)(2,1)} %copy.13), channel_id=1, source_target_pairs={{16,24},{17,25},{18,26},{19,27}} | collective-permute-start | bytes 5971976 | tf_op jit(solution)/shard_map/ppermute | solution.py:306
  83.3 9.2 %copy-start.10 = (bf16[2,16,1536]{2,1,0:T(8,128)(2,1)S(1)}, bf16[2,16,1536]{2,1,0:T(8,128)(2,1)}, u32[]{:S(2)}) copy-start(bf16[2,16,1536]{2,1,0:T(8,128)(2,1)} %param.11) | copy-start | bytes 294916
  83.3 9.2 %copy-start.13 = (bf16[2,8,1536]{2,1,0:T(8,128)(2,1)S(1)}, bf16[2,8,1536]{2,1,0:T(8,128)(2,1)}, u32[]{:S(2)}) copy-start(bf16[2,8,1536]{2,1,0:T(8,128)(2,1)} %param.10) | copy-start | bytes 147460
  83.3 12.4 %copy-start.7 = (bf16[3456,128]{1,0:T(8,128)(2,1)S(1)}, bf16[3456,128]{1,0:T(8,128)(2,1)}, u32[]{:S(2)}) copy-start(bf16[3456,128]{1,0:T(8,128)(2,1)} %get-tuple-element.23.k3_own) | copy-start | bytes 2654212
  85.9 12.3 %all-to-all-start.1 = ((bf16[8,128,192]{1,2,0:T(8,128)(2,1)}), bf16[8,128,192]{1,2,0:T(8,128)(2,1)S(1)}, u32[]{:S(2)}, u32[]{:S(2)}) async-start(bf16[8,128,192]{1,2,0:T(8,128)(2,1)} %broadcast_in_dim.5), calls=%async_computation.1 | async-start | bytes 786432 | tf_op jit(solution)/shard_map/all_to_all | solution.py:1027
  93.2 9.2 %collective-permute-start.15 = (bf16[48,1536]{1,0:T(8,128)(2,1)}, bf16[48,1536]{1,0:T(8,128)(2,1)}, u32[]{:S(2)}, u32[]{:S(2)}) collective-permute-start(bf16[48,1536]{1,0:T(8,128)(2,1)} %pad_maximum_fusion.1), channel_id=1, source_target_pairs={{16,17},{17,16},{18,19},{19,18},{20,21},{21,20},{22,23},{23,22},{2... | collective-permute-start | bytes 442376 | tf_op jit(solution)/shard_map/ppermute | solution.py:306
  95.7 40.6 %collective-permute-start.19 = (bf16[3456,128]{1,0:T(8,128)(2,1)S(1)}, bf16[3456,128]{1,0:T(8,128)(2,1)}, u32[]{:S(2)}, u32[]{:S(2)}) collective-permute-start(bf16[3456,128]{1,0:T(8,128)(2,1)S(1)} %copy-done.7), channel_id=1, source_target_pairs={{24,16},{25,17},{26,18},{27,19}} | collective-permute-start | bytes 2654216 | tf_op jit(solution)/shard_map/ppermute | solution.py:306
  99.2 1.7 copy-start.8
  100.3 9.2 %collective-permute-start.4 = (bf16[768,192]{1,0:T(8,128)(2,1)}, bf16[768,192]{1,0:T(8,128)(2,1)S(1)}, u32[]{:S(2)}, u32[]{:S(2)}) collective-permute-start(bf16[768,192]{1,0:T(8,128)(2,1)} %shard_map.75), channel_id=1, source_target_pairs={{0,8},{1,9},{2,10},{3,11}} | collective-permute-start | bytes 884744 | tf_op jit(solution)/shard_map/ppermute | solution.py:306
  101.0 28.3 %collective-permute-start.20 = (bf16[192,1152]{1,0:T(8,128)(2,1)S(1)}, bf16[192,1152]{1,0:T(8,128)(2,1)}, u32[]{:S(2)}, u32[]{:S(2)}) collective-permute-start(bf16[192,1152]{1,0:T(8,128)(2,1)S(1)} %copy-done.8), channel_id=1, source_target_pairs={{16,24},{17,25},{18,26},{19,27},{24,16},{25,17},{26,18},{27,19}} | collective-permute-start | bytes 1327112 | tf_op jit(solution)/shard_map/ppermute | solution.py:306
  104.0 18.6 %collective-permute-start.16 = (bf16[96,1536]{1,0:T(8,128)(2,1)}, bf16[96,1536]{1,0:T(8,128)(2,1)}, u32[]{:S(2)}, u32[]{:S(2)}) collective-permute-start(bf16[96,1536]{1,0:T(8,128)(2,1)} %pad_maximum_fusion.b0_any), channel_id=1, source_target_pairs={{18,16},{19,17},{20,18},{21,19},{26,24},{27,25},{28,26},{29,27}} | collective-permute-start | bytes 884744 | tf_op jit(solution)/shard_map/ppermute | solution.py:306
  109.5 2.4 %copy-start.9 = (bf16[768,192]{1,0:T(8,128)(2,1)}, bf16[768,192]{1,0:T(8,128)(2,1)S(1)}, u32[]{:S(2)}) copy-start(bf16[768,192]{1,0:T(8,128)(2,1)S(1)} %collective-permute-done.4.x_any) | copy-start | bytes 884740
  109.5 19.2 %collective-permute-start.17 = (bf16[96,1536]{1,0:T(8,128)(2,1)}, bf16[96,1536]{1,0:T(8,128)(2,1)}, u32[]{:S(2)}, u32[]{:S(2)}) collective-permute-start(bf16[96,1536]{1,0:T(8,128)(2,1)} %pad_maximum_fusion.b0_any), channel_id=1, source_target_pairs={{20,16},{21,17},{22,18},{23,19},{28,24},{29,25},{30,26},{31,27}} | collective-permute-start | bytes 884744 | tf_op jit(solution)/shard_map/ppermute | solution.py:306
  122.7 13.6 %collective-permute-start.11 = (bf16[320,384]{1,0:T(8,128)(2,1)}, bf16[320,384]{1,0:T(8,128)(2,1)S(1)}, u32[]{:S(2)}, u32[]{:S(2)}) collective-permute-start(bf16[320,384]{1,0:T(8,128)(2,1)} %shard_map.76), channel_id=1, source_target_pairs={{8,16},{9,17},{10,18},{11,19}} | collective-permute-start | bytes 737288 | tf_op jit(solution)/shard_map/ppermute | solution.py:306
  128.6 7.7 %collective-permute-start.12 = (bf16[320,384]{1,0:T(8,128)(2,1)}, bf16[320,384]{1,0:T(8,128)(2,1)S(1)}, u32[]{:S(2)}, u32[]{:S(2)}) collective-permute-start(bf16[320,384]{1,0:T(8,128)(2,1)} %shard_map.76), channel_id=1, source_target_pairs={{8,24},{9,25},{10,26},{11,27}} | collective-permute-start | bytes 737288 | tf_op jit(solution)/shard_map/ppermute | solution.py:306
  129.3 7.0 %collective-permute-start.13 = (bf16[320,384]{1,0:T(8,128)(2,1)}, bf16[320,384]{1,0:T(8,128)(2,1)}, u32[]{:S(2)}, u32[]{:S(2)}) collective-permute-start(bf16[320,384]{1,0:T(8,128)(2,1)} %shard_map.76), channel_id=1, source_target_pairs={{8,17},{9,16},{10,19},{11,18}} | collective-permute-start | bytes 737288 | tf_op jit(solution)/shard_map/ppermute | solution.py:306
  130.7 5.6 %collective-permute-start.14 = (bf16[320,384]{1,0:T(8,128)(2,1)}, bf16[320,384]{1,0:T(8,128)(2,1)}, u32[]{:S(2)}, u32[]{:S(2)}) collective-permute-start(bf16[320,384]{1,0:T(8,128)(2,1)} %shard_map.76), channel_id=1, source_target_pairs={{8,25},{9,24},{10,27},{11,26}} | collective-permute-start | bytes 737288 | tf_op jit(solution)/shard_map/ppermute | solution.py:306
  136.3 0.7 copy-start.11
  136.3 0.8 copy-start.12
  138.1 3.4 %collective-permute-start.23 = (bf16[1024,96]{1,0:T(8,128)(2,1)}, bf16[1024,96]{1,0:T(8,128)(2,1)S(1)}, u32[]{:S(2)}, u32[]{:S(2)}) collective-permute-start(bf16[1024,96]{1,0:T(8,128)(2,1)} %get-tuple-element.27), channel_id=1, source_target_pairs={{16,2},{17,10},{18,6},{19,14},{24,18},{25,26},{26,22},{27,30}} | collective-permute-start | bytes 589832 | tf_op jit(solution)/shard_map/ppermute | solution.py:306
  138.8 2.7 %collective-permute-start.24 = (bf16[1024,96]{1,0:T(8,128)(2,1)}, bf16[1024,96]{1,0:T(8,128)(2,1)S(1)}, u32[]{:S(2)}, u32[]{:S(2)}) collective-permute-start(bf16[1024,96]{1,0:T(8,128)(2,1)} %get-tuple-element.28), channel_id=1, source_target_pairs={{16,3},{17,11},{18,7},{19,15},{24,19},{25,27},{26,23},{27,31}} | collective-permute-start | bytes 589832 | tf_op jit(solution)/shard_map/ppermute | solution.py:306
  139.4 2.0 %collective-permute-start.21 = (bf16[1024,96]{1,0:T(8,128)(2,1)}, bf16[1024,96]{1,0:T(8,128)(2,1)S(1)}, u32[]{:S(2)}, u32[]{:S(2)}) collective-permute-start(bf16[1024,96]{1,0:T(8,128)(2,1)} %get-tuple-element.25), channel_id=1, source_target_pairs={{16,0},{17,8},{18,4},{19,12},{24,16},{25,24},{26,20},{27,28}} | collective-permute-start | bytes 589832 | tf_op jit(solution)/shard_map/ppermute | solution.py:306
  140.1 44.0 %collective-permute-start.22 = (bf16[1024,96]{1,0:T(8,128)(2,1)}, bf16[1024,96]{1,0:T(8,128)(2,1)S(1)}, u32[]{:S(2)}, u32[]{:S(2)}) collective-permute-start(bf16[1024,96]{1,0:T(8,128)(2,1)} %get-tuple-element.26), channel_id=1, source_target_pairs={{16,1},{17,9},{18,5},{19,13},{24,17},{25,25},{26,21},{27,29}} | collective-permute-start | bytes 589832 | tf_op jit(solution)/shard_map/ppermute | solution.py:306
where the time goes:
time: 186 us; the launch traced here: 185 us
  waiting for transfers between devices  58.9 us (32%)
  blocking collectives  58.4 us (31%)
  starting transfers between devices  37.9 us (20%)
  local copies, waits for them, and re-layouts  17.6 us (9%)
  Pallas kernels  8.85 us (5%)
  other arithmetic  2.99 us (2%)
    all_to_all x1, blocking collectives, relay(): lax.all_to_all(jnp.broadcast_to(tiles[None], (8, 20, 768)), ('ha', 'wa'),...  58.4 us
    ppermute x25, waiting for transfers between devices, send(): return lax.ppermute(value, AXES, [(place(*a), place(*b)) for a, b in pairs])  58.1 us
    ppermute x25, starting transfers between devices, send(): return lax.ppermute(value, AXES, [(place(*a), place(*b)) for a, b in pairs])  31.3 us
    pallas_call x7, Pallas kernels, kernel_call(): pl.pallas_call(body, out_shape=out_shape, in_specs=[pl.BlockSpec(memory_s...  8.85 us
    all_to_all x1, starting transfers between devices, relay(): lax.all_to_all(jnp.broadcast_to(partial_sums[None], (8, 128, 192)), ('ha'...  6.62 us
    unnamed x36, local copies, waits for them, and re-layouts  5.85 us
    pallas_call x2, local copies, waits for them, and re-layouts, kernel_call(): pl.pallas_call(body, out_shape=out_shape, in_specs=[pl.BlockSpec(memory_s...  5.3 us
  transfers between devices with their start and end apart: 26, of which 4 were waited for; matrix products, arithmetic and copies ran while one was open for 5% of the time, Pallas kernels for 2%

commit v1 on v0

--- a/solution.py
+++ b/solution.py
@@ -316,7 +316,7 @@
     return pl.pallas_call(
         body,
         out_shape=out_shape,
-        in_specs=[pl.BlockSpec(memory_space=pltpu.SMEM)] + [pl.BlockSpec(memory_space=pl.ANY)] * (len(args) - 1),
+        in_specs=[pl.BlockSpec(memory_space=pl.ANY)] * len(args),
         out_specs=jax.tree.map(lambda _: pl.BlockSpec(memory_space=pl.ANY), out_shape),
         scratch_shapes=scratch + [pltpu.SemaphoreType.DMA((copies,))],
         compiler_params=pltpu.CompilerParams(vmem_limit_bytes=VMEM),
@@ -338,6 +338,10 @@
 
 def dot(a, b):
     return jnp.dot(a, b, preferred_element_type=jnp.float32)
+
+
+def dot_t(a, b):
+    return lax.dot_general(a, b, (((1,), (1,)), ((), ())), preferred_element_type=jnp.float32)
 
 
 def index_of(shape):
@@ -388,8 +392,8 @@
             )
 
 
-def conv0_body(ids, g_any, k_any, out_any, g_ref, k_ref, gf, base, xx, acc, buf, out_ref, sems):
-    s, h = ids[0], ids[1]
+def conv0_body(g_any, k_any, out_any, g_ref, k_ref, gf, base, xx, acc, buf, out_ref, sems):
+    s, h = lax.axis_index("segment"), lax.axis_index("ha")
 
     @pl.when(s == 0)
     def _():
@@ -420,7 +424,7 @@
                     dt, dy, dx = tap // 9, tap // 3 % 3, tap % 3
                     start = dt * 160 + dy * 16
                     k0 = at - part * 2592
-                    term = dot(xx[dx, start : start + 608, c0:c1], k_ref[k0 : k0 + c1 - c0, :])
+                    term = dot_t(xx[dx, start : start + 608, c0:c1], k_ref[:, k0 : k0 + c1 - c0])
                     total = term if total is None else total + term
                     at += c1 - c0
                 acc[...] = total
@@ -429,27 +433,29 @@
             for r in range(8):
                 to, at = (frame * 8 + r) * 4, frame * 160 + r * 16
                 buf[to : to + 4, :] = acc[at : at + 4, :]
-        out_ref[...] = buf[...].astype(jnp.bfloat16)
-        wait_all(start_all([(out_ref, out_any)], sems))
-
-
-def conv0(ids, gathered, k):
+        out_ref[0:128, :] = buf[:, 0:128].astype(jnp.bfloat16)
+        tail = jnp.concatenate([buf[0:64, 128:192], buf[64:128, 128:192]], axis=1)
+        out_ref[128:192, :] = tail.astype(jnp.bfloat16)
+        wait_all(start_all([(out_ref, out_any.at[n]) for n in range(8)], sems))
+
+
+def conv0(gathered, k):
     f32, bf16 = jnp.float32, jnp.bfloat16
     return kernel_call(
         conv0_body,
-        jax.ShapeDtypeStruct((128, 192), bf16),
+        jax.ShapeDtypeStruct((8, 192, 128), bf16),
         [
             pltpu.VMEM((8, 20, 768), bf16),
-            pltpu.VMEM((2592, 192), bf16),
+            pltpu.VMEM((192, 2592), bf16),
             pltpu.VMEM((8, 20, 768), f32),
             pltpu.VMEM((960, 384), f32),
             pltpu.VMEM((3, 960, 384), bf16),
             pltpu.VMEM((608, 192), f32),
             pltpu.VMEM((128, 192), f32),
-            pltpu.VMEM((128, 192), bf16),
+            pltpu.VMEM((192, 128), bf16),
         ],
-        ids, gathered, k,
-        copies=2,
+        gathered, k,
+        copies=8,
     )
 
 
@@ -467,9 +473,9 @@
         taps_ref[:, tap * lanes : tap * lanes + width] = cat_ref[:, tap * width : (tap + 1) * width]
 
 
-def up0_body(ids, y_any, own_any, z_any, x_any, d_any, out_any, y_ref, own, nz, nx, nd, cat, taps, hbuf, hs, p, t,
+def up0_body(y_any, own_any, z_any, x_any, d_any, out_any, y_ref, own, nz, nx, nd, cat, taps, hbuf, hs, p, t,
              out_ref, sems):
-    s, h, w = ids[0], ids[1], ids[2]
+    s, h, w = (lax.axis_index(axis) for axis in AXES)
 
     @pl.when((s == 0) & (h < 2))
     def _():
@@ -480,7 +486,8 @@
             total = y_ref[ww].astype(jnp.float32)
             for hh in range(1, 4):
                 total = total + y_ref[hh * 2 + ww].astype(jnp.float32)
-            halves.append(total)
+            tail = jnp.concatenate([total[128:192, 0:64], total[128:192, 64:128]], axis=0)
+            halves.append(jnp.concatenate([total[0:128], tail], axis=1))
         squares = sum(jnp.sum(half * half, axis=1, keepdims=True) for half in halves)
         inverse = lax.rsqrt(squares / 384.0 + EPSILON)
         active = [silu(half * inverse) for half in halves]
@@ -519,13 +526,13 @@
         wait_all(start_all([(out_ref, out_any)], sems))
 
 
-def up0(ids, partials, ups):
+def up0(partials, ups):
     f32, bf16 = jnp.float32, jnp.bfloat16
     return kernel_call(
         up0_body,
         jax.ShapeDtypeStruct((768, 192), bf16),
         [
-            pltpu.VMEM((8, 128, 192), bf16),
+            pltpu.VMEM((8, 192, 128), bf16),
             *[pltpu.VMEM((384, 432), bf16)] * 4,
             pltpu.VMEM((192, 1728), bf16),
             pltpu.VMEM((192, 2304), bf16),
@@ -535,39 +542,32 @@
             pltpu.VMEM((4, 576, 128), f32),
             pltpu.VMEM((768, 192), bf16),
         ],
-        ids, partials, *ups,
+        partials, *ups,
         copies=5,
     )
 
 
 def group_rows(first, second, group):
-    parts, at, end = [], group * 576, group * 576 + 576
-    while at < end:
-        quarter, row = divmod(at, 1296)
-        count = min(1296 - row, end - at)
-        source = (first, second)[quarter // 2]
-        lane = quarter % 2 * 192
-        parts.append(source[row : row + count, lane : lane + 192])
-        at += count
-    return parts[0] if len(parts) == 1 else jnp.concatenate(parts, axis=0)
-
-
-def section1_body(ids, x_any, g_any, *refs):
-    kernels_any, ups_any, out_any = refs[0:8], refs[8:12], refs[12]
-    x_ref, g_ref = refs[13:15]
-    k_own, k_z, k_x, k_d, own, nz, nx, nd = refs[15:23]
-    gf, full, base, xx, acc, hs, cat, taps, p, t, out_ref, sems = refs[23:]
-    s, h, w = ids[0], ids[1], ids[2]
+    at, end = group * 576, group * 576 + 576
+    if end <= 2592:
+        return first[:, at:end]
+    if at >= 2592:
+        return second[:, at - 2592 : end - 2592]
+    return jnp.concatenate([first[:, at:2592], second[:, 0 : end - 2592]], axis=1)
+
+
+def section1_body(x_any, g_any, *refs):
+    kernels_any, ups_any, out_any = refs[0:4], refs[4:8], refs[8]
+    x_ref, g_ref = refs[9:11]
+    k_own, k_z, k_x, k_d, own, nz, nx, nd = refs[11:19]
+    gf, full, base, xx, acc, hs, cat, taps, p, t, out_ref, sems = refs[19:]
+    s, h, w = (lax.axis_index(axis) for axis in AXES)
 
     @pl.when((s == 1) & (h < 2))
     def _():
         coming = start_all([(x_any, x_ref), (g_any, g_ref)], sems)
-        pairs = []
-        for number, piece in enumerate((k_own, k_z, k_x, k_d)):
-            pairs.append((kernels_any[2 * number], piece.at[0:640]))
-            pairs.append((kernels_any[2 * number + 1], piece.at[640:1296]))
-        arriving = start_all(pairs, sems, 2)
-        rising = start_all(list(zip(ups_any, (own, nz, nx, nd))), sems, 10)
+        arriving = start_all(list(zip(kernels_any, (k_own, k_z, k_x, k_d))), sems, 2)
+        rising = start_all(list(zip(ups_any, (own, nz, nx, nd))), sems, 6)
         wait_all(coming)
 
         @pl.when(w == 0)
@@ -603,7 +603,7 @@
                     total = None
                     for group in range(9):
                         start = group // 3 * 192 + group % 3 * 16
-                        term = dot(xx[start : start + 352, :], group_rows(first, second, group))
+                        term = dot_t(xx[start : start + 352, :], group_rows(first, second, group))
                         total = term if total is None else total + term
                     acc[k] = total
 
@@ -641,7 +641,7 @@
         wait_all(start_all([(out_ref, out_any)], sems))
 
 
-def section1(ids, frames, gathered, kernels, ups):
+def section1(frames, gathered, kernels, ups):
     f32, bf16 = jnp.float32, jnp.bfloat16
     return kernel_call(
         section1_body,
@@ -649,7 +649,7 @@
         [
             pltpu.VMEM((768, 192), bf16),
             pltpu.VMEM((8, 20, 768), bf16),
-            *[pltpu.VMEM((1296, 384), bf16)] * 4,
+            *[pltpu.VMEM((192, 2592), bf16)] * 4,
             *[pltpu.VMEM((384, 432), bf16)] * 4,
             pltpu.VMEM((8, 20, 768), f32),
             pltpu.VMEM((576, 192), f32),
@@ -663,82 +663,45 @@
             pltpu.VMEM((4, 768, 128), f32),
             pltpu.VMEM((320, 384), bf16),
         ],
-        ids, frames, gathered, *kernels, *ups,
-        copies=14,
-    )
-
-
-def pick(across, step, count, at):
-    source = lax.broadcasted_iota(jnp.int32, (192, 192), 1 if across else 0)
-    target = lax.broadcasted_iota(jnp.int32, (192, 192), 0 if across else 1) - at
+        frames, gathered, *kernels, *ups,
+        copies=10,
+    )
+
+
+def pick(step, count, at):
+    source = lax.broadcasted_iota(jnp.int32, (192, 192), 1)
+    target = lax.broadcasted_iota(jnp.int32, (192, 192), 0) - at
     return ((source == target * step) & (target >= 0) & (target < count)).astype(jnp.bfloat16)
 
 
-def pack_body(ids, k_any, u_any, upper_any, lower_any, up_any, k, u, upper, lower, up, sems):
-    s, w = ids[0], ids[2]
+def merge_body(*refs):
+    kernels_any, ups_any, (k2_any, k3_any, up_any) = refs[0:4], refs[4:8], refs[8:11]
+    pieces, ups = refs[11:15], refs[15:19]
+    k2, wide, k3, cat, up, sems = refs[19:]
+    s, h = lax.axis_index("segment"), lax.axis_index("ha")
     bf16 = jnp.bfloat16
-    coming = start_all([(k_any, k), (u_any, u)], sems)
-    wait_all(coming)
-
-    @pl.when(s < 2)
-    def _():
-        for half in range(2):
-            lane = half * 192
-            upper[:, lane : lane + 192] = k[half * 1296 : half * 1296 + 640]
-            lower[:, lane : lane + 192] = k[half * 1296 + 640 : half * 1296 + 1296]
-        up[...] = u[...]
-
-    for level, step, count in ((2, 2, 96), (3, 4, 48)):
-
-        @pl.when(s == level)
-        def _():
-            columns = pick(False, step, count, w * count)
-            for half in range(2):
-                lane = half * 192
-                upper[:, lane : lane + 192] = dot(k[half * 1296 : half * 1296 + 640], columns).astype(bf16)
-                lower[:, lane : lane + 192] = dot(k[half * 1296 + 640 : half * 1296 + 1296], columns).astype(bf16)
-            up[...] = dot(pick(True, step, count, w * count), u[...]).astype(bf16)
-
-    wait_all(start_all([(upper, upper_any), (lower, lower_any), (up, up_any)], sems))
-
-
-def pack(ids, k, u):
-    bf16 = jnp.bfloat16
-    shapes = ((640, 384), (656, 384), (192, 432))
-    return kernel_call(
-        pack_body,
-        tuple(jax.ShapeDtypeStruct(shape, bf16) for shape in shapes),
-        [pltpu.VMEM((2592, 192), bf16), pltpu.VMEM((192, 432), bf16)] + [pltpu.VMEM(shape, bf16) for shape in shapes],
-        ids, k, u,
-        copies=3,
-    )
-
-
-def merge_body(ids, *refs):
-    kernels_any, ups_any, (k2_any, k3_any, up_any) = refs[0:8], refs[8:12], refs[12:15]
-    pieces, ups = refs[15:19], refs[19:23]
-    k2, wide, k3, cat, up, sems = refs[23:]
-    s, h = ids[0], ids[1]
 
     @pl.when((s >= 2) & (h < 2))
     def _():
-        pairs = []
-        for number, piece in enumerate(pieces):
-            pairs.append((kernels_any[2 * number], piece.at[0:640]))
-            pairs.append((kernels_any[2 * number + 1], piece.at[640:1296]))
-        coming = start_all(pairs, sems)
-        rising = start_all([(a.at[0:192], b) for a, b in zip(ups_any, ups)], sems, 8)
+        coming = start_all(list(zip(kernels_any, pieces)), sems)
+        rising = start_all([(a.at[0:192], b) for a, b in zip(ups_any, ups)], sems, 4)
         wait_all(rising)
+        step = jnp.where(s == 2, 2, 4)
+        count = jnp.where(s == 2, 96, 48)
+        mine, theirs = pick(step, count, 0), pick(step, count, count)
+        near = (dot(mine, ups[0][...]) + dot(theirs, ups[2][...])).astype(bf16)
+        far = (dot(mine, ups[1][...]) + dot(theirs, ups[3][...])).astype(bf16)
         for z in range(2):
 
             @pl.when(h == z)
             def _():
-                cat[:, z * 432 : z * 432 + 432] = ups[0][...] + ups[2][...]
-                cat[:, (1 - z) * 432 : (1 - z) * 432 + 432] = ups[1][...] + ups[3][...]
+                cat[:, z * 432 : z * 432 + 432] = near
+                cat[:, (1 - z) * 432 : (1 - z) * 432 + 432] = far
 
         up[...] = jnp.zeros_like(up)
         for tap in range(9):
             up[:, tap * 128 : tap * 128 + 96] = cat[:, tap * 96 : (tap + 1) * 96]
+        sending = start_all([(up, up_any)], sems, 4)
         wait_all(coming)
         own, nz, nx, nd = pieces
 
@@ -749,10 +712,8 @@
                 @pl.when(h == z)
                 def _():
                     for part, (a, b) in enumerate(((own, nx), (nz, nd))):
-                        part = part ^ z
-                        for half in range(2):
-                            at, lane = (part * 2 + half) * 1296, half * 192
-                            k2[at : at + 1296, :] = a[:, lane : lane + 192] + b[:, lane : lane + 192]
+                        at = (part ^ z) * 2592
+                        k2[:, at : at + 2592] = (dot(mine, a[...]) + dot(theirs, b[...])).astype(bf16)
 
             wait_all(start_all([(k2, k2_any)], sems))
 
@@ -763,46 +724,46 @@
                 @pl.when(h == z)
                 def _():
                     a, b = ((own, nx), (nz, nd))[z]
-                    for half in range(2):
-                        lane = half * 192
-                        rows = a[:, lane : lane + 128] + b[:, lane : lane + 128]
-                        wide[half * 1296 : half * 1296 + 1296, :] = rows
+                    wide[...] = (dot(mine[0:96], a[...]) + dot(theirs[0:96], b[...])).astype(bf16)
 
             k3[...] = jnp.zeros_like(k3)
             for tap in range(27):
-                k3[tap * 128 : tap * 128 + 96, :] = wide[tap * 96 : tap * 96 + 96, :]
+                k3[:, tap * 128 : tap * 128 + 96] = wide[:, tap * 96 : tap * 96 + 96]
             wait_all(start_all([(k3, k3_any)], sems))
 
-        wait_all(start_all([(up, up_any)], sems))
-
-
-def merge(ids, kernels, ups):
+        wait_all(sending)
+
+
+def merge(kernels, ups):
     bf16 = jnp.bfloat16
-    shapes = ((5184, 192), (3456, 128), (192, 1152))
+    shapes = ((192, 5184), (96, 3456), (192, 1152))
     return kernel_call(
         merge_body,
         tuple(jax.ShapeDtypeStruct(shape, bf16) for shape in shapes),
         [
-            *[pltpu.VMEM((1296, 384), bf16)] * 4,
+            *[pltpu.VMEM((192, 2592), bf16)] * 4,
             *[pltpu.VMEM((192, 432), bf16)] * 4,
-            pltpu.VMEM((5184, 192), bf16),
-            pltpu.VMEM((2592, 128), bf16),
-            pltpu.VMEM((3456, 128), bf16),
+            pltpu.VMEM((192, 5184), bf16),
+            pltpu.VMEM((96, 2592), bf16),
+            pltpu.VMEM((96, 3456), bf16),
             pltpu.VMEM((192, 864), bf16),
             pltpu.VMEM((192, 1152), bf16),
         ],
-        ids, *kernels, *ups,
-        copies=12,
-    )
-
-
-def caches_body(ids, b0_any, b1_any, b2_any, c_any, d_any, bands, wide, c_full, d_full, c, d, sems):
-    s, h, w = ids[0], ids[1], ids[2]
+        *kernels, *ups,
+        copies=8,
+    )
+
+
+def caches_body(*refs):
+    parts, (c_any, d_any) = refs[0:6], refs[6:8]
+    bands, wide, c_full, d_full, c, d, sems = refs[8:]
+    s, h, w = (lax.axis_index(axis) for axis in AXES)
     f32, bf16 = jnp.float32, jnp.bfloat16
 
     @pl.when((s >= 2) & (h < 2))
     def _():
-        wait_all(start_all([(a, bands.at[n]) for n, a in enumerate((b0_any, b1_any, b2_any))], sems))
+        pairs = [(a, bands.at[n // 2, n % 2 * 48 : n % 2 * 48 + 48]) for n, a in enumerate(parts)]
+        wait_all(start_all(pairs, sems))
         c_full[...] = jnp.zeros_like(c_full)
         d_full[...] = jnp.zeros_like(d_full)
         for band in range(3):
@@ -833,7 +794,7 @@
         wait_all(start_all([(c, c_any), (d, d_any)], sems))
 
 
-def caches(ids, bands):
+def caches(bands):
     f32, bf16 = jnp.float32, jnp.bfloat16
     return kernel_call(
         caches_body,
@@ -846,15 +807,15 @@
             pltpu.VMEM((640, 192), bf16),
             pltpu.VMEM((2240, 96), bf16),
         ],
-        ids, *bands,
-        copies=3,
-    )
-
-
-def sections23_body(ids, same2, same3, other2, other3, c_any, d_any, k2_own, k2_sent, k3_own, k3_sent, u_own, u_sent,
-                    out0, out1, out2, out3, pairs, d_ref, k2, k3, u2, u3, line, base, xx, hs, p, t, base3, xx3, hs3, p3, t3, out_ref,
+        *bands,
+        copies=6,
+    )
+
+
+def sections23_body(same2, same3, other2, other3, c_any, d_any, k2_own, k2_sent, k3_own, k3_sent, u_own, u_sent,
+                    out0, out1, out2, out3, pairs, d_ref, k2, k3, u2, u3, line, base, xx, hs, p, t, base3, xx3, hs3, p3, t3, rows3, out_ref,
                     sems):
-    s, h, w = ids[0], ids[1], ids[2]
+    s, h, w = (lax.axis_index(axis) for axis in AXES)
     f32, bf16 = jnp.float32, jnp.bfloat16
 
     @pl.when((s >= 2) & (h < 2))
@@ -909,7 +870,7 @@
         total = None
         for group in range(9):
             start = group // 3 * 320 + group % 3 * 16
-            term = dot(xx[start : start + 928, :], k2[group * 576 : (group + 1) * 576, :])
+            term = dot_t(xx[start : start + 928, :], k2[:, group * 576 : (group + 1) * 576])
             total = term if total is None else total + term
         inverse = lax.rsqrt(jnp.sum(total * total, axis=1, keepdims=True) / 192.0 + EPSILON)
         keep = index_of((928, 192)) % 320 < 288
@@ -949,7 +910,7 @@
         total = None
         for group in range(9):
             start = group // 3 * 1120 + group % 3 * 32
-            term = dot(xx3[start : start + 1056, :], k3[group * 384 : (group + 1) * 384, 0:96])
+            term = dot_t(xx3[start : start + 1056, :], k3[:, group * 384 : (group + 1) * 384])
             total = term if total is None else total + term
         inverse = lax.rsqrt(jnp.sum(total * total, axis=1, keepdims=True) / 96.0 + EPSILON)
         hs3[0:1056] = silu(total * inverse).astype(bf16)
@@ -960,26 +921,33 @@
 
             @pl.when(h == z)
             def _():
-                for r in range(64):
-                    y = r + 2 * z
-                    row = t3[y % 2, (y // 2) * 64 : (y // 2) * 64 + 64, 0:96].astype(bf16)
-                    for half in range(2):
-                        at = r % 32 * 32
-                        out_ref[r // 32 * 2 + half, at : at + 32, :] = row[half * 32 : half * 32 + 32]
+                for a in range(2):
+                    for four in range(16):
+                        parts = [
+                            t3[a, pl.ds(z * 64 + four * 4 + n, 32, stride=64), :][:, 0:96] for n in range(4)
+                        ]
+                        row = jnp.concatenate(parts, axis=1)
+                        for n in range(3):
+                            rows3[four * 3 + n, pl.ds(a, 32, stride=2), :] = row[:, n * 128 : (n + 1) * 128]
+        for tile in range(48):
+            lane = tile % 24 * 128
+            for n in range(2):
+                part = rows3[tile, n * 32 : n * 32 + 32, :].astype(bf16)
+                out_ref[n * 2 + tile // 24, :, lane : lane + 128] = part
 
         wait_all(start_all([(out_ref.at[n], target) for n, target in enumerate((out0, out1, out2, out3))], sems))
 
 
-def sections23(ids, received, c, d, kernels):
+def sections23(received, c, d, kernels):
     f32, bf16 = jnp.float32, jnp.bfloat16
     return kernel_call(
         sections23_body,
-        tuple([jax.ShapeDtypeStruct((1024, 96), bf16)] * 4),
+        tuple([jax.ShapeDtypeStruct((32, 3072), bf16)] * 4),
         [
             pltpu.VMEM((2, 320, 384), bf16),
             pltpu.VMEM((2240, 96), bf16),
-            pltpu.VMEM((5184, 192), bf16),
-            pltpu.VMEM((3456, 128), bf16),
+            pltpu.VMEM((192, 5184), bf16),
+            pltpu.VMEM((96, 3456), bf16),
             pltpu.VMEM((192, 1152), bf16),
             pltpu.VMEM((96, 1152), bf16),
             pltpu.VMEM((2560, 192), bf16),
@@ -993,64 +961,62 @@
             pltpu.VMEM((1120, 96), bf16),
             pltpu.VMEM((1120, 1152), f32),
             pltpu.VMEM((2, 2240, 128), f32),
-            pltpu.VMEM((4, 1024, 96), bf16),
+            pltpu.VMEM((48, 64, 128), f32),
+            pltpu.VMEM((4, 32, 3072), bf16),
         ],
-        ids, *received, c, d, *kernels,
+        *received, c, d, *kernels,
         copies=8,
     )
 
 
 def relay(latent, cache_a, cache_b, cache_c, cache_d, conv_pack, up_pack):
-    s, h, w = (lax.axis_index(axis) for axis in AXES)
-    ids = jnp.stack([s, h, w]).astype(jnp.int32)
-    k = conv_pack[0]
-
-    upper, lower, u = pack(ids, k, up_pack[0])
-    later = (1, 2, 3)
+    h, w = lax.axis_index("ha"), lax.axis_index("wa")
+    k, u = conv_pack[0].T, up_pack[0]
+
+    along_z = square((1, 2), 1, 0) + [((3, 0, w_), (3, 1, w_)) for w_ in range(2)]
+    along_x = square((1, 2), 0, 1) + [((3, 0, w_), (3, 0, w_ ^ 1)) for w_ in range(2)]
+    across = square((1, 2), 0, 1) + [((3, 1, w_), (3, 1, w_ ^ 1)) for w_ in range(2)]
     u_far = send(u, [((s_, h_ + 2, w_), (s_, h_, w_)) for s_ in (0, 1) for h_ in range(2) for w_ in range(2)])
-    upper_z, lower_z = (send(part, square(later, 1, 0)) for part in (upper, lower))
-    upper_x, lower_x = (send(part, square(later, 0, 1)) for part in (upper, lower))
-    ups = jnp.concatenate([u, u_far], axis=0)
-    u_z = send(ups, square(range(4), 1, 0))
-    u_x = send(ups, square(range(4), 0, 1))
-    u_d = send(u_z, square(range(4), 0, 1))
-    upper_d = send(upper_z, square(later, 0, 1))
-    lower_d = send(lower_x, square(later, 1, 0))
-    kernels = (upper, lower, upper_z, lower_z, upper_x, lower_x, upper_d, lower_d)
-    risers = (ups, u_z, u_x, u_d)
+    k_z, k_x = send(k, along_z), send(k, along_x)
 
     tiles = jnp.concatenate([latent.reshape(8, 768), cache_a.reshape(4, 768), cache_b.reshape(8, 768)], axis=0)
     gathered = lax.all_to_all(
         jnp.broadcast_to(tiles[None], (8, 20, 768)), ("ha", "wa"), split_axis=0, concat_axis=0, tiled=True
     )
-    partial_sums = conv0(ids, gathered, k)
-    partials = lax.all_to_all(
-        jnp.broadcast_to(partial_sums[None], (8, 128, 192)), ("ha", "wa"), split_axis=0, concat_axis=0, tiled=True
-    )
-    risen = up0(ids, partials, risers)
+    gathered, u_far = lax.optimization_barrier((gathered, u_far))
+    ups = jnp.concatenate([u, u_far], axis=0)
+    u_z, u_x = send(ups, square(range(4), 1, 0)), send(ups, square(range(4), 0, 1))
+    partial_sums = conv0(gathered, k)
+    partial_sums, k_z, u_x = lax.optimization_barrier((partial_sums, k_z, u_x))
+    k_d = send(k_z, across)
+    u_d = send(u_x, square(range(4), 1, 0))
+    partials = lax.all_to_all(partial_sums, ("ha", "wa"), split_axis=0, concat_axis=0, tiled=True)
+    kernels, risers = (k, k_z, k_x, k_d), (ups, u_z, u_x, u_d)
+    risen = up0(partials, risers)
     given = send(risen, [((0, h_, w_), (1, h_, w_)) for h_ in range(2) for w_ in range(2)])
 
-    out1 = section1(ids, given, gathered, kernels, risers)
+    out1 = section1(given, gathered, kernels, risers)
     received = [
         send(out1, [((1, h_, w_), (s_, h_, w_ ^ dw)) for h_ in range(2) for w_ in range(2)])
         for dw in range(2)
         for s_ in (2, 3)
     ]
 
-    k2, k3, u23 = merge(ids, kernels, risers)
+    out1, cache_c, cache_d, u_z = lax.optimization_barrier((out1, cache_c, cache_d, u_z))
+    own = jnp.concatenate([cache_c.reshape(16, 1536), cache_d.reshape(32, 1536)], axis=0)
+    bands = [own] + [
+        send(own, [((s_, h_ + n, w_ ^ dw), (s_, h_, w_)) for s_ in (2, 3) for h_ in range(2) for w_ in range(2)])
+        for n in range(3)
+        for dw in range(2)
+        if n + dw
+    ]
+    k2, k3, u23 = merge(kernels, (ups, u_z, u_x, u_d))
     pairs = [((s_, h_, w_), (s_ ^ 1, h_, w_)) for s_ in (2, 3) for h_ in range(2) for w_ in range(2)]
     k2_sent = send(k2, [pair for pair in pairs if pair[0][0] == 2])
     k3_sent = send(k3, [pair for pair in pairs if pair[0][0] == 3])
     u_sent = send(u23, pairs)
-    own = jnp.concatenate([cache_c.reshape(16, 1536), cache_d.reshape(32, 1536)], axis=0)
-    beside = send(own, [((s_, h_, w_), (s_, h_, w_ ^ 1)) for s_ in (2, 3) for h_ in range(4) for w_ in range(2)])
-    both = jnp.concatenate([own, beside], axis=0)
-    bands = [both] + [
-        send(both, [((s_, h_ + n, w_), (s_, h_, w_)) for s_ in (2, 3) for h_ in range(2) for w_ in range(2)])
-        for n in (1, 2)
-    ]
-    c, d = caches(ids, bands)
-    blocks = sections23(ids, received, c, d, (k2, k2_sent, k3, k3_sent, u23, u_sent))
+    c, d = caches(bands)
+    blocks = sections23(received, c, d, (k2, k2_sent, k3, k3_sent, u23, u_sent))
 
     arrived = [
         send(
@@ -1062,7 +1028,7 @@
     ]
     lower_half = jnp.where(w == 0, arrived[2], arrived[3])
     upper_half = jnp.where(w == 0, arrived[0], arrived[1])
-    return jnp.where(h % 2 == 0, upper_half, lower_half).reshape(1, 32, 3072)
+    return jnp.where(h % 2 == 0, upper_half, lower_half)[None]
 
 
 def solution(mesh):

time: 186 us -> 177 us (0.952)
  the two profiles are of different devices: /device:TPU:22 before, /device:TPU:31 now
where the time goes in v1:
time: 177 us; the launch traced here: 176 us
  starting transfers between devices  88.5 us (50%)
  waiting for transfers between devices  77 us (44%)
  local copies, waits for them, and re-layouts  7.23 us (4%)
  other arithmetic  1.82 us (1%)
    ppermute x24, starting transfers between devices, send(): return lax.ppermute(value, AXES, [(place(*a), place(*b)) for a, b in pairs])  65.8 us
    ppermute x24, waiting for transfers between devices, send(): return lax.ppermute(value, AXES, [(place(*a), place(*b)) for a, b in pairs])  56.4 us
    all_to_all x1, starting transfers between devices, relay(): lax.all_to_all(partial_sums, ('ha', 'wa'), split_axis=0, concat_axis=0, t...  17 us
    all_to_all x1, waiting for transfers between devices, relay(): lax.all_to_all(jnp.broadcast_to(tiles[None], (8, 20, 768)), ('ha', 'wa'),...  16.7 us
    all_to_all x1, starting transfers between devices, relay(): lax.all_to_all(jnp.broadcast_to(tiles[None], (8, 20, 768)), ('ha', 'wa'),...  5.82 us
    unnamed x46, local copies, waits for them, and re-layouts  4.37 us
    all_to_all x1, waiting for transfers between devices, relay(): lax.all_to_all(partial_sums, ('ha', 'wa'), split_axis=0, concat_axis=0, t...  3.85 us
  transfers between devices with their start and end apart: 26, of which 5 were waited for; matrix products, arithmetic and copies ran while one was open for 2% of the time, Pallas kernels for 0%

profile of v1, /device:TPU:31, one launch (start us, length us, event | category | flops | bytes accessed | tf_op | source)
XLA Modules:
  0.0 175.7 jit_solution(16691960498427993312)
XLA Ops:
  0.0 0.7 collective-permute-start.1
  0.7 0.7 reshape.16
  1.4 0.7 reshape.18
  2.2 0.7 reshape.17
  2.9 0.7 broadcast_in_dim.4
  3.6 5.8 %all-to-all-start = ((bf16[8,20,768]{2,1,0:T(8,128)(2,1)}), bf16[8,20,768]{2,1,0:T(8,128)(2,1)S(1)}, u32[]{:S(2)}, u32[]{:S(2)}) async-start(bf16[8,20,768]{2,1,0:T(8,128)(2,1)} %broadcast_in_dim.4), calls=%async_computation | async-start | bytes 589824 | tf_op jit(solution)/shard_map/all_to_all | solution.py:983
  9.4 0.7 collective-permute-start
  10.1 16.7 %all-to-all-done.g_any = bf16[8,20,768]{2,1,0:T(8,128)(2,1)S(1)} async-done(((bf16[8,20,768]{2,1,0:T(8,128)(2,1)}), bf16[8,20,768]{2,1,0:T(8,128)(2,1)S(1)}, u32[]{:S(2)}, u32[]{:S(2)}) %all-to-all-start) | async-done | bytes 245792 | tf_op jit(solution)/shard_map/all_to_all | solution.py:983
  26.8 1.1 pad_maximum_fusion.own_any.refs_4_
  27.9 0.8 collective-permute-start.2
  28.8 0.1 shard_map.73
  28.9 0.8 copy-done.5
  29.7 17.0 %all-to-all-start.1 = ((bf16[8,192,128]{2,1,0:T(8,128)(2,1)}), bf16[8,192,128]{2,1,0:T(8,128)(2,1)}, u32[]{:S(2)}, u32[]{:S(2)}) async-start(bf16[8,192,128]{2,1,0:T(8,128)(2,1)} %shard_map.73), calls=%async_computation.1 | async-start | bytes 786432 | tf_op jit(solution)/shard_map/all_to_all | solution.py:993
  46.6 0.7 collective-permute-start.6
  47.3 1.7 collective-permute-start.7
  49.0 0.7 collective-permute-start.3
  49.7 1.4 collective-permute-start.4
  51.1 0.8 copy-done.6
  51.9 3.8 %all-to-all-done.1.y_any = bf16[8,192,128]{2,1,0:T(8,128)(2,1)} async-done(((bf16[8,192,128]{2,1,0:T(8,128)(2,1)}), bf16[8,192,128]{2,1,0:T(8,128)(2,1)}, u32[]{:S(2)}, u32[]{:S(2)}) %all-to-all-start.1) | async-done | bytes 393248 | tf_op jit(solution)/shard_map/all_to_all | solution.py:993
  55.8 0.7 collective-permute-start.5
  56.5 1.0 copy-done.2
  57.5 0.1 copy-done.10
  57.6 0.1 shard_map.75
  57.8 0.1 shard_map.77
  57.9 0.9 collective-permute-start.17
  58.9 0.7 collective-permute-start.12
  59.5 0.7 collective-permute-start.13
  60.2 0.7 collective-permute-start.18
  60.9 0.7 collective-permute-start.14
  61.6 46.1 %collective-permute-start.15 = (bf16[48,1536]{1,0:T(8,128)(2,1)S(1)}, bf16[48,1536]{1,0:T(8,128)(2,1)S(1)}, u32[]{:S(2)}, u32[]{:S(2)}) collective-permute-start(bf16[48,1536]{1,0:T(8,128)(2,1)S(1)} %pad_maximum_fusion.1.refs_0_), channel_id=1, source_target_pairs={{20,16},{21,17},{22,18},{23,19},{28,24},{29,25},{30,26},{31,27}} | collective-permute-start | bytes 442376 | tf_op jit(solution)/shard_map/ppermute | solution.py:306
  107.8 1.3 collective-permute-start.16
  109.1 0.7 collective-permute-start.10
  109.8 1.6 collective-permute-done.15.refs_4_
  111.4 0.7 collective-permute-start.11
  112.1 2.3 %collective-permute-done.16.refs_5_ = bf16[48,1536]{1,0:T(8,128)(2,1)S(1)} collective-permute-done((bf16[48,1536]{1,0:T(8,128)(2,1)S(1)}, bf16[48,1536]{1,0:T(8,128)(2,1)S(1)}, u32[]{:S(2)}, u32[]{:S(2)}) %collective-permute-start.16) | collective-permute-done | bytes 147488 | tf_op jit(solution)/shard_map/ppermute | solution.py:306
  114.4 0.7 collective-permute-start.19
  115.1 0.7 collective-permute-start.8
  115.9 1.4 collective-permute-start.9
  117.4 0.6 copy-done.14
  118.0 0.2 copy-done.9
  118.2 0.3 copy-done.8
  118.5 0.6 copy-done.4
  119.1 0.7 collective-permute-start.20
  119.8 0.7 collective-permute-start.21
  120.5 0.7 collective-permute-start.22
  121.2 1.3 collective-permute-start.23
  122.5 52.4 %collective-permute-done.23 = bf16[32,3072]{1,0:T(8,128)(2,1)S(1)} collective-permute-done((bf16[32,3072]{1,0:T(8,128)(2,1)}, bf16[32,3072]{1,0:T(8,128)(2,1)S(1)}, u32[]{:S(2)}, u32[]{:S(2)}) %collective-permute-start.23) | collective-permute-done | bytes 196640 | tf_op jit(solution)/shard_map/ppermute | solution.py:306
  175.0 0.7 select_bitcast_fusion
  (64 shorter events, 0.3 us)
Async XLA Ops:
  0.0 29.6 %collective-permute-start.1 = (bf16[192,2592]{1,0:T(8,128)(2,1)}, bf16[192,2592]{1,0:T(8,128)(2,1)S(1)}, u32[]{:S(2)}, u32[]{:S(2)}) collective-permute-start(bf16[192,2592]{1,0:T(8,128)(2,1)} %bitcast.8), channel_id=1, source_target_pairs={{8,10},{9,11},{10,8},{11,9},{16,18},{17,19},{18,16},{19,17},{24,26... | collective-permute-start | bytes 2985992 | tf_op jit(solution)/shard_map/ppermute | solution.py:306
  3.6 23.2 %all-to-all-start = ((bf16[8,20,768]{2,1,0:T(8,128)(2,1)}), bf16[8,20,768]{2,1,0:T(8,128)(2,1)S(1)}, u32[]{:S(2)}, u32[]{:S(2)}) async-start(bf16[8,20,768]{2,1,0:T(8,128)(2,1)} %broadcast_in_dim.4), calls=%async_computation | async-start | bytes 589824 | tf_op jit(solution)/shard_map/all_to_all | solution.py:983
  9.4 0.7 collective-permute-start
  26.8 1.9 %copy-start.7 = (bf16[8,20,768]{2,1,0:T(8,128)(2,1)}, bf16[8,20,768]{2,1,0:T(8,128)(2,1)S(1)}, u32[]{:S(2)}) copy-start(bf16[8,20,768]{2,1,0:T(8,128)(2,1)S(1)} %all-to-all-done.g_any) | copy-start | bytes 737284
  27.9 21.1 %copy-start.3 = (bf16[384,432]{1,0:T(8,128)(2,1)}, bf16[384,432]{1,0:T(8,128)(2,1)S(1)}, u32[]{:S(2)}) copy-start(bf16[384,432]{1,0:T(8,128)(2,1)S(1)} %pad_maximum_fusion.own_any.refs_4_) | copy-start | bytes 995332
  27.9 18.7 %copy-start = (bf16[1,2592,192]{1,2,0:T(8,128)(2,1)S(1)}, bf16[1,2592,192]{1,2,0:T(8,128)(2,1)}, u32[]{:S(2)}) copy-start(bf16[1,2592,192]{1,2,0:T(8,128)(2,1)} %param.12) | copy-start | bytes 2985988
  27.9 0.9 collective-permute-start.2
  28.9 0.8 copy-start.5
  29.7 26.1 %copy-start.1 = (bf16[192,2592]{1,0:T(8,128)(2,1)}, bf16[192,2592]{1,0:T(8,128)(2,1)S(1)}, u32[]{:S(2)}) copy-start(bf16[192,2592]{1,0:T(8,128)(2,1)S(1)} %collective-permute-done.1.refs_1_) | copy-start | bytes 2985988
  29.7 26.1 %all-to-all-start.1 = ((bf16[8,192,128]{2,1,0:T(8,128)(2,1)}), bf16[8,192,128]{2,1,0:T(8,128)(2,1)}, u32[]{:S(2)}, u32[]{:S(2)}) async-start(bf16[8,192,128]{2,1,0:T(8,128)(2,1)} %shard_map.73), calls=%async_computation.1 | async-start | bytes 786432 | tf_op jit(solution)/shard_map/all_to_all | solution.py:993
  46.6 9.9 %collective-permute-start.6 = (bf16[192,2592]{1,0:T(8,128)(2,1)S(1)}, bf16[192,2592]{1,0:T(8,128)(2,1)S(1)}, u32[]{:S(2)}, u32[]{:S(2)}) collective-permute-start(bf16[192,2592]{1,0:T(8,128)(2,1)S(1)} %bitcast.12), channel_id=1, source_target_pairs={{8,9},{9,8},{10,11},{11,10},{16,17},{17,16},{18,19},{19,18},{24,25... | collective-permute-start | bytes 2985992 | tf_op jit(solution)/shard_map/ppermute | solution.py:306
  47.3 9.2 %collective-permute-start.7 = (bf16[192,2592]{1,0:T(8,128)(2,1)S(1)}, bf16[192,2592]{1,0:T(8,128)(2,1)}, u32[]{:S(2)}, u32[]{:S(2)}) collective-permute-start(bf16[192,2592]{1,0:T(8,128)(2,1)S(1)} %collective-permute-done.1.refs_1_), channel_id=1, source_target_pairs={{8,9},{9,8},{10,11},{11,10},{16,17},{17,16},{18,19},{19,18},{26,27... | collective-permute-start | bytes 2985992 | tf_op jit(solution)/shard_map/ppermute | solution.py:306
  49.0 2.1 %collective-permute-start.3 = (bf16[384,432]{1,0:T(8,128)(2,1)S(1)}, bf16[384,432]{1,0:T(8,128)(2,1)S(1)}, u32[]{:S(2)}, u32[]{:S(2)}) collective-permute-start(bf16[384,432]{1,0:T(8,128)(2,1)S(1)} %pad_maximum_fusion.own_any.refs_4_), channel_id=1, source_target_pairs={{0,2},{1,3},{2,0},{3,1},{8,10},{9,11},{10,8},{11,9},{16,18},{17,19... | collective-permute-start | bytes 995336 | tf_op jit(solution)/shard_map/ppermute | solution.py:306
  49.7 2.2 %collective-permute-start.4 = (bf16[384,432]{1,0:T(8,128)(2,1)}, bf16[384,432]{1,0:T(8,128)(2,1)}, u32[]{:S(2)}, u32[]{:S(2)}) collective-permute-start(bf16[384,432]{1,0:T(8,128)(2,1)} %copy-done.5), channel_id=1, source_target_pairs={{0,2},{1,3},{2,0},{3,1},{8,10},{9,11},{10,8},{11,9},{16,18},{17,19... | collective-permute-start | bytes 995336 | tf_op jit(solution)/shard_map/ppermute | solution.py:306
  51.1 0.8 copy-start.6
  55.8 0.7 collective-permute-start.5
  56.5 1.0 copy-start.2
  56.5 1.1 copy-start.10
  57.7 1.1 copy-start.16
  57.7 1.1 copy-start.17
  57.8 51.3 %copy-start.11 = (bf16[320,384]{1,0:T(8,128)(2,1)S(1)}, bf16[320,384]{1,0:T(8,128)(2,1)}, u32[]{:S(2)}) copy-start(bf16[320,384]{1,0:T(8,128)(2,1)} %shard_map.75) | copy-start | bytes 737284
  57.9 59.5 %collective-permute-start.17 = (bf16[192,5184]{1,0:T(8,128)(2,1)}, bf16[192,5184]{1,0:T(8,128)(2,1)S(1)}, u32[]{:S(2)}, u32[]{:S(2)}) collective-permute-start(bf16[192,5184]{1,0:T(8,128)(2,1)} %get-tuple-element.32.k2_own), channel_id=1, source_target_pairs={{16,24},{17,25},{18,26},{19,27}} | collective-permute-start | bytes 5971976 | tf_op jit(solution)/shard_map/ppermute | solution.py:306
  58.8 55.6 %copy-start.15 = (bf16[48,1536]{1,0:T(8,128)(2,1)}, bf16[48,1536]{1,0:T(8,128)(2,1)S(1)}, u32[]{:S(2)}) copy-start(bf16[48,1536]{1,0:T(8,128)(2,1)S(1)} %pad_maximum_fusion.1.refs_0_) | copy-start | bytes 442372
  58.9 2.7 %collective-permute-start.12 = (bf16[48,1536]{1,0:T(8,128)(2,1)S(1)}, bf16[48,1536]{1,0:T(8,128)(2,1)S(1)}, u32[]{:S(2)}, u32[]{:S(2)}) collective-permute-start(bf16[48,1536]{1,0:T(8,128)(2,1)S(1)} %pad_maximum_fusion.1.refs_0_), channel_id=1, source_target_pairs={{17,16},{16,17},{19,18},{18,19},{25,24},{24,25},{27,26},{26,27}} | collective-permute-start | bytes 442376 | tf_op jit(solution)/shard_map/ppermute | solution.py:306
  59.5 48.2 %collective-permute-start.13 = (bf16[48,1536]{1,0:T(8,128)(2,1)S(1)}, bf16[48,1536]{1,0:T(8,128)(2,1)S(1)}, u32[]{:S(2)}, u32[]{:S(2)}) collective-permute-start(bf16[48,1536]{1,0:T(8,128)(2,1)S(1)} %pad_maximum_fusion.1.refs_0_), channel_id=1, source_target_pairs={{18,16},{19,17},{20,18},{21,19},{26,24},{27,25},{28,26},{29,27}} | collective-permute-start | bytes 442376 | tf_op jit(solution)/shard_map/ppermute | solution.py:306
  60.2 57.1 %collective-permute-start.18 = (bf16[96,3456]{1,0:T(8,128)(2,1)}, bf16[96,3456]{1,0:T(8,128)(2,1)S(1)}, u32[]{:S(2)}, u32[]{:S(2)}) collective-permute-start(bf16[96,3456]{1,0:T(8,128)(2,1)} %get-tuple-element.33.k3_own), channel_id=1, source_target_pairs={{24,16},{25,17},{26,18},{27,19}} | collective-permute-start | bytes 1990664 | tf_op jit(solution)/shard_map/ppermute | solution.py:306
  60.9 48.2 %collective-permute-start.14 = (bf16[48,1536]{1,0:T(8,128)(2,1)S(1)}, bf16[48,1536]{1,0:T(8,128)(2,1)S(1)}, u32[]{:S(2)}, u32[]{:S(2)}) collective-permute-start(bf16[48,1536]{1,0:T(8,128)(2,1)S(1)} %pad_maximum_fusion.1.refs_0_), channel_id=1, source_target_pairs={{19,16},{18,17},{21,18},{20,19},{27,24},{26,25},{29,26},{28,27}} | collective-permute-start | bytes 442376 | tf_op jit(solution)/shard_map/ppermute | solution.py:306
  61.6 54.2 %copy-start.18 = (bf16[48,1536]{1,0:T(8,128)(2,1)}, bf16[48,1536]{1,0:T(8,128)(2,1)S(1)}, u32[]{:S(2)}) copy-start(bf16[48,1536]{1,0:T(8,128)(2,1)S(1)} %collective-permute-done.12.refs_1_) | copy-start | bytes 442372
  61.6 49.8 %collective-permute-start.15 = (bf16[48,1536]{1,0:T(8,128)(2,1)S(1)}, bf16[48,1536]{1,0:T(8,128)(2,1)S(1)}, u32[]{:S(2)}, u32[]{:S(2)}) collective-permute-start(bf16[48,1536]{1,0:T(8,128)(2,1)S(1)} %pad_maximum_fusion.1.refs_0_), channel_id=1, source_target_pairs={{20,16},{21,17},{22,18},{23,19},{28,24},{29,25},{30,26},{31,27}} | collective-permute-start | bytes 442376 | tf_op jit(solution)/shard_map/ppermute | solution.py:306
  107.8 8.1 %copy-start.19 = (bf16[48,1536]{1,0:T(8,128)(2,1)}, bf16[48,1536]{1,0:T(8,128)(2,1)S(1)}, u32[]{:S(2)}) copy-start(bf16[48,1536]{1,0:T(8,128)(2,1)S(1)} %collective-permute-done.13.refs_2_) | copy-start | bytes 442372
  107.8 6.6 %collective-permute-start.16 = (bf16[48,1536]{1,0:T(8,128)(2,1)S(1)}, bf16[48,1536]{1,0:T(8,128)(2,1)S(1)}, u32[]{:S(2)}, u32[]{:S(2)}) collective-permute-start(bf16[48,1536]{1,0:T(8,128)(2,1)S(1)} %pad_maximum_fusion.1.refs_0_), channel_id=1, source_target_pairs={{21,16},{20,17},{23,18},{22,19},{29,24},{28,25},{31,26},{30,27}} | collective-permute-start | bytes 442376 | tf_op jit(solution)/shard_map/ppermute | solution.py:306
  109.1 6.7 %copy-start.20 = (bf16[48,1536]{1,0:T(8,128)(2,1)}, bf16[48,1536]{1,0:T(8,128)(2,1)S(1)}, u32[]{:S(2)}) copy-start(bf16[48,1536]{1,0:T(8,128)(2,1)S(1)} %collective-permute-done.14.refs_3_) | copy-start | bytes 442372
  109.1 6.0 %collective-permute-start.10 = (bf16[320,384]{1,0:T(8,128)(2,1)S(1)}, bf16[320,384]{1,0:T(8,128)(2,1)S(1)}, u32[]{:S(2)}, u32[]{:S(2)}) collective-permute-start(bf16[320,384]{1,0:T(8,128)(2,1)S(1)} %copy-done.11), channel_id=1, source_target_pairs={{8,17},{9,16},{10,19},{11,18}} | collective-permute-start | bytes 737288 | tf_op jit(solution)/shard_map/ppermute | solution.py:306
  111.4 4.4 %copy-start.21 = (bf16[48,1536]{1,0:T(8,128)(2,1)}, bf16[48,1536]{1,0:T(8,128)(2,1)S(1)}, u32[]{:S(2)}) copy-start(bf16[48,1536]{1,0:T(8,128)(2,1)S(1)} %collective-permute-done.15.refs_4_) | copy-start | bytes 442372
  111.4 4.4 %collective-permute-start.11 = (bf16[320,384]{1,0:T(8,128)(2,1)S(1)}, bf16[320,384]{1,0:T(8,128)(2,1)S(1)}, u32[]{:S(2)}, u32[]{:S(2)}) collective-permute-start(bf16[320,384]{1,0:T(8,128)(2,1)S(1)} %copy-done.11), channel_id=1, source_target_pairs={{8,25},{9,24},{10,27},{11,26}} | collective-permute-start | bytes 737288 | tf_op jit(solution)/shard_map/ppermute | solution.py:306
  114.4 1.4 copy-start.22
  114.4 2.9 %collective-permute-start.19 = (bf16[192,1152]{1,0:T(8,128)(2,1)}, bf16[192,1152]{1,0:T(8,128)(2,1)S(1)}, u32[]{:S(2)}, u32[]{:S(2)}) collective-permute-start(bf16[192,1152]{1,0:T(8,128)(2,1)} %get-tuple-element.34.u_own), channel_id=1, source_target_pairs={{16,24},{17,25},{18,26},{19,27},{24,16},{25,17},{26,18},{27,19}} | collective-permute-start | bytes 1327112 | tf_op jit(solution)/shard_map/ppermute | solution.py:306
  115.1 2.3 %copy-start.12 = (bf16[320,384]{1,0:T(8,128)(2,1)}, bf16[320,384]{1,0:T(8,128)(2,1)S(1)}, u32[]{:S(2)}) copy-start(bf16[320,384]{1,0:T(8,128)(2,1)S(1)} %collective-permute-done.10.other2) | copy-start | bytes 737284
  115.1 2.2 %collective-permute-start.8 = (bf16[320,384]{1,0:T(8,128)(2,1)S(1)}, bf16[320,384]{1,0:T(8,128)(2,1)S(1)}, u32[]{:S(2)}, u32[]{:S(2)}) collective-permute-start(bf16[320,384]{1,0:T(8,128)(2,1)S(1)} %copy-done.11), channel_id=1, source_target_pairs={{8,16},{9,17},{10,18},{11,19}} | collective-permute-start | bytes 737288 | tf_op jit(solution)/shard_map/ppermute | solution.py:306
  115.9 1.6 copy-start.13
  115.9 1.5 collective-permute-start.9
  117.3 0.9 copy-start.9
  117.4 1.1 copy-start.8
  117.4 1.7 copy-start.4
  119.1 3.4 %collective-permute-start.20 = (bf16[32,3072]{1,0:T(8,128)(2,1)}, bf16[32,3072]{1,0:T(8,128)(2,1)S(1)}, u32[]{:S(2)}, u32[]{:S(2)}) collective-permute-start(bf16[32,3072]{1,0:T(8,128)(2,1)} %get-tuple-element.35), channel_id=1, source_target_pairs={{16,0},{17,8},{18,4},{19,12},{24,16},{25,24},{26,20},{27,28}} | collective-permute-start | bytes 589832 | tf_op jit(solution)/shard_map/ppermute | solution.py:306
  119.8 2.7 %collective-permute-start.21 = (bf16[32,3072]{1,0:T(8,128)(2,1)}, bf16[32,3072]{1,0:T(8,128)(2,1)S(1)}, u32[]{:S(2)}, u32[]{:S(2)}) collective-permute-start(bf16[32,3072]{1,0:T(8,128)(2,1)} %get-tuple-element.36), channel_id=1, source_target_pairs={{16,1},{17,9},{18,5},{19,13},{24,17},{25,25},{26,21},{27,29}} | collective-permute-start | bytes 589832 | tf_op jit(solution)/shard_map/ppermute | solution.py:306
  120.5 2.0 %collective-permute-start.22 = (bf16[32,3072]{1,0:T(8,128)(2,1)}, bf16[32,3072]{1,0:T(8,128)(2,1)S(1)}, u32[]{:S(2)}, u32[]{:S(2)}) collective-permute-start(bf16[32,3072]{1,0:T(8,128)(2,1)} %get-tuple-element.37), channel_id=1, source_target_pairs={{16,2},{17,10},{18,6},{19,14},{24,18},{25,26},{26,22},{27,30}} | collective-permute-start | bytes 589832 | tf_op jit(solution)/shard_map/ppermute | solution.py:306
  121.2 53.8 %collective-permute-start.23 = (bf16[32,3072]{1,0:T(8,128)(2,1)}, bf16[32,3072]{1,0:T(8,128)(2,1)S(1)}, u32[]{:S(2)}, u32[]{:S(2)}) collective-permute-start(bf16[32,3072]{1,0:T(8,128)(2,1)} %get-tuple-element.38), channel_id=1, source_target_pairs={{16,3},{17,11},{18,7},{19,15},{24,19},{25,27},{26,23},{27,31}} | collective-permute-start | bytes 589832 | tf_op jit(solution)/shard_map/ppermute | solution.py:306
  (1 other events, 0.7 us)

commit v2 on v1

--- a/solution.py
+++ b/solution.py
@@ -312,7 +312,7 @@
     ]
 
 
-def kernel_call(body, out_shape, scratch, *args, copies=0, flops=10**9):
+def kernel_call(body, out_shape, scratch, *args, copies=0, flops=1000):
     return pl.pallas_call(
         body,
         out_shape=out_shape,
@@ -320,7 +320,7 @@
         out_specs=jax.tree.map(lambda _: pl.BlockSpec(memory_space=pl.ANY), out_shape),
         scratch_shapes=scratch + [pltpu.SemaphoreType.DMA((copies,))],
         compiler_params=pltpu.CompilerParams(vmem_limit_bytes=VMEM),
-        cost_estimate=pl.CostEstimate(flops=flops, bytes_accessed=4 * 10**6, transcendentals=0),
+        cost_estimate=pl.CostEstimate(flops=flops, bytes_accessed=1000, transcendentals=0),
     )(*args)
 
 
@@ -392,6 +392,43 @@
             )
 
 
+def tiles_body(latent_any, a_any, b_any, out_any, latent, a, b, rows, out, sems):
+    wait_all(start_all([(latent_any, latent), (a_any, a), (b_any, b)], sems))
+
+    @pl.when(lax.axis_index("segment") == 0)
+    def _():
+        for frame in range(4):
+            rows[frame * 2 : frame * 2 + 2] = latent[frame].astype(jnp.float32)
+        for frame in range(2):
+            rows[8 + frame * 2 : 10 + frame * 2] = a[frame].astype(jnp.float32)
+
+    @pl.when(lax.axis_index("segment") > 0)
+    def _():
+        for frame in range(2):
+            rows[frame * 4 : frame * 4 + 4] = b[frame].astype(jnp.float32)
+        rows[8:12] = jnp.zeros((4, 768), jnp.float32)
+
+    out[...] = rows[...].astype(jnp.bfloat16)
+    wait_all(start_all([(out, out_any.at[n]) for n in range(8)], sems))
+
+
+def spread_tiles(latent, cache_a, cache_b):
+    bf16 = jnp.bfloat16
+    return kernel_call(
+        tiles_body,
+        jax.ShapeDtypeStruct((8, 12, 768), bf16),
+        [
+            pltpu.VMEM((4, 2, 768), bf16),
+            pltpu.VMEM((2, 2, 768), bf16),
+            pltpu.VMEM((2, 4, 768), bf16),
+            pltpu.VMEM((12, 768), jnp.float32),
+            pltpu.VMEM((12, 768), bf16),
+        ],
+        latent, cache_a, cache_b,
+        copies=8,
+    )
+
+
 def conv0_body(g_any, k_any, out_any, g_ref, k_ref, gf, base, xx, acc, buf, out_ref, sems):
     s, h = lax.axis_index("segment"), lax.axis_index("ha")
 
@@ -436,18 +473,18 @@
         out_ref[0:128, :] = buf[:, 0:128].astype(jnp.bfloat16)
         tail = jnp.concatenate([buf[0:64, 128:192], buf[64:128, 128:192]], axis=1)
         out_ref[128:192, :] = tail.astype(jnp.bfloat16)
-        wait_all(start_all([(out_ref, out_any.at[n]) for n in range(8)], sems))
+        wait_all(start_all([(out_ref, out_any)], sems))
 
 
 def conv0(gathered, k):
     f32, bf16 = jnp.float32, jnp.bfloat16
     return kernel_call(
         conv0_body,
-        jax.ShapeDtypeStruct((8, 192, 128), bf16),
+        jax.ShapeDtypeStruct((192, 128), bf16),
         [
-            pltpu.VMEM((8, 20, 768), bf16),
+            pltpu.VMEM((8, 12, 768), bf16),
             pltpu.VMEM((192, 2592), bf16),
-            pltpu.VMEM((8, 20, 768), f32),
+            pltpu.VMEM((8, 12, 768), f32),
             pltpu.VMEM((960, 384), f32),
             pltpu.VMEM((3, 960, 384), bf16),
             pltpu.VMEM((608, 192), f32),
@@ -459,6 +496,27 @@
     )
 
 
+def fold_body(own_any, far_any, out_any, own, far, out, sems):
+    s, h = lax.axis_index("segment"), lax.axis_index("ha")
+
+    @pl.when((s == 0) & (h < 2))
+    def _():
+        wait_all(start_all([(own_any, own), (far_any, far)], sems))
+        out[...] = (own[...].astype(jnp.float32) + far[...].astype(jnp.float32)).astype(jnp.bfloat16)
+        wait_all(start_all([(out, out_any)], sems))
+
+
+def fold(own, far):
+    shape = (192, 128)
+    return kernel_call(
+        fold_body,
+        jax.ShapeDtypeStruct(shape, jnp.bfloat16),
+        [pltpu.VMEM(shape, jnp.bfloat16)] * 3,
+        own, far,
+        copies=2,
+    )
+
+
 def join_taps(h, pieces_own, pieces_z, cat_ref, taps_ref, width, lanes):
     for z in range(2):
 
@@ -473,19 +531,20 @@
         taps_ref[:, tap * lanes : tap * lanes + width] = cat_ref[:, tap * width : (tap + 1) * width]
 
 
-def up0_body(y_any, own_any, z_any, x_any, d_any, out_any, y_ref, own, nz, nx, nd, cat, taps, hbuf, hs, p, t,
-             out_ref, sems):
-    s, h, w = (lax.axis_index(axis) for axis in AXES)
+def up0_body(*refs):
+    sums_any, ups_any, out_any = refs[0:4], refs[4:8], refs[8]
+    y, own, nz, nx, nd = refs[9:14]
+    cat, taps, hbuf, hs, p, t, out_ref, sems = refs[14:]
+    s, h = lax.axis_index("segment"), lax.axis_index("ha")
 
     @pl.when((s == 0) & (h < 2))
     def _():
-        coming = start_all([(y_any, y_ref), (own_any, own), (z_any, nz), (x_any, nx), (d_any, nd)], sems)
-        coming[0].wait()
+        coming = start_all([(a, y.at[n]) for n, a in enumerate(sums_any)], sems)
+        rising = start_all(list(zip(ups_any, (own, nz, nx, nd))), sems, 4)
+        wait_all(coming)
         halves = []
-        for ww in range(2):
-            total = y_ref[ww].astype(jnp.float32)
-            for hh in range(1, 4):
-                total = total + y_ref[hh * 2 + ww].astype(jnp.float32)
+        for side in range(2):
+            total = y[2 * side].astype(jnp.float32) + y[2 * side + 1].astype(jnp.float32)
             tail = jnp.concatenate([total[128:192, 0:64], total[128:192, 64:128]], axis=0)
             halves.append(jnp.concatenate([total[0:128], tail], axis=1))
         squares = sum(jnp.sum(half * half, axis=1, keepdims=True) for half in halves)
@@ -493,12 +552,12 @@
         active = [silu(half * inverse) for half in halves]
         hs[...] = jnp.zeros_like(hs)
         for k in range(2):
-            hbuf[...] = jnp.where(w == k, active[0], active[1])
+            hbuf[...] = active[k]
             for frame in range(4):
                 for r in range(8):
                     to, at = frame * 72 + r * 8, (frame * 8 + r) * 4
                     hs[k, to : to + 4, :] = hbuf[at : at + 4, :]
-        wait_all(coming[1:])
+        wait_all(rising)
         for k, (mine, other) in enumerate(((own, nz), (nx, nd))):
             join_taps(h, (mine[0:192], mine[192:384]), (other[0:192], other[192:384]), cat, taps, 192, 256)
             term = dot(hs[k].astype(jnp.bfloat16), taps[...])
@@ -526,13 +585,13 @@
         wait_all(start_all([(out_ref, out_any)], sems))
 
 
-def up0(partials, ups):
+def up0(sums, ups):
     f32, bf16 = jnp.float32, jnp.bfloat16
     return kernel_call(
         up0_body,
         jax.ShapeDtypeStruct((768, 192), bf16),
         [
-            pltpu.VMEM((8, 192, 128), bf16),
+            pltpu.VMEM((4, 192, 128), bf16),
             *[pltpu.VMEM((384, 432), bf16)] * 4,
             pltpu.VMEM((192, 1728), bf16),
             pltpu.VMEM((192, 2304), bf16),
@@ -542,8 +601,8 @@
             pltpu.VMEM((4, 576, 128), f32),
             pltpu.VMEM((768, 192), bf16),
         ],
-        partials, *ups,
-        copies=5,
+        *sums, *ups,
+        copies=8,
     )
 
 
@@ -579,7 +638,7 @@
                     for ww in range(2):
                         for r in range(4):
                             for c in range(4):
-                                row = 12 + frame * 4 + r
+                                row = frame * 4 + r
                                 at = frame * 288 + (1 + hh * 4 + r) * 16 + ww * 4 + c
                                 full[at : at + 1, :] = gf[hh * 2 + ww, row : row + 1, c * 192 : (c + 1) * 192]
             for frame in range(2):
@@ -648,10 +707,10 @@
         jax.ShapeDtypeStruct((320, 384), bf16),
         [
             pltpu.VMEM((768, 192), bf16),
-            pltpu.VMEM((8, 20, 768), bf16),
+            pltpu.VMEM((8, 12, 768), bf16),
             *[pltpu.VMEM((192, 2592), bf16)] * 4,
             *[pltpu.VMEM((384, 432), bf16)] * 4,
-            pltpu.VMEM((8, 20, 768), f32),
+            pltpu.VMEM((8, 12, 768), f32),
             pltpu.VMEM((576, 192), f32),
             pltpu.VMEM((768, 192), f32),
             pltpu.VMEM((768, 576), bf16),
@@ -668,89 +727,85 @@
     )
 
 
-def pick(step, count, at):
-    source = lax.broadcasted_iota(jnp.int32, (192, 192), 1)
-    target = lax.broadcasted_iota(jnp.int32, (192, 192), 0) - at
-    return ((source == target * step) & (target >= 0) & (target < count)).astype(jnp.bfloat16)
+def pick_body(k_any, u_any, out_any, k, u, out, sems):
+    s = lax.axis_index("segment")
+
+    @pl.when(s >= 2)
+    def _():
+        coming = start_all([(k_any, k), (u_any, u)], sems)
+        step = jnp.where(s == 2, 2, 4)
+        source = lax.broadcasted_iota(jnp.int32, (96, 192), 1)
+        target = lax.broadcasted_iota(jnp.int32, (96, 192), 0)
+        picked = ((source == target * step) & (target * step < 192)).astype(jnp.bfloat16)
+        wait_all(coming)
+        out[:, 0:2592] = dot(picked, k[...]).astype(jnp.bfloat16)
+        out[:, 2688:3120] = dot(picked, u[...]).astype(jnp.bfloat16)
+        wait_all(start_all([(out, out_any)], sems))
+
+
+def pick(k, u):
+    bf16 = jnp.bfloat16
+    return kernel_call(
+        pick_body,
+        jax.ShapeDtypeStruct((96, 3200), bf16),
+        [pltpu.VMEM((192, 2592), bf16), pltpu.VMEM((192, 432), bf16), pltpu.VMEM((96, 3200), bf16)],
+        k, u,
+        copies=2,
+    )
 
 
 def merge_body(*refs):
-    kernels_any, ups_any, (k2_any, k3_any, up_any) = refs[0:4], refs[4:8], refs[8:11]
-    pieces, ups = refs[11:15], refs[15:19]
-    k2, wide, k3, cat, up, sems = refs[19:]
+    pieces_any, (k2_any, k3_any, up_any) = refs[0:4], refs[4:7]
+    pieces = refs[7:11]
+    k2, k3, cat, up, sems = refs[11:]
     s, h = lax.axis_index("segment"), lax.axis_index("ha")
     bf16 = jnp.bfloat16
 
     @pl.when((s >= 2) & (h < 2))
     def _():
-        coming = start_all(list(zip(kernels_any, pieces)), sems)
-        rising = start_all([(a.at[0:192], b) for a, b in zip(ups_any, ups)], sems, 4)
-        wait_all(rising)
-        step = jnp.where(s == 2, 2, 4)
-        count = jnp.where(s == 2, 96, 48)
-        mine, theirs = pick(step, count, 0), pick(step, count, count)
-        near = (dot(mine, ups[0][...]) + dot(theirs, ups[2][...])).astype(bf16)
-        far = (dot(mine, ups[1][...]) + dot(theirs, ups[3][...])).astype(bf16)
+        wait_all(start_all(list(zip(pieces_any, pieces)), sems))
+        own, nz, nx, nd = pieces
+        up[...] = jnp.zeros_like(up)
         for z in range(2):
-
-            @pl.when(h == z)
-            def _():
-                cat[:, z * 432 : z * 432 + 432] = near
-                cat[:, (1 - z) * 432 : (1 - z) * 432 + 432] = far
-
-        up[...] = jnp.zeros_like(up)
+            for segment, count in ((2, 96), (3, 48)):
+
+                @pl.when((h == z) & (s == segment))
+                def _():
+                    for part, (a, b) in enumerate(((own, nx), (nz, nd))):
+                        at = (part ^ z) * 432
+                        cat[0:count, at : at + 432] = a[0:count, 2688:3120]
+                        cat[count : 2 * count, at : at + 432] = b[0:count, 2688:3120]
+                        if segment == 2:
+                            at = (part ^ z) * 2592
+                            k2[0:96, at : at + 2592] = a[:, 0:2592]
+                            k2[96:192, at : at + 2592] = b[:, 0:2592]
+                    if segment == 3:
+                        a, b = ((own, nx), (nz, nd))[z]
+                        k3[...] = jnp.zeros_like(k3)
+                        for tap in range(27):
+                            k3[0:48, tap * 128 : tap * 128 + 96] = a[0:48, tap * 96 : tap * 96 + 96]
+                            k3[48:96, tap * 128 : tap * 128 + 96] = b[0:48, tap * 96 : tap * 96 + 96]
+
         for tap in range(9):
             up[:, tap * 128 : tap * 128 + 96] = cat[:, tap * 96 : (tap + 1) * 96]
-        sending = start_all([(up, up_any)], sems, 4)
-        wait_all(coming)
-        own, nz, nx, nd = pieces
-
-        @pl.when(s == 2)
-        def _():
-            for z in range(2):
-
-                @pl.when(h == z)
-                def _():
-                    for part, (a, b) in enumerate(((own, nx), (nz, nd))):
-                        at = (part ^ z) * 2592
-                        k2[:, at : at + 2592] = (dot(mine, a[...]) + dot(theirs, b[...])).astype(bf16)
-
-            wait_all(start_all([(k2, k2_any)], sems))
-
-        @pl.when(s == 3)
-        def _():
-            for z in range(2):
-
-                @pl.when(h == z)
-                def _():
-                    a, b = ((own, nx), (nz, nd))[z]
-                    wide[...] = (dot(mine[0:96], a[...]) + dot(theirs[0:96], b[...])).astype(bf16)
-
-            k3[...] = jnp.zeros_like(k3)
-            for tap in range(27):
-                k3[:, tap * 128 : tap * 128 + 96] = wide[:, tap * 96 : tap * 96 + 96]
-            wait_all(start_all([(k3, k3_any)], sems))
-
-        wait_all(sending)
-
-
-def merge(kernels, ups):
+        wait_all(start_all([(up, up_any), (k2, k2_any), (k3, k3_any)], sems))
+
+
+def merge(pieces):
     bf16 = jnp.bfloat16
     shapes = ((192, 5184), (96, 3456), (192, 1152))
     return kernel_call(
         merge_body,
         tuple(jax.ShapeDtypeStruct(shape, bf16) for shape in shapes),
         [
-            *[pltpu.VMEM((192, 2592), bf16)] * 4,
-            *[pltpu.VMEM((192, 432), bf16)] * 4,
+            *[pltpu.VMEM((96, 3200), bf16)] * 4,
             pltpu.VMEM((192, 5184), bf16),
-            pltpu.VMEM((96, 2592), bf16),
             pltpu.VMEM((96, 3456), bf16),
             pltpu.VMEM((192, 864), bf16),
             pltpu.VMEM((192, 1152), bf16),
         ],
-        *kernels, *ups,
-        copies=8,
+        *pieces,
+        copies=4,
     )
 
 
@@ -760,7 +815,7 @@
     s, h, w = (lax.axis_index(axis) for axis in AXES)
     f32, bf16 = jnp.float32, jnp.bfloat16
 
-    @pl.when((s >= 2) & (h < 2))
+    @pl.when((s == 2) & (h < 2))
     def _():
         pairs = [(a, bands.at[n // 2, n % 2 * 48 : n % 2 * 48 + 48]) for n, a in enumerate(parts)]
         wait_all(start_all(pairs, sems))
@@ -812,7 +867,7 @@
     )
 
 
-def sections23_body(same2, same3, other2, other3, c_any, d_any, k2_own, k2_sent, k3_own, k3_sent, u_own, u_sent,
+def sections23_body(same2, same3, other2, other3, c_own, c_sent, d_any, k2_own, k2_sent, k3_own, k3_sent, u_own, u_sent,
                     out0, out1, out2, out3, pairs, d_ref, k2, k3, u2, u3, line, base, xx, hs, p, t, base3, xx3, hs3, p3, t3, rows3, out_ref,
                     sems):
     s, h, w = (lax.axis_index(axis) for axis in AXES)
@@ -826,6 +881,7 @@
 
             @pl.when(s == segment)
             def _():
+                c_any = c_own if segment == 2 else c_sent
                 held2, held3 = (k2_own, k3_sent) if segment == 2 else (k2_sent, k3_own)
                 up2, up3 = (u_own, u_sent) if segment == 2 else (u_sent, u_own)
                 start_all(
@@ -848,7 +904,7 @@
                 [
                     (same2, pairs.at[0]),
                     (other2, pairs.at[1]),
-                    (c_any, line.at[640:1280]),
+                    (c_own, line.at[640:1280]),
                     (k2_own, k2),
                     (u_own, u2),
                     (d_any, d_ref),
@@ -938,7 +994,7 @@
         wait_all(start_all([(out_ref.at[n], target) for n, target in enumerate((out0, out1, out2, out3))], sems))
 
 
-def sections23(received, c, d, kernels):
+def sections23(received, c, c_sent, d, kernels):
     f32, bf16 = jnp.float32, jnp.bfloat16
     return kernel_call(
         sections23_body,
@@ -964,59 +1020,74 @@
             pltpu.VMEM((48, 64, 128), f32),
             pltpu.VMEM((4, 32, 3072), bf16),
         ],
-        *received, c, d, *kernels,
+        *received, c, c_sent, d, *kernels,
         copies=8,
     )
 
 
+def blank_body(*refs):
+    pass
+
+
+def blank(some, shapes):
+    return kernel_call(blank_body, [jax.ShapeDtypeStruct(shape, jnp.bfloat16) for shape in shapes], [], some, copies=1)
+
+
+LATER = ((192, 5184), (96, 3456), (192, 1152), (192, 5184), (96, 3456), (192, 1152), (640, 192), (640, 192), (2240, 96))
+
+
+def sections01(latent, cache_a, cache_b, cache_c, cache_d, k, u):
+    u_far = send(u, [((s_, h_ + 2, w_), (s_, h_, w_)) for s_ in (0, 1) for h_ in range(2) for w_ in range(2)])
+    k_x, k_z = send(k, square((1,), 0, 1)), send(k, square((1,), 1, 0))
+    gathered = lax.all_to_all(
+        spread_tiles(latent, cache_a, cache_b), ("ha", "wa"), split_axis=0, concat_axis=0, tiled=True
+    )
+    ups = jnp.concatenate([u, u_far], axis=0)
+    gathered, ups = lax.optimization_barrier((gathered, ups))
+    u_z, u_x, u_d = (send(ups, square((0, 1), dh, dw)) for dh, dw in ((1, 0), (0, 1), (1, 1)))
+    partial_sums = conv0(gathered, k)
+    partial_sums, k_x, k_z = lax.optimization_barrier((partial_sums, k_x, k_z))
+    far_sums = send(partial_sums, [((0, h_ + 2, w_), (0, h_, w_)) for h_ in range(2) for w_ in range(2)])
+    k_d = send(k_z, square((1,), 0, 1))
+    sums = fold(partial_sums, far_sums)
+    sums = [sums] + [send(sums, square((0,), dh, dw)) for dh, dw in ((1, 0), (0, 1), (1, 1))]
+    risen = up0(sums, (ups, u_z, u_x, u_d))
+    given = send(risen, [((0, h_, w_), (1, h_, w_)) for h_ in range(2) for w_ in range(2)])
+    out1 = section1(given, gathered, (k, k_z, k_x, k_d), (ups, u_z, u_x, u_d))
+    return (out1, *blank(k, LATER))
+
+
+def before_sections23(latent, cache_a, cache_b, cache_c, cache_d, k, u):
+    own = jnp.concatenate([cache_c.reshape(16, 1536), cache_d.reshape(32, 1536)], axis=0)
+    bands = [own] + [
+        send(own, [((2, h_ + n, w_ ^ dw), (2, h_, w_)) for h_ in range(2) for w_ in range(2)])
+        for n in range(3)
+        for dw in range(2)
+        if n + dw
+    ]
+    picked = pick(k, u)
+    picked_x, picked_z = send(picked, square((2, 3), 0, 1)), send(picked, square((2, 3), 1, 0))
+    picked_d = send(picked_z, square((2, 3), 0, 1))
+    k2, k3, u23 = merge((picked, picked_z, picked_x, picked_d))
+    pairs = [((s_, h_, w_), (s_ ^ 1, h_, w_)) for s_ in (2, 3) for h_ in range(2) for w_ in range(2)]
+    rise, fall = [pair for pair in pairs if pair[0][0] == 2], [pair for pair in pairs if pair[0][0] == 3]
+    c, d = caches(bands)
+    c_sent, k2_sent, k3_sent, u_sent = send(c, rise), send(k2, rise), send(k3, fall), send(u23, pairs)
+    return (*blank(k, ((320, 384),)), k2, k3, u23, k2_sent, k3_sent, u_sent, c, c_sent, d)
+
+
 def relay(latent, cache_a, cache_b, cache_c, cache_d, conv_pack, up_pack):
-    h, w = lax.axis_index("ha"), lax.axis_index("wa")
+    s, h, w = (lax.axis_index(axis) for axis in AXES)
     k, u = conv_pack[0].T, up_pack[0]
-
-    along_z = square((1, 2), 1, 0) + [((3, 0, w_), (3, 1, w_)) for w_ in range(2)]
-    along_x = square((1, 2), 0, 1) + [((3, 0, w_), (3, 0, w_ ^ 1)) for w_ in range(2)]
-    across = square((1, 2), 0, 1) + [((3, 1, w_), (3, 1, w_ ^ 1)) for w_ in range(2)]
-    u_far = send(u, [((s_, h_ + 2, w_), (s_, h_, w_)) for s_ in (0, 1) for h_ in range(2) for w_ in range(2)])
-    k_z, k_x = send(k, along_z), send(k, along_x)
-
-    tiles = jnp.concatenate([latent.reshape(8, 768), cache_a.reshape(4, 768), cache_b.reshape(8, 768)], axis=0)
-    gathered = lax.all_to_all(
-        jnp.broadcast_to(tiles[None], (8, 20, 768)), ("ha", "wa"), split_axis=0, concat_axis=0, tiled=True
-    )
-    gathered, u_far = lax.optimization_barrier((gathered, u_far))
-    ups = jnp.concatenate([u, u_far], axis=0)
-    u_z, u_x = send(ups, square(range(4), 1, 0)), send(ups, square(range(4), 0, 1))
-    partial_sums = conv0(gathered, k)
-    partial_sums, k_z, u_x = lax.optimization_barrier((partial_sums, k_z, u_x))
-    k_d = send(k_z, across)
-    u_d = send(u_x, square(range(4), 1, 0))
-    partials = lax.all_to_all(partial_sums, ("ha", "wa"), split_axis=0, concat_axis=0, tiled=True)
-    kernels, risers = (k, k_z, k_x, k_d), (ups, u_z, u_x, u_d)
-    risen = up0(partials, risers)
-    given = send(risen, [((0, h_, w_), (1, h_, w_)) for h_ in range(2) for w_ in range(2)])
-
-    out1 = section1(given, gathered, kernels, risers)
+    out1, k2, k3, u23, k2_sent, k3_sent, u_sent, c, c_sent, d = lax.cond(
+        s < 2, sections01, before_sections23, latent, cache_a, cache_b, cache_c, cache_d, k, u
+    )
     received = [
         send(out1, [((1, h_, w_), (s_, h_, w_ ^ dw)) for h_ in range(2) for w_ in range(2)])
         for dw in range(2)
         for s_ in (2, 3)
     ]
-
-    out1, cache_c, cache_d, u_z = lax.optimization_barrier((out1, cache_c, cache_d, u_z))
-    own = jnp.concatenate([cache_c.reshape(16, 1536), cache_d.reshape(32, 1536)], axis=0)
-    bands = [own] + [
-        send(own, [((s_, h_ + n, w_ ^ dw), (s_, h_, w_)) for s_ in (2, 3) for h_ in range(2) for w_ in range(2)])
-        for n in range(3)
-        for dw in range(2)
-        if n + dw
-    ]
-    k2, k3, u23 = merge(kernels, (ups, u_z, u_x, u_d))
-    pairs = [((s_, h_, w_), (s_ ^ 1, h_, w_)) for s_ in (2, 3) for h_ in range(2) for w_ in range(2)]
-    k2_sent = send(k2, [pair for pair in pairs if pair[0][0] == 2])
-    k3_sent = send(k3, [pair for pair in pairs if pair[0][0] == 3])
-    u_sent = send(u23, pairs)
-    c, d = caches(bands)
-    blocks = sections23(received, c, d, (k2, k2_sent, k3, k3_sent, u23, u_sent))
+    blocks = sections23(received, c, c_sent, d, (k2, k2_sent, k3, k3_sent, u23, u_sent))
 
     arrived = [
         send(

time: 177 us -> 129 us (0.73)
  starting transfers between devices: 88.5 us -> 19.4 us
  waiting for transfers between devices: 77 us -> 101 us
  local copies, waits for them, and re-layouts: 7.23 us -> 2.5 us
  Pallas kernels: 0.44 us -> 2.63 us
    ppermute x24 -> x20, starting transfers between devices: 65.8 us -> 19.4 us  [send(): return lax.ppermute(value, AXES, [(place(*a), place(*b)) for a, b in pairs])]
    ppermute x24 -> x20, waiting for transfers between devices: 56.4 us -> 101 us  [send(): return lax.ppermute(value, AXES, [(place(*a), place(*b)) for a, b in pairs])]
    all_to_all x2 -> x0, starting transfers between devices: 22.8 us -> none  [the longest x1 17 us: relay(): lax.all_to_all(partial_sums, ('ha', 'wa'), split_axis=0, concat_axis=0, t...]
    all_to_all x2 -> x0, waiting for transfers between devices: 20.6 us -> none  [the longest x1 16.7 us: relay(): lax.all_to_all(jnp.broadcast_to(tiles[None], (8, 20, 768)), ('ha', 'wa'),...]
    unnamed x46 -> x8, local copies, waits for them, and re-layouts: 4.37 us -> 0.96 us
    pallas_call x6 -> x5, Pallas kernels: 0.44 us -> 2.63 us  [kernel_call(): pl.pallas_call(body, out_shape=out_shape, in_specs=[pl.BlockSpec(memory_s...]
    reshape x3 -> x0, local copies, waits for them, and re-layouts: 2.14 us -> none  [the longest x1 0.72 us: relay(): latent.reshape(8, 768)]
  transfers between devices with their start and end apart: 26 -> 20, of which waited for: 5 -> 1; matrix products, arithmetic and copies ran while one was open for 2% -> 1% of each run, Pallas kernels for 0% -> 0%
where the time goes in v2:
time: 129 us; the launch traced here: 128 us
  waiting for transfers between devices  101 us (78%)
  starting transfers between devices  19.4 us (15%)
  Pallas kernels  2.63 us (2%)
  local copies, waits for them, and re-layouts  2.5 us (2%)
  other arithmetic  1.62 us (1%)
    ppermute x20, waiting for transfers between devices, send(): return lax.ppermute(value, AXES, [(place(*a), place(*b)) for a, b in pairs])  101 us
    ppermute x20, starting transfers between devices, send(): return lax.ppermute(value, AXES, [(place(*a), place(*b)) for a, b in pairs])  19.4 us
    pallas_call x5, Pallas kernels, kernel_call(): pl.pallas_call(body, out_shape=out_shape, in_specs=[pl.BlockSpec(memory_s...  2.63 us
  transfers between devices with their start and end apart: 20, of which 1 were waited for; matrix products, arithmetic and copies ran while one was open for 1% of the time, Pallas kernels for 0%

profile of v2, /device:TPU:31, one launch (start us, length us, event | category | flops | bytes accessed | tf_op | source)
XLA Modules:
  0.0 127.6 jit_solution(9340238152274929526)
XLA Ops:
  0.0 18.9 %conditional.1 = (bf16[320,384]{1,0:T(8,128)(2,1)}, bf16[192,5184]{1,0:T(8,128)(2,1)S(1)}, bf16[96,3456]{1,0:T(8,128)(2,1)}, bf16[192,1152]{1,0:T(8,128)(2,1)S(1...) conditional(s32[]{:T(128)} %convert_element_type.3, ...), branch_computations={%region_0.0_spmd, %region_1.0_spmd} | conditional | flops 669552 | bytes 35836592 | solution.py:1082
  0.0 2.4 %branch_0_fun.5.refs_0_ = bf16[96,3200]{1,0:T(8,128)(2,1)} custom-call(bf16[192,2592]{1,0:T(8,128)(2,1)} %get-tuple-element.23.refs_0_.k_any, bf16[192,432]{1,0:T(8,128)(2,1)} %get-tuple-element.24.u_any), custom_call_target="tpu_custom_call" | custom-call | flops 1000 | bytes 1000 | tf_op jit(solution)/shard_map/cond/branch_0_fun/pallas_call | solution.py:316
  2.4 0.0 copy-start
  2.4 0.8 collective-permute-start
  3.3 0.7 collective-permute-start.1
  4.0 0.0 collective-permute-done.refs_1_
  4.0 1.5 %collective-permute-start.2 = (bf16[96,3200]{1,0:T(8,128)(2,1)S(1)}, bf16[96,3200]{1,0:T(8,128)(2,1)}, u32[]{:S(2)}, u32[]{:S(2)}) collective-permute-start(bf16[96,3200]{1,0:T(8,128)(2,1)S(1)} %collective-permute-done.refs_1_), channel_id=1, source_target_pairs={{16,17},{17,16},{18,19},{19,18},{24,25},{25,24},{26,27},{27,26}} | collective-permute-start | bytes 1843208 | tf_op jit(solution)/shard_map/cond/branch_0_fun/ppermute | solution.py:306
  5.5 0.0 collective-permute-done.1.refs_2_
  5.5 0.8 copy-done.9
  6.4 0.0 collective-permute-done.2.refs_3_
  6.4 2.0 %collective-permute-start.3 = (bf16[192,5184]{1,0:T(8,128)(2,1)S(1)}, bf16[192,5184]{1,0:T(8,128)(2,1)}, u32[]{:S(2)}, u32[]{:S(2)}) collective-permute-start(bf16[192,5184]{1,0:T(8,128)(2,1)S(1)} %get-tuple-element.90), channel_id=1, source_target_pairs={{16,24},{17,25},{18,26},{19,27}} | collective-permute-start | bytes 5971976 | tf_op jit(solution)/shard_map/cond/branch_0_fun/ppermute | solution.py:306
  8.4 1.5 %collective-permute-start.4 = (bf16[96,3456]{1,0:T(8,128)(2,1)}, bf16[96,3456]{1,0:T(8,128)(2,1)}, u32[]{:S(2)}, u32[]{:S(2)}) collective-permute-start(bf16[96,3456]{1,0:T(8,128)(2,1)} %get-tuple-element.91), channel_id=1, source_target_pairs={{24,16},{25,17},{26,18},{27,19}} | collective-permute-start | bytes 1990664 | tf_op jit(solution)/shard_map/cond/branch_0_fun/ppermute | solution.py:306
  9.9 0.9 pad_maximum_fusion.refs_0_
  10.8 0.0 copy-start.10
  10.8 0.7 collective-permute-start.10
  11.5 0.7 collective-permute-start.6
  12.2 0.7 collective-permute-start.7
  12.9 0.0 collective-permute-done.10.refs_5_
  12.9 1.5 %collective-permute-start.5 = (bf16[192,1152]{1,0:T(8,128)(2,1)S(1)}, bf16[192,1152]{1,0:T(8,128)(2,1)}, u32[]{:S(2)}, u32[]{:S(2)}) collective-permute-start(bf16[192,1152]{1,0:T(8,128)(2,1)S(1)} %get-tuple-element.92), channel_id=1, source_target_pairs={{16,24},{17,25},{18,26},{19,27},{24,16},{25,17},{26,18},{27,19}} | collective-permute-start | bytes 1327112 | tf_op jit(solution)/shard_map/cond/branch_0_fun/ppermute | solution.py:306
  14.4 0.0 collective-permute-done.6.refs_1_
  14.4 0.7 collective-permute-start.8
  15.0 0.0 collective-permute-done.7.refs_2_
  15.1 1.3 %collective-permute-start.9 = (bf16[48,1536]{1,0:T(8,128)(2,1)S(1)}, bf16[48,1536]{1,0:T(8,128)(2,1)}, u32[]{:S(2)}, u32[]{:S(2)}) collective-permute-start(bf16[48,1536]{1,0:T(8,128)(2,1)S(1)} %pad_maximum_fusion.refs_0_), channel_id=1, source_target_pairs={{20,16},{21,17},{22,18},{23,19}} | collective-permute-start | bytes 442376 | tf_op jit(solution)/shard_map/cond/branch_0_fun/ppermute | solution.py:306
  16.4 0.0 collective-permute-done.8.refs_3_
  16.4 0.7 copy-done.19
  17.1 0.0 collective-permute-done.9.refs_4_
  17.1 0.1 branch_0_fun.7
  17.2 1.4 %collective-permute-start.11 = (bf16[640,192]{1,0:T(8,128)(2,1)}, bf16[640,192]{1,0:T(8,128)(2,1)}, u32[]{:S(2)}, u32[]{:S(2)}) collective-permute-start(bf16[640,192]{1,0:T(8,128)(2,1)} %get-tuple-element.96), channel_id=1, source_target_pairs={{16,24},{17,25},{18,26},{19,27}} | collective-permute-start | bytes 737288 | tf_op jit(solution)/shard_map/cond/branch_0_fun/ppermute | solution.py:306
  18.6 0.0 collective-permute-done.5
  18.9 0.7 collective-permute-start.24
  19.6 0.7 collective-permute-start.25
  20.2 0.7 collective-permute-start.26
  20.9 0.7 collective-permute-start.27
  21.6 0.0 collective-permute-done.25.same3
  21.6 0.0 collective-permute-done.26.other2
  21.7 0.7 copy-done.12
  22.3 0.1 copy-done.13
  22.4 0.1 copy-done.14
  22.5 0.1 copy-done.15
  22.6 0.1 shard_map.78
  22.7 0.7 collective-permute-start.28
  23.4 0.7 collective-permute-start.29
  24.1 0.7 collective-permute-start.30
  24.8 1.3 %collective-permute-start.31 = (bf16[32,3072]{1,0:T(8,128)(2,1)}, bf16[32,3072]{1,0:T(8,128)(2,1)S(1)}, u32[]{:S(2)}, u32[]{:S(2)}) collective-permute-start(bf16[32,3072]{1,0:T(8,128)(2,1)} %get-tuple-element.78), channel_id=1, source_target_pairs={{16,3},{17,11},{18,7},{19,15},{24,19},{25,27},{26,23},{27,31}} | collective-permute-start | bytes 589832 | tf_op jit(solution)/shard_map/ppermute | solution.py:306
  26.1 0.0 collective-permute-done.28
  26.1 0.0 collective-permute-done.29
  26.1 100.7 %collective-permute-done.31 = bf16[32,3072]{1,0:T(8,128)(2,1)S(1)} collective-permute-done((bf16[32,3072]{1,0:T(8,128)(2,1)}, bf16[32,3072]{1,0:T(8,128)(2,1)S(1)}, u32[]{:S(2)}, u32[]{:S(2)}) %collective-permute-start.31) | collective-permute-done | bytes 196640 | tf_op jit(solution)/shard_map/ppermute | solution.py:306
  126.9 0.7 select_bitcast_fusion
  (24 shorter events, 0.1 us)
Async XLA Ops:
  2.4 16.2 %copy-start = (bf16[192,2592]{1,0:T(8,128)(2,1)S(1)}, bf16[192,2592]{1,0:T(8,128)(2,1)}, u32[]{:S(2)}) copy-start(bf16[192,2592]{1,0:T(8,128)(2,1)} %get-tuple-element.23.refs_0_.k_any) | copy-start | bytes 2985988 | tf_op jit(solution)/shard_map/cond
  2.4 1.6 %collective-permute-start = (bf16[96,3200]{1,0:T(8,128)(2,1)}, bf16[96,3200]{1,0:T(8,128)(2,1)S(1)}, u32[]{:S(2)}, u32[]{:S(2)}) collective-permute-start(bf16[96,3200]{1,0:T(8,128)(2,1)} %branch_0_fun.5.refs_0_), channel_id=1, source_target_pairs={{16,18},{17,19},{18,16},{19,17},{24,26},{25,27},{26,24},{27,25}} | collective-permute-start | bytes 1843208 | tf_op jit(solution)/shard_map/cond/branch_0_fun/ppermute | solution.py:306
  3.3 2.2 %collective-permute-start.1 = (bf16[96,3200]{1,0:T(8,128)(2,1)}, bf16[96,3200]{1,0:T(8,128)(2,1)S(1)}, u32[]{:S(2)}, u32[]{:S(2)}) collective-permute-start(bf16[96,3200]{1,0:T(8,128)(2,1)} %branch_0_fun.5.refs_0_), channel_id=1, source_target_pairs={{16,17},{17,16},{18,19},{19,18},{24,25},{25,24},{26,27},{27,26}} | collective-permute-start | bytes 1843208 | tf_op jit(solution)/shard_map/cond/branch_0_fun/ppermute | solution.py:306
  4.0 2.4 %copy-start.8 = (bf16[96,3200]{1,0:T(8,128)(2,1)}, bf16[96,3200]{1,0:T(8,128)(2,1)S(1)}, u32[]{:S(2)}) copy-start(bf16[96,3200]{1,0:T(8,128)(2,1)S(1)} %collective-permute-done.refs_1_) | copy-start | bytes 1843204 | tf_op jit(solution)/shard_map/cond
  4.0 2.4 %collective-permute-start.2 = (bf16[96,3200]{1,0:T(8,128)(2,1)S(1)}, bf16[96,3200]{1,0:T(8,128)(2,1)}, u32[]{:S(2)}, u32[]{:S(2)}) collective-permute-start(bf16[96,3200]{1,0:T(8,128)(2,1)S(1)} %collective-permute-done.refs_1_), channel_id=1, source_target_pairs={{16,17},{17,16},{18,19},{19,18},{24,25},{25,24},{26,27},{27,26}} | collective-permute-start | bytes 1843208 | tf_op jit(solution)/shard_map/cond/branch_0_fun/ppermute | solution.py:306
  5.5 0.8 copy-start.9
  6.4 12.2 %collective-permute-start.3 = (bf16[192,5184]{1,0:T(8,128)(2,1)S(1)}, bf16[192,5184]{1,0:T(8,128)(2,1)}, u32[]{:S(2)}, u32[]{:S(2)}) collective-permute-start(bf16[192,5184]{1,0:T(8,128)(2,1)S(1)} %get-tuple-element.90), channel_id=1, source_target_pairs={{16,24},{17,25},{18,26},{19,27}} | collective-permute-start | bytes 5971976 | tf_op jit(solution)/shard_map/cond/branch_0_fun/ppermute | solution.py:306
  8.4 10.2 %collective-permute-start.4 = (bf16[96,3456]{1,0:T(8,128)(2,1)}, bf16[96,3456]{1,0:T(8,128)(2,1)}, u32[]{:S(2)}, u32[]{:S(2)}) collective-permute-start(bf16[96,3456]{1,0:T(8,128)(2,1)} %get-tuple-element.91), channel_id=1, source_target_pairs={{24,16},{25,17},{26,18},{27,19}} | collective-permute-start | bytes 1990664 | tf_op jit(solution)/shard_map/cond/branch_0_fun/ppermute | solution.py:306
  10.8 6.2 %copy-start.10 = (bf16[48,1536]{1,0:T(8,128)(2,1)}, bf16[48,1536]{1,0:T(8,128)(2,1)S(1)}, u32[]{:S(2)}) copy-start(bf16[48,1536]{1,0:T(8,128)(2,1)S(1)} %pad_maximum_fusion.refs_0_) | copy-start | bytes 442372 | tf_op jit(solution)/shard_map/cond
  10.8 2.0 %collective-permute-start.10 = (bf16[48,1536]{1,0:T(8,128)(2,1)S(1)}, bf16[48,1536]{1,0:T(8,128)(2,1)S(1)}, u32[]{:S(2)}, u32[]{:S(2)}) collective-permute-start(bf16[48,1536]{1,0:T(8,128)(2,1)S(1)} %pad_maximum_fusion.refs_0_), channel_id=1, source_target_pairs={{21,16},{20,17},{23,18},{22,19}} | collective-permute-start | bytes 442376 | tf_op jit(solution)/shard_map/cond/branch_0_fun/ppermute | solution.py:306
  11.5 2.9 %collective-permute-start.6 = (bf16[48,1536]{1,0:T(8,128)(2,1)S(1)}, bf16[48,1536]{1,0:T(8,128)(2,1)S(1)}, u32[]{:S(2)}, u32[]{:S(2)}) collective-permute-start(bf16[48,1536]{1,0:T(8,128)(2,1)S(1)} %pad_maximum_fusion.refs_0_), channel_id=1, source_target_pairs={{17,16},{16,17},{19,18},{18,19}} | collective-permute-start | bytes 442376 | tf_op jit(solution)/shard_map/cond/branch_0_fun/ppermute | solution.py:306
  12.2 2.9 %collective-permute-start.7 = (bf16[48,1536]{1,0:T(8,128)(2,1)S(1)}, bf16[48,1536]{1,0:T(8,128)(2,1)S(1)}, u32[]{:S(2)}, u32[]{:S(2)}) collective-permute-start(bf16[48,1536]{1,0:T(8,128)(2,1)S(1)} %pad_maximum_fusion.refs_0_), channel_id=1, source_target_pairs={{18,16},{19,17},{20,18},{21,19}} | collective-permute-start | bytes 442376 | tf_op jit(solution)/shard_map/cond/branch_0_fun/ppermute | solution.py:306
  12.9 4.2 %copy-start.16 = (bf16[48,1536]{1,0:T(8,128)(2,1)}, bf16[48,1536]{1,0:T(8,128)(2,1)S(1)}, u32[]{:S(2)}) copy-start(bf16[48,1536]{1,0:T(8,128)(2,1)S(1)} %collective-permute-done.10.refs_5_) | copy-start | bytes 442372 | tf_op jit(solution)/shard_map/cond
  12.9 5.7 %collective-permute-start.5 = (bf16[192,1152]{1,0:T(8,128)(2,1)S(1)}, bf16[192,1152]{1,0:T(8,128)(2,1)}, u32[]{:S(2)}, u32[]{:S(2)}) collective-permute-start(bf16[192,1152]{1,0:T(8,128)(2,1)S(1)} %get-tuple-element.92), channel_id=1, source_target_pairs={{16,24},{17,25},{18,26},{19,27},{24,16},{25,17},{26,18},{27,19}} | collective-permute-start | bytes 1327112 | tf_op jit(solution)/shard_map/cond/branch_0_fun/ppermute | solution.py:306
  14.4 2.7 %copy-start.17 = (bf16[48,1536]{1,0:T(8,128)(2,1)}, bf16[48,1536]{1,0:T(8,128)(2,1)S(1)}, u32[]{:S(2)}) copy-start(bf16[48,1536]{1,0:T(8,128)(2,1)S(1)} %collective-permute-done.6.refs_1_) | copy-start | bytes 442372 | tf_op jit(solution)/shard_map/cond
  14.4 2.0 %collective-permute-start.8 = (bf16[48,1536]{1,0:T(8,128)(2,1)S(1)}, bf16[48,1536]{1,0:T(8,128)(2,1)S(1)}, u32[]{:S(2)}, u32[]{:S(2)}) collective-permute-start(bf16[48,1536]{1,0:T(8,128)(2,1)S(1)} %pad_maximum_fusion.refs_0_), channel_id=1, source_target_pairs={{19,16},{18,17},{21,18},{20,19}} | collective-permute-start | bytes 442376 | tf_op jit(solution)/shard_map/cond/branch_0_fun/ppermute | solution.py:306
  15.1 2.0 %copy-start.18 = (bf16[48,1536]{1,0:T(8,128)(2,1)}, bf16[48,1536]{1,0:T(8,128)(2,1)S(1)}, u32[]{:S(2)}) copy-start(bf16[48,1536]{1,0:T(8,128)(2,1)S(1)} %collective-permute-done.7.refs_2_) | copy-start | bytes 442372 | tf_op jit(solution)/shard_map/cond
  15.1 2.0 %collective-permute-start.9 = (bf16[48,1536]{1,0:T(8,128)(2,1)S(1)}, bf16[48,1536]{1,0:T(8,128)(2,1)}, u32[]{:S(2)}, u32[]{:S(2)}) collective-permute-start(bf16[48,1536]{1,0:T(8,128)(2,1)S(1)} %pad_maximum_fusion.refs_0_), channel_id=1, source_target_pairs={{20,16},{21,17},{22,18},{23,19}} | collective-permute-start | bytes 442376 | tf_op jit(solution)/shard_map/cond/branch_0_fun/ppermute | solution.py:306
  16.4 0.7 copy-start.19
  17.2 1.4 %collective-permute-start.11 = (bf16[640,192]{1,0:T(8,128)(2,1)}, bf16[640,192]{1,0:T(8,128)(2,1)}, u32[]{:S(2)}, u32[]{:S(2)}) collective-permute-start(bf16[640,192]{1,0:T(8,128)(2,1)} %get-tuple-element.96), channel_id=1, source_target_pairs={{16,24},{17,25},{18,26},{19,27}} | collective-permute-start | bytes 737288 | tf_op jit(solution)/shard_map/cond/branch_0_fun/ppermute | solution.py:306
  18.9 2.7 %collective-permute-start.24 = (bf16[320,384]{1,0:T(8,128)(2,1)}, bf16[320,384]{1,0:T(8,128)(2,1)S(1)}, u32[]{:S(2)}, u32[]{:S(2)}) collective-permute-start(bf16[320,384]{1,0:T(8,128)(2,1)} %get-tuple-element.65), channel_id=1, source_target_pairs={{8,16},{9,17},{10,18},{11,19}} | collective-permute-start | bytes 737288 | tf_op jit(solution)/shard_map/ppermute | solution.py:306
  19.6 2.1 %collective-permute-start.25 = (bf16[320,384]{1,0:T(8,128)(2,1)}, bf16[320,384]{1,0:T(8,128)(2,1)S(1)}, u32[]{:S(2)}, u32[]{:S(2)}) collective-permute-start(bf16[320,384]{1,0:T(8,128)(2,1)} %get-tuple-element.65), channel_id=1, source_target_pairs={{8,24},{9,25},{10,26},{11,27}} | collective-permute-start | bytes 737288 | tf_op jit(solution)/shard_map/ppermute | solution.py:306
  20.2 1.4 %collective-permute-start.26 = (bf16[320,384]{1,0:T(8,128)(2,1)}, bf16[320,384]{1,0:T(8,128)(2,1)S(1)}, u32[]{:S(2)}, u32[]{:S(2)}) collective-permute-start(bf16[320,384]{1,0:T(8,128)(2,1)} %get-tuple-element.65), channel_id=1, source_target_pairs={{8,17},{9,16},{10,19},{11,18}} | collective-permute-start | bytes 737288 | tf_op jit(solution)/shard_map/ppermute | solution.py:306
  20.9 0.7 collective-permute-start.27
  21.6 0.7 copy-start.12
  21.6 0.8 copy-start.13
  21.7 0.9 copy-start.14
  21.7 1.0 copy-start.15
  22.7 3.4 %collective-permute-start.28 = (bf16[32,3072]{1,0:T(8,128)(2,1)}, bf16[32,3072]{1,0:T(8,128)(2,1)S(1)}, u32[]{:S(2)}, u32[]{:S(2)}) collective-permute-start(bf16[32,3072]{1,0:T(8,128)(2,1)} %get-tuple-element.75), channel_id=1, source_target_pairs={{16,0},{17,8},{18,4},{19,12},{24,16},{25,24},{26,20},{27,28}} | collective-permute-start | bytes 589832 | tf_op jit(solution)/shard_map/ppermute | solution.py:306
  23.4 2.7 %collective-permute-start.29 = (bf16[32,3072]{1,0:T(8,128)(2,1)}, bf16[32,3072]{1,0:T(8,128)(2,1)S(1)}, u32[]{:S(2)}, u32[]{:S(2)}) collective-permute-start(bf16[32,3072]{1,0:T(8,128)(2,1)} %get-tuple-element.76), channel_id=1, source_target_pairs={{16,1},{17,9},{18,5},{19,13},{24,17},{25,25},{26,21},{27,29}} | collective-permute-start | bytes 589832 | tf_op jit(solution)/shard_map/ppermute | solution.py:306
  24.1 2.0 %collective-permute-start.30 = (bf16[32,3072]{1,0:T(8,128)(2,1)}, bf16[32,3072]{1,0:T(8,128)(2,1)S(1)}, u32[]{:S(2)}, u32[]{:S(2)}) collective-permute-start(bf16[32,3072]{1,0:T(8,128)(2,1)} %get-tuple-element.77), channel_id=1, source_target_pairs={{16,2},{17,10},{18,6},{19,14},{24,18},{25,26},{26,22},{27,30}} | collective-permute-start | bytes 589832 | tf_op jit(solution)/shard_map/ppermute | solution.py:306
  24.8 102.1 %collective-permute-start.31 = (bf16[32,3072]{1,0:T(8,128)(2,1)}, bf16[32,3072]{1,0:T(8,128)(2,1)S(1)}, u32[]{:S(2)}, u32[]{:S(2)}) collective-permute-start(bf16[32,3072]{1,0:T(8,128)(2,1)} %get-tuple-element.78), channel_id=1, source_target_pairs={{16,3},{17,11},{18,7},{19,15},{24,19},{25,27},{26,23},{27,31}} | collective-permute-start | bytes 589832 | tf_op jit(solution)/shard_map/ppermute | solution.py:306

commit v3 on v2

--- a/solution.py
+++ b/solution.py
@@ -295,7 +295,7 @@
 
 
 AXES = ("segment", "ha", "wa")
-VMEM = 60 * 1024 * 1024
+MIB = 1024 * 1024
 
 
 def place(s, h, w):
@@ -312,15 +312,15 @@
     ]
 
 
-def kernel_call(body, out_shape, scratch, *args, copies=0, flops=1000):
+def kernel_call(body, out_shape, scratch, *args, copies=0, vmem=16, cost=1000, place=pl.ANY):
     return pl.pallas_call(
         body,
         out_shape=out_shape,
-        in_specs=[pl.BlockSpec(memory_space=pl.ANY)] * len(args),
+        in_specs=[pl.BlockSpec(memory_space=place)] * len(args),
         out_specs=jax.tree.map(lambda _: pl.BlockSpec(memory_space=pl.ANY), out_shape),
         scratch_shapes=scratch + [pltpu.SemaphoreType.DMA((copies,))],
-        compiler_params=pltpu.CompilerParams(vmem_limit_bytes=VMEM),
-        cost_estimate=pl.CostEstimate(flops=flops, bytes_accessed=1000, transcendentals=0),
+        compiler_params=pltpu.CompilerParams(vmem_limit_bytes=vmem * MIB),
+        cost_estimate=pl.CostEstimate(flops=1000 * cost, bytes_accessed=1000, transcendentals=0),
     )(*args)
 
 
@@ -473,14 +473,14 @@
         out_ref[0:128, :] = buf[:, 0:128].astype(jnp.bfloat16)
         tail = jnp.concatenate([buf[0:64, 128:192], buf[64:128, 128:192]], axis=1)
         out_ref[128:192, :] = tail.astype(jnp.bfloat16)
-        wait_all(start_all([(out_ref, out_any)], sems))
+        wait_all(start_all([(out_ref, out_any.at[n]) for n in range(8)], sems))
 
 
 def conv0(gathered, k):
     f32, bf16 = jnp.float32, jnp.bfloat16
     return kernel_call(
         conv0_body,
-        jax.ShapeDtypeStruct((192, 128), bf16),
+        jax.ShapeDtypeStruct((8, 192, 128), bf16),
         [
             pltpu.VMEM((8, 12, 768), bf16),
             pltpu.VMEM((192, 2592), bf16),
@@ -493,58 +493,62 @@
         ],
         gathered, k,
         copies=8,
-    )
-
-
-def fold_body(own_any, far_any, out_any, own, far, out, sems):
+        cost=20 * 10**6,
+    )
+
+
+def join_body(own, nz, nx, nd, mine_any, other_any, cat, taps, sems):
     s, h = lax.axis_index("segment"), lax.axis_index("ha")
+
+    @pl.when((s < 2) & (h < 2))
+    def _():
+        sending = []
+        for half, (near, far, target) in enumerate(((own, nz, mine_any), (nx, nd, other_any))):
+            for z in range(2):
+
+                @pl.when(h == z)
+                def _():
+                    for first, pieces in ((z, near), (1 - z, far)):
+                        for n in range(2):
+                            at = (first + 2 * n) * 432
+                            cat[:, at : at + 432] = pieces[:, n * 432 : (n + 1) * 432]
+
+            for tap in range(9):
+                taps[half, :, tap * 256 : tap * 256 + 192] = cat[:, tap * 192 : (tap + 1) * 192]
+                taps[half, :, tap * 256 + 192 : (tap + 1) * 256] = jnp.zeros((192, 64), jnp.bfloat16)
+            sending += start_all([(taps.at[half], target)], sems, half)
+        wait_all(sending)
+
+
+def join(pieces):
+    bf16 = jnp.bfloat16
+    return kernel_call(
+        join_body,
+        (jax.ShapeDtypeStruct((192, 2304), bf16), jax.ShapeDtypeStruct((192, 2304), bf16)),
+        [pltpu.VMEM((192, 1728), bf16), pltpu.VMEM((2, 192, 2304), bf16)],
+        *pieces,
+        copies=2,
+        vmem=8,
+        cost=20 * 10**6,
+        place=pltpu.VMEM,
+    )
+
+
+def up0_body(*refs):
+    y_any, taps_any, out_any = refs[0], refs[1:3], refs[3]
+    y, taps, hbuf, hs, p, t, out_ref, sems = refs[4:]
+    s, h, w = (lax.axis_index(axis) for axis in AXES)
 
     @pl.when((s == 0) & (h < 2))
     def _():
-        wait_all(start_all([(own_any, own), (far_any, far)], sems))
-        out[...] = (own[...].astype(jnp.float32) + far[...].astype(jnp.float32)).astype(jnp.bfloat16)
-        wait_all(start_all([(out, out_any)], sems))
-
-
-def fold(own, far):
-    shape = (192, 128)
-    return kernel_call(
-        fold_body,
-        jax.ShapeDtypeStruct(shape, jnp.bfloat16),
-        [pltpu.VMEM(shape, jnp.bfloat16)] * 3,
-        own, far,
-        copies=2,
-    )
-
-
-def join_taps(h, pieces_own, pieces_z, cat_ref, taps_ref, width, lanes):
-    for z in range(2):
-
-        @pl.when(h == z)
-        def _():
-            for mine, pieces in ((z, pieces_own), (1 - z, pieces_z)):
-                for number, piece in enumerate(pieces):
-                    at = (mine + 2 * number) * 432
-                    cat_ref[:, at : at + 432] = piece
-
-    for tap in range(9):
-        taps_ref[:, tap * lanes : tap * lanes + width] = cat_ref[:, tap * width : (tap + 1) * width]
-
-
-def up0_body(*refs):
-    sums_any, ups_any, out_any = refs[0:4], refs[4:8], refs[8]
-    y, own, nz, nx, nd = refs[9:14]
-    cat, taps, hbuf, hs, p, t, out_ref, sems = refs[14:]
-    s, h = lax.axis_index("segment"), lax.axis_index("ha")
-
-    @pl.when((s == 0) & (h < 2))
-    def _():
-        coming = start_all([(a, y.at[n]) for n, a in enumerate(sums_any)], sems)
-        rising = start_all(list(zip(ups_any, (own, nz, nx, nd))), sems, 4)
+        coming = start_all([(y_any, y)], sems)
+        rising = start_all([(a, taps.at[n]) for n, a in enumerate(taps_any)], sems, 1)
         wait_all(coming)
         halves = []
         for side in range(2):
-            total = y[2 * side].astype(jnp.float32) + y[2 * side + 1].astype(jnp.float32)
+            total = y[side].astype(jnp.float32)
+            for hh in range(1, 4):
+                total = total + y[hh * 2 + side].astype(jnp.float32)
             tail = jnp.concatenate([total[128:192, 0:64], total[128:192, 64:128]], axis=0)
             halves.append(jnp.concatenate([total[0:128], tail], axis=1))
         squares = sum(jnp.sum(half * half, axis=1, keepdims=True) for half in halves)
@@ -552,19 +556,13 @@
         active = [silu(half * inverse) for half in halves]
         hs[...] = jnp.zeros_like(hs)
         for k in range(2):
-            hbuf[...] = active[k]
+            hbuf[...] = jnp.where(w == k, active[0], active[1])
             for frame in range(4):
                 for r in range(8):
                     to, at = frame * 72 + r * 8, (frame * 8 + r) * 4
                     hs[k, to : to + 4, :] = hbuf[at : at + 4, :]
         wait_all(rising)
-        for k, (mine, other) in enumerate(((own, nz), (nx, nd))):
-            join_taps(h, (mine[0:192], mine[192:384]), (other[0:192], other[192:384]), cat, taps, 192, 256)
-            term = dot(hs[k].astype(jnp.bfloat16), taps[...])
-            if k == 0:
-                p[...] = term
-            else:
-                p[...] = p[...] + term
+        p[...] = dot(hs[0].astype(jnp.bfloat16), taps[0]) + dot(hs[1].astype(jnp.bfloat16), taps[1])
         upsample(p, t, 8, 4, 256)
         column = index_of((16, 192))
         out_ref[...] = jnp.zeros_like(out_ref)
@@ -585,24 +583,22 @@
         wait_all(start_all([(out_ref, out_any)], sems))
 
 
-def up0(sums, ups):
+def up0(partials, ups):
     f32, bf16 = jnp.float32, jnp.bfloat16
     return kernel_call(
         up0_body,
         jax.ShapeDtypeStruct((768, 192), bf16),
         [
-            pltpu.VMEM((4, 192, 128), bf16),
-            *[pltpu.VMEM((384, 432), bf16)] * 4,
-            pltpu.VMEM((192, 1728), bf16),
-            pltpu.VMEM((192, 2304), bf16),
+            pltpu.VMEM((8, 192, 128), bf16),
+            pltpu.VMEM((2, 192, 2304), bf16),
             pltpu.VMEM((128, 192), f32),
             pltpu.VMEM((2, 288, 192), f32),
             pltpu.VMEM((288, 2304), f32),
             pltpu.VMEM((4, 576, 128), f32),
             pltpu.VMEM((768, 192), bf16),
         ],
-        *sums, *ups,
-        copies=8,
+        partials, *ups,
+        copies=3,
     )
 
 
@@ -616,17 +612,17 @@
 
 
 def section1_body(x_any, g_any, *refs):
-    kernels_any, ups_any, out_any = refs[0:4], refs[4:8], refs[8]
-    x_ref, g_ref = refs[9:11]
-    k_own, k_z, k_x, k_d, own, nz, nx, nd = refs[11:19]
-    gf, full, base, xx, acc, hs, cat, taps, p, t, out_ref, sems = refs[19:]
+    kernels_any, taps_any, out_any = refs[0:4], refs[4:6], refs[6]
+    x_ref, g_ref = refs[7:9]
+    k_own, k_z, k_x, k_d = refs[9:13]
+    gf, full, base, xx, acc, hs, taps, p, t, out_ref, sems = refs[13:]
     s, h, w = (lax.axis_index(axis) for axis in AXES)
 
     @pl.when((s == 1) & (h < 2))
     def _():
         coming = start_all([(x_any, x_ref), (g_any, g_ref)], sems)
         arriving = start_all(list(zip(kernels_any, (k_own, k_z, k_x, k_d))), sems, 2)
-        rising = start_all(list(zip(ups_any, (own, nz, nx, nd))), sems, 6)
+        rising = start_all([(a, taps.at[n]) for n, a in enumerate(taps_any)], sems, 6)
         wait_all(coming)
 
         @pl.when(w == 0)
@@ -674,13 +670,7 @@
             hs[k, 0:352] = jnp.where(keep, silu(acc[k] * inverse), 0.0).astype(jnp.bfloat16)
             hs[k, 352:384] = jnp.zeros((32, 192), jnp.bfloat16)
         wait_all(rising)
-        for k, (mine, other) in enumerate(((own, nz), (nx, nd))):
-            join_taps(h, (mine[0:192], mine[192:384]), (other[0:192], other[192:384]), cat, taps, 192, 256)
-            term = dot(hs[k], taps[...])
-            if k == 0:
-                p[...] = term
-            else:
-                p[...] = p[...] + term
+        p[...] = dot(hs[0], taps[0]) + dot(hs[1], taps[1])
         upsample(p, t, 16, 8, 256)
         out_ref[...] = jnp.zeros_like(out_ref)
         for z in range(2):
@@ -709,21 +699,20 @@
             pltpu.VMEM((768, 192), bf16),
             pltpu.VMEM((8, 12, 768), bf16),
             *[pltpu.VMEM((192, 2592), bf16)] * 4,
-            *[pltpu.VMEM((384, 432), bf16)] * 4,
             pltpu.VMEM((8, 12, 768), f32),
             pltpu.VMEM((576, 192), f32),
             pltpu.VMEM((768, 192), f32),
             pltpu.VMEM((768, 576), bf16),
             pltpu.VMEM((2, 352, 192), f32),
             pltpu.VMEM((2, 384, 192), bf16),
-            pltpu.VMEM((192, 1728), bf16),
-            pltpu.VMEM((192, 2304), bf16),
+            pltpu.VMEM((2, 192, 2304), bf16),
             pltpu.VMEM((384, 2304), f32),
             pltpu.VMEM((4, 768, 128), f32),
             pltpu.VMEM((320, 384), bf16),
         ],
         frames, gathered, *kernels, *ups,
-        copies=10,
+        copies=8,
+        vmem=26,
     )
 
 
@@ -806,6 +795,7 @@
         ],
         *pieces,
         copies=4,
+        vmem=12,
     )
 
 
@@ -864,6 +854,8 @@
         ],
         *bands,
         copies=6,
+        vmem=16,
+        cost=60 * 10**6,
     )
 
 
@@ -1022,6 +1014,26 @@
         ],
         *received, c, c_sent, d, *kernels,
         copies=8,
+        vmem=44,
+    )
+
+
+def beside_body(near_any, far_any, out_any, near, far, out, sems):
+    wait_all(start_all([(near_any, near), (far_any, far)], sems))
+    out[:, 0:432] = near[...]
+    out[:, 432:864] = far[...]
+    wait_all(start_all([(out, out_any)], sems))
+
+
+def beside(near, far):
+    shape, bf16 = (192, 864), jnp.bfloat16
+    return kernel_call(
+        beside_body,
+        jax.ShapeDtypeStruct(shape, bf16),
+        [pltpu.VMEM((192, 432), bf16), pltpu.VMEM((192, 432), bf16), pltpu.VMEM(shape, bf16)],
+        near, far,
+        copies=2,
+        cost=15000000,
     )
 
 
@@ -1042,18 +1054,16 @@
     gathered = lax.all_to_all(
         spread_tiles(latent, cache_a, cache_b), ("ha", "wa"), split_axis=0, concat_axis=0, tiled=True
     )
-    ups = jnp.concatenate([u, u_far], axis=0)
-    gathered, ups = lax.optimization_barrier((gathered, ups))
+    ups = beside(u, u_far)
     u_z, u_x, u_d = (send(ups, square((0, 1), dh, dw)) for dh, dw in ((1, 0), (0, 1), (1, 1)))
     partial_sums = conv0(gathered, k)
     partial_sums, k_x, k_z = lax.optimization_barrier((partial_sums, k_x, k_z))
-    far_sums = send(partial_sums, [((0, h_ + 2, w_), (0, h_, w_)) for h_ in range(2) for w_ in range(2)])
     k_d = send(k_z, square((1,), 0, 1))
-    sums = fold(partial_sums, far_sums)
-    sums = [sums] + [send(sums, square((0,), dh, dw)) for dh, dw in ((1, 0), (0, 1), (1, 1))]
-    risen = up0(sums, (ups, u_z, u_x, u_d))
+    partials = lax.all_to_all(partial_sums, ("ha", "wa"), split_axis=0, concat_axis=0, tiled=True)
+    taps = join((ups, u_z, u_x, u_d))
+    risen = up0(partials, taps)
     given = send(risen, [((0, h_, w_), (1, h_, w_)) for h_ in range(2) for w_ in range(2)])
-    out1 = section1(given, gathered, (k, k_z, k_x, k_d), (ups, u_z, u_x, u_d))
+    out1 = section1(given, gathered, (k, k_z, k_x, k_d), taps)
     return (out1, *blank(k, LATER))
 
 
@@ -1066,8 +1076,7 @@
         if n + dw
     ]
     picked = pick(k, u)
-    picked_x, picked_z = send(picked, square((2, 3), 0, 1)), send(picked, square((2, 3), 1, 0))
-    picked_d = send(picked_z, square((2, 3), 0, 1))
+    picked_x, picked_z, picked_d = (send(picked, square((2, 3), dh, dw)) for dh, dw in ((0, 1), (1, 0), (1, 1)))
     k2, k3, u23 = merge((picked, picked_z, picked_x, picked_d))
     pairs = [((s_, h_, w_), (s_ ^ 1, h_, w_)) for s_ in (2, 3) for h_ in range(2) for w_ in range(2)]
     rise, fall = [pair for pair in pairs if pair[0][0] == 2], [pair for pair in pairs if pair[0][0] == 3]

time: 129 us -> 112 us (0.87)
  waiting for transfers between devices: 101 us -> 88.5 us
  local copies, waits for them, and re-layouts: 2.5 us -> 0.01 us
  starting transfers between devices: 19.4 us -> 17.9 us
    ppermute x20, waiting for transfers between devices: 101 us -> 88.5 us  [send(): return lax.ppermute(value, AXES, [(place(*a), place(*b)) for a, b in pairs])]
    cond x16 -> x2, local copies, waits for them, and re-layouts: 1.54 us -> 0.01 us
    ppermute x20, starting transfers between devices: 19.4 us -> 17.9 us  [send(): return lax.ppermute(value, AXES, [(place(*a), place(*b)) for a, b in pairs])]
where the time goes in v3:
time: 112 us; the launch traced here: 111 us
  waiting for transfers between devices  88.5 us (79%)
  starting transfers between devices  17.9 us (16%)
  Pallas kernels  2.25 us (2%)
  other arithmetic  1.62 us (1%)
    ppermute x20, waiting for transfers between devices, send(): return lax.ppermute(value, AXES, [(place(*a), place(*b)) for a, b in pairs])  88.5 us
    ppermute x20, starting transfers between devices, send(): return lax.ppermute(value, AXES, [(place(*a), place(*b)) for a, b in pairs])  17.9 us
    pallas_call x5, Pallas kernels, kernel_call(): pl.pallas_call(body, out_shape=out_shape, in_specs=[pl.BlockSpec(memory_s...  2.25 us
  transfers between devices with their start and end apart: 20, of which 1 were waited for; matrix products, arithmetic and copies ran while one was open for 1% of the time, Pallas kernels for 0%

profile of v3, /device:TPU:31, one launch (start us, length us, event | category | flops | bytes accessed | tf_op | source)
XLA Modules:
  0.0 110.8 jit_solution(13680952203045668699)
XLA Ops:
  0.0 15.1 %conditional.1 = (bf16[320,384]{1,0:T(8,128)(2,1)}, bf16[192,5184]{1,0:T(8,128)(2,1)}, bf16[96,3456]{1,0:T(8,128)(2,1)}, bf16[192,1152]{1,0:T(8,128)(2,1)}, bf16...) conditional(s32[]{:T(128)} %convert_element_type.3, ...), branch_computations={%region_0.0_spmd, %region_1.0_spmd} | conditional | flops 60003295232 | bytes 34094628 | solution.py:1091
  0.0 1.7 %branch_0_fun.5.refs_0_ = bf16[96,3200]{1,0:T(8,128)(2,1)S(1)} custom-call(bf16[192,2592]{1,0:T(8,128)(2,1)} %get-tuple-element.23.refs_0_.k_any, bf16[192,432]{1,0:T(8,128)(2,1)} %get-tuple-element.24.u_any), custom_call_target="tpu_custom_call" | custom-call | flops 1000000 | bytes 1000 | tf_op jit(solution)/shard_map/cond/branch_0_fun/pallas_call | solution.py:316
  1.7 0.7 collective-permute-start.10
  2.5 0.7 collective-permute-start.8
  3.2 0.7 collective-permute-start.9
  3.9 0.9 pad_maximum_fusion.refs_0_
  4.8 0.7 collective-permute-start.14
  5.5 0.7 collective-permute-start.15
  6.1 0.0 collective-permute-done.10.refs_3_
  6.1 0.7 collective-permute-start.16
  6.8 0.0 collective-permute-done.8.refs_1_
  6.8 0.7 collective-permute-start.17
  7.5 0.0 collective-permute-done.9.refs_2_
  7.5 0.7 collective-permute-start.18
  8.2 0.1 branch_0_fun.6
  8.3 0.0 collective-permute-done.14.refs_1_
  8.3 2.0 %collective-permute-start.11 = (bf16[192,5184]{1,0:T(8,128)(2,1)}, bf16[192,5184]{1,0:T(8,128)(2,1)}, u32[]{:S(2)}, u32[]{:S(2)}) collective-permute-start(bf16[192,5184]{1,0:T(8,128)(2,1)} %get-tuple-element.90), channel_id=1, source_target_pairs={{16,24},{17,25},{18,26},{19,27}} | collective-permute-start | bytes 5971976 | tf_op jit(solution)/shard_map/cond/branch_0_fun/ppermute | solution.py:306
  10.2 0.0 collective-permute-done.15.refs_2_
  10.2 1.5 %collective-permute-start.12 = (bf16[96,3456]{1,0:T(8,128)(2,1)}, bf16[96,3456]{1,0:T(8,128)(2,1)}, u32[]{:S(2)}, u32[]{:S(2)}) collective-permute-start(bf16[96,3456]{1,0:T(8,128)(2,1)} %get-tuple-element.91), channel_id=1, source_target_pairs={{24,16},{25,17},{26,18},{27,19}} | collective-permute-start | bytes 1990664 | tf_op jit(solution)/shard_map/cond/branch_0_fun/ppermute | solution.py:306
  11.8 0.0 collective-permute-done.16.refs_3_
  11.8 1.6 %collective-permute-start.13 = (bf16[192,1152]{1,0:T(8,128)(2,1)}, bf16[192,1152]{1,0:T(8,128)(2,1)}, u32[]{:S(2)}, u32[]{:S(2)}) collective-permute-start(bf16[192,1152]{1,0:T(8,128)(2,1)} %get-tuple-element.92), channel_id=1, source_target_pairs={{16,24},{17,25},{18,26},{19,27},{24,16},{25,17},{26,18},{27,19}} | collective-permute-start | bytes 1327112 | tf_op jit(solution)/shard_map/cond/branch_0_fun/ppermute | solution.py:306
  13.3 0.0 collective-permute-done.17.refs_4_
  13.3 0.0 collective-permute-done.18.refs_5_
  13.3 0.1 branch_0_fun.7
  13.4 1.4 %collective-permute-start.19 = (bf16[640,192]{1,0:T(8,128)(2,1)}, bf16[640,192]{1,0:T(8,128)(2,1)}, u32[]{:S(2)}, u32[]{:S(2)}) collective-permute-start(bf16[640,192]{1,0:T(8,128)(2,1)} %get-tuple-element.96), channel_id=1, source_target_pairs={{16,24},{17,25},{18,26},{19,27}} | collective-permute-start | bytes 737288 | tf_op jit(solution)/shard_map/cond/branch_0_fun/ppermute | solution.py:306
  14.8 0.0 copy-done.8
  14.8 0.0 collective-permute-done.19
  14.8 0.0 collective-permute-done.13
  14.8 0.0 collective-permute-done.12
  14.9 0.0 collective-permute-done.11
  15.1 0.7 collective-permute-start.20
  15.8 0.7 collective-permute-start.21
  16.5 0.7 collective-permute-start.22
  17.1 0.7 collective-permute-start.23
  17.8 0.0 collective-permute-done.20.same2
  17.8 0.0 collective-permute-done.21.same3
  17.9 0.0 collective-permute-done.22.other2
  17.9 0.0 collective-permute-done.23.other3
  17.9 0.4 shard_map.78
  18.3 0.7 collective-permute-start.24
  19.0 0.7 collective-permute-start.25
  19.6 0.7 collective-permute-start.26
  20.3 1.3 %collective-permute-start.27 = (bf16[32,3072]{1,0:T(8,128)(2,1)S(1)}, bf16[32,3072]{1,0:T(8,128)(2,1)S(1)}, u32[]{:S(2)}, u32[]{:S(2)}) collective-permute-start(bf16[32,3072]{1,0:T(8,128)(2,1)S(1)} %get-tuple-element.78), channel_id=1, source_target_pairs={{16,3},{17,11},{18,7},{19,15},{24,19},{25,27},{26,23},{27,31}} | collective-permute-start | bytes 589832 | tf_op jit(solution)/shard_map/ppermute | solution.py:306
  21.6 0.0 collective-permute-done.24
  21.6 0.0 collective-permute-done.25
  21.7 0.0 collective-permute-done.26
  21.7 88.4 %collective-permute-done.27 = bf16[32,3072]{1,0:T(8,128)(2,1)S(1)} collective-permute-done((bf16[32,3072]{1,0:T(8,128)(2,1)S(1)}, bf16[32,3072]{1,0:T(8,128)(2,1)S(1)}, u32[]{:S(2)}, u32[]{:S(2)}) %collective-permute-start.27) | collective-permute-done | bytes 196640 | tf_op jit(solution)/shard_map/ppermute | solution.py:306
  110.1 0.7 select_bitcast_fusion
  (2 shorter events, 0.0 us)
Async XLA Ops:
  1.7 4.4 %collective-permute-start.10 = (bf16[96,3200]{1,0:T(8,128)(2,1)S(1)}, bf16[96,3200]{1,0:T(8,128)(2,1)S(1)}, u32[]{:S(2)}, u32[]{:S(2)}) collective-permute-start(bf16[96,3200]{1,0:T(8,128)(2,1)S(1)} %branch_0_fun.5.refs_0_), channel_id=1, source_target_pairs={{16,19},{17,18},{18,17},{19,16},{24,27},{25,26},{26,25},{27,24}} | collective-permute-start | bytes 1843208 | tf_op jit(solution)/shard_map/cond/branch_0_fun/ppermute | solution.py:306
  2.5 4.4 %collective-permute-start.8 = (bf16[96,3200]{1,0:T(8,128)(2,1)S(1)}, bf16[96,3200]{1,0:T(8,128)(2,1)S(1)}, u32[]{:S(2)}, u32[]{:S(2)}) collective-permute-start(bf16[96,3200]{1,0:T(8,128)(2,1)S(1)} %branch_0_fun.5.refs_0_), channel_id=1, source_target_pairs={{16,18},{17,19},{18,16},{19,17},{24,26},{25,27},{26,24},{27,25}} | collective-permute-start | bytes 1843208 | tf_op jit(solution)/shard_map/cond/branch_0_fun/ppermute | solution.py:306
  3.2 4.4 %collective-permute-start.9 = (bf16[96,3200]{1,0:T(8,128)(2,1)S(1)}, bf16[96,3200]{1,0:T(8,128)(2,1)S(1)}, u32[]{:S(2)}, u32[]{:S(2)}) collective-permute-start(bf16[96,3200]{1,0:T(8,128)(2,1)S(1)} %branch_0_fun.5.refs_0_), channel_id=1, source_target_pairs={{16,17},{17,16},{18,19},{19,18},{24,25},{25,24},{26,27},{27,26}} | collective-permute-start | bytes 1843208 | tf_op jit(solution)/shard_map/cond/branch_0_fun/ppermute | solution.py:306
  4.8 3.5 %collective-permute-start.14 = (bf16[48,1536]{1,0:T(8,128)(2,1)S(1)}, bf16[48,1536]{1,0:T(8,128)(2,1)S(1)}, u32[]{:S(2)}, u32[]{:S(2)}) collective-permute-start(bf16[48,1536]{1,0:T(8,128)(2,1)S(1)} %pad_maximum_fusion.refs_0_), channel_id=1, source_target_pairs={{17,16},{16,17},{19,18},{18,19}} | collective-permute-start | bytes 442376 | tf_op jit(solution)/shard_map/cond/branch_0_fun/ppermute | solution.py:306
  5.5 4.8 %collective-permute-start.15 = (bf16[48,1536]{1,0:T(8,128)(2,1)S(1)}, bf16[48,1536]{1,0:T(8,128)(2,1)S(1)}, u32[]{:S(2)}, u32[]{:S(2)}) collective-permute-start(bf16[48,1536]{1,0:T(8,128)(2,1)S(1)} %pad_maximum_fusion.refs_0_), channel_id=1, source_target_pairs={{18,16},{19,17},{20,18},{21,19}} | collective-permute-start | bytes 442376 | tf_op jit(solution)/shard_map/cond/branch_0_fun/ppermute | solution.py:306
  6.1 5.6 %collective-permute-start.16 = (bf16[48,1536]{1,0:T(8,128)(2,1)S(1)}, bf16[48,1536]{1,0:T(8,128)(2,1)S(1)}, u32[]{:S(2)}, u32[]{:S(2)}) collective-permute-start(bf16[48,1536]{1,0:T(8,128)(2,1)S(1)} %pad_maximum_fusion.refs_0_), channel_id=1, source_target_pairs={{19,16},{18,17},{21,18},{20,19}} | collective-permute-start | bytes 442376 | tf_op jit(solution)/shard_map/cond/branch_0_fun/ppermute | solution.py:306
  6.8 6.5 %collective-permute-start.17 = (bf16[48,1536]{1,0:T(8,128)(2,1)S(1)}, bf16[48,1536]{1,0:T(8,128)(2,1)S(1)}, u32[]{:S(2)}, u32[]{:S(2)}) collective-permute-start(bf16[48,1536]{1,0:T(8,128)(2,1)S(1)} %pad_maximum_fusion.refs_0_), channel_id=1, source_target_pairs={{20,16},{21,17},{22,18},{23,19}} | collective-permute-start | bytes 442376 | tf_op jit(solution)/shard_map/cond/branch_0_fun/ppermute | solution.py:306
  7.5 5.8 %collective-permute-start.18 = (bf16[48,1536]{1,0:T(8,128)(2,1)S(1)}, bf16[48,1536]{1,0:T(8,128)(2,1)S(1)}, u32[]{:S(2)}, u32[]{:S(2)}) collective-permute-start(bf16[48,1536]{1,0:T(8,128)(2,1)S(1)} %pad_maximum_fusion.refs_0_), channel_id=1, source_target_pairs={{21,16},{20,17},{23,18},{22,19}} | collective-permute-start | bytes 442376 | tf_op jit(solution)/shard_map/cond/branch_0_fun/ppermute | solution.py:306
  8.3 6.6 %collective-permute-start.11 = (bf16[192,5184]{1,0:T(8,128)(2,1)}, bf16[192,5184]{1,0:T(8,128)(2,1)}, u32[]{:S(2)}, u32[]{:S(2)}) collective-permute-start(bf16[192,5184]{1,0:T(8,128)(2,1)} %get-tuple-element.90), channel_id=1, source_target_pairs={{16,24},{17,25},{18,26},{19,27}} | collective-permute-start | bytes 5971976 | tf_op jit(solution)/shard_map/cond/branch_0_fun/ppermute | solution.py:306
  10.2 4.6 %collective-permute-start.12 = (bf16[96,3456]{1,0:T(8,128)(2,1)}, bf16[96,3456]{1,0:T(8,128)(2,1)}, u32[]{:S(2)}, u32[]{:S(2)}) collective-permute-start(bf16[96,3456]{1,0:T(8,128)(2,1)} %get-tuple-element.91), channel_id=1, source_target_pairs={{24,16},{25,17},{26,18},{27,19}} | collective-permute-start | bytes 1990664 | tf_op jit(solution)/shard_map/cond/branch_0_fun/ppermute | solution.py:306
  11.8 3.0 %copy-start.8 = (bf16[192,2592]{1,0:T(8,128)(2,1)S(1)}, bf16[192,2592]{1,0:T(8,128)(2,1)}, u32[]{:S(2)}) copy-start(bf16[192,2592]{1,0:T(8,128)(2,1)} %get-tuple-element.23.refs_0_.k_any) | copy-start | bytes 2985988 | tf_op jit(solution)/shard_map/cond
  11.8 3.1 %collective-permute-start.13 = (bf16[192,1152]{1,0:T(8,128)(2,1)}, bf16[192,1152]{1,0:T(8,128)(2,1)}, u32[]{:S(2)}, u32[]{:S(2)}) collective-permute-start(bf16[192,1152]{1,0:T(8,128)(2,1)} %get-tuple-element.92), channel_id=1, source_target_pairs={{16,24},{17,25},{18,26},{19,27},{24,16},{25,17},{26,18},{27,19}} | collective-permute-start | bytes 1327112 | tf_op jit(solution)/shard_map/cond/branch_0_fun/ppermute | solution.py:306
  13.4 1.4 %collective-permute-start.19 = (bf16[640,192]{1,0:T(8,128)(2,1)}, bf16[640,192]{1,0:T(8,128)(2,1)}, u32[]{:S(2)}, u32[]{:S(2)}) collective-permute-start(bf16[640,192]{1,0:T(8,128)(2,1)} %get-tuple-element.96), channel_id=1, source_target_pairs={{16,24},{17,25},{18,26},{19,27}} | collective-permute-start | bytes 737288 | tf_op jit(solution)/shard_map/cond/branch_0_fun/ppermute | solution.py:306
  15.1 2.7 %collective-permute-start.20 = (bf16[320,384]{1,0:T(8,128)(2,1)}, bf16[320,384]{1,0:T(8,128)(2,1)S(1)}, u32[]{:S(2)}, u32[]{:S(2)}) collective-permute-start(bf16[320,384]{1,0:T(8,128)(2,1)} %get-tuple-element.65), channel_id=1, source_target_pairs={{8,16},{9,17},{10,18},{11,19}} | collective-permute-start | bytes 737288 | tf_op jit(solution)/shard_map/ppermute | solution.py:306
  15.8 2.1 %collective-permute-start.21 = (bf16[320,384]{1,0:T(8,128)(2,1)}, bf16[320,384]{1,0:T(8,128)(2,1)S(1)}, u32[]{:S(2)}, u32[]{:S(2)}) collective-permute-start(bf16[320,384]{1,0:T(8,128)(2,1)} %get-tuple-element.65), channel_id=1, source_target_pairs={{8,24},{9,25},{10,26},{11,27}} | collective-permute-start | bytes 737288 | tf_op jit(solution)/shard_map/ppermute | solution.py:306
  16.5 1.4 %collective-permute-start.22 = (bf16[320,384]{1,0:T(8,128)(2,1)}, bf16[320,384]{1,0:T(8,128)(2,1)S(1)}, u32[]{:S(2)}, u32[]{:S(2)}) collective-permute-start(bf16[320,384]{1,0:T(8,128)(2,1)} %get-tuple-element.65), channel_id=1, source_target_pairs={{8,17},{9,16},{10,19},{11,18}} | collective-permute-start | bytes 737288 | tf_op jit(solution)/shard_map/ppermute | solution.py:306
  17.1 0.7 collective-permute-start.23
  18.3 3.4 %collective-permute-start.24 = (bf16[32,3072]{1,0:T(8,128)(2,1)S(1)}, bf16[32,3072]{1,0:T(8,128)(2,1)S(1)}, u32[]{:S(2)}, u32[]{:S(2)}) collective-permute-start(bf16[32,3072]{1,0:T(8,128)(2,1)S(1)} %get-tuple-element.75), channel_id=1, source_target_pairs={{16,0},{17,8},{18,4},{19,12},{24,16},{25,24},{26,20},{27,28}} | collective-permute-start | bytes 589832 | tf_op jit(solution)/shard_map/ppermute | solution.py:306
  19.0 2.7 %collective-permute-start.25 = (bf16[32,3072]{1,0:T(8,128)(2,1)S(1)}, bf16[32,3072]{1,0:T(8,128)(2,1)S(1)}, u32[]{:S(2)}, u32[]{:S(2)}) collective-permute-start(bf16[32,3072]{1,0:T(8,128)(2,1)S(1)} %get-tuple-element.76), channel_id=1, source_target_pairs={{16,1},{17,9},{18,5},{19,13},{24,17},{25,25},{26,21},{27,29}} | collective-permute-start | bytes 589832 | tf_op jit(solution)/shard_map/ppermute | solution.py:306
  19.6 2.0 %collective-permute-start.26 = (bf16[32,3072]{1,0:T(8,128)(2,1)S(1)}, bf16[32,3072]{1,0:T(8,128)(2,1)S(1)}, u32[]{:S(2)}, u32[]{:S(2)}) collective-permute-start(bf16[32,3072]{1,0:T(8,128)(2,1)S(1)} %get-tuple-element.77), channel_id=1, source_target_pairs={{16,2},{17,10},{18,6},{19,14},{24,18},{25,26},{26,22},{27,30}} | collective-permute-start | bytes 589832 | tf_op jit(solution)/shard_map/ppermute | solution.py:306
  20.3 89.8 %collective-permute-start.27 = (bf16[32,3072]{1,0:T(8,128)(2,1)S(1)}, bf16[32,3072]{1,0:T(8,128)(2,1)S(1)}, u32[]{:S(2)}, u32[]{:S(2)}) collective-permute-start(bf16[32,3072]{1,0:T(8,128)(2,1)S(1)} %get-tuple-element.78), channel_id=1, source_target_pairs={{16,3},{17,11},{18,7},{19,15},{24,19},{25,27},{26,23},{27,31}} | collective-permute-start | bytes 589832 | tf_op jit(solution)/shard_map/ppermute | solution.py:306

commit v4 on v3

--- a/solution.py
+++ b/solution.py
@@ -915,15 +915,16 @@
         for dx, moved in enumerate(shifts(base[...], 16, 16)):
             xx[:, dx * 192 : (dx + 1) * 192] = moved.astype(bf16)
         coming[3].wait()
-        total = None
-        for group in range(9):
-            start = group // 3 * 320 + group % 3 * 16
-            term = dot_t(xx[start : start + 928, :], k2[:, group * 576 : (group + 1) * 576])
-            total = term if total is None else total + term
-        inverse = lax.rsqrt(jnp.sum(total * total, axis=1, keepdims=True) / 192.0 + EPSILON)
-        keep = index_of((928, 192)) % 320 < 288
-        hs[0:928] = jnp.where(keep, silu(total * inverse), 0.0).astype(bf16)
-        hs[928:960] = jnp.zeros((32, 192), bf16)
+        for moment in range(3):
+            total = None
+            for group in range(9):
+                start = (group // 3 + moment) * 320 + group % 3 * 16
+                term = dot_t(xx[start : start + 288, :], k2[:, group * 576 : (group + 1) * 576])
+                total = term if total is None else total + term
+            inverse = lax.rsqrt(jnp.sum(total * total, axis=1, keepdims=True) / 192.0 + EPSILON)
+            at = moment * 320
+            hs[at : at + 288] = silu(total * inverse).astype(bf16)
+            hs[moment * 320 + 288 : moment * 320 + 320] = jnp.zeros((32, 192), bf16)
         coming[4].wait()
         p[...] = dot(hs[...], u2[...])
         upsample(p, t, 16, 16, 128)
@@ -1092,7 +1093,7 @@
         s < 2, sections01, before_sections23, latent, cache_a, cache_b, cache_c, cache_d, k, u
     )
     received = [
-        send(out1, [((1, h_, w_), (s_, h_, w_ ^ dw)) for h_ in range(2) for w_ in range(2)])
+        send(out1, [((1, h_, w_), (s_, h_, w_ ^ dw)) for h_ in range(2) for w_ in range(s_ - 1)])
         for dw in range(2)
         for s_ in (2, 3)
     ]

time: 112 us -> 106 us (0.946)
  waiting for transfers between devices: 88.5 us -> 83.2 us
    ppermute x20, waiting for transfers between devices: 88.5 us -> 83.2 us  [send(): return lax.ppermute(value, AXES, [(place(*a), place(*b)) for a, b in pairs])]
where the time goes in v4:
time: 106 us; the launch traced here: 105 us
  waiting for transfers between devices  83.2 us (78%)
  starting transfers between devices  17.9 us (17%)
  Pallas kernels  1.95 us (2%)
  other arithmetic  1.62 us (2%)
    ppermute x20, waiting for transfers between devices, send(): return lax.ppermute(value, AXES, [(place(*a), place(*b)) for a, b in pairs])  83.2 us
    ppermute x20, starting transfers between devices, send(): return lax.ppermute(value, AXES, [(place(*a), place(*b)) for a, b in pairs])  17.9 us
  transfers between devices with their start and end apart: 20, of which 1 were waited for; matrix products, arithmetic and copies ran while one was open for 1% of the time, Pallas kernels for 0%

profile of v4, /device:TPU:31, one launch (start us, length us, event | category | flops | bytes accessed | tf_op | source)
XLA Modules:
  0.0 105.3 jit_solution(9499529280529858757)
XLA Ops:
  0.0 15.1 %conditional.1 = (bf16[320,384]{1,0:T(8,128)(2,1)}, bf16[192,5184]{1,0:T(8,128)(2,1)}, bf16[96,3456]{1,0:T(8,128)(2,1)}, bf16[192,1152]{1,0:T(8,128)(2,1)}, bf16...) conditional(s32[]{:T(128)} %convert_element_type.3, ...), branch_computations={%region_0.0_spmd, %region_1.0_spmd} | conditional | flops 60003295232 | bytes 34094628 | solution.py:1092
  0.0 1.7 %branch_0_fun.5.refs_0_ = bf16[96,3200]{1,0:T(8,128)(2,1)S(1)} custom-call(bf16[192,2592]{1,0:T(8,128)(2,1)} %get-tuple-element.23.refs_0_.k_any, bf16[192,432]{1,0:T(8,128)(2,1)} %get-tuple-element.24.u_any), custom_call_target="tpu_custom_call" | custom-call | flops 1000000 | bytes 1000 | tf_op jit(solution)/shard_map/cond/branch_0_fun/pallas_call | solution.py:316
  1.7 0.7 collective-permute-start.10
  2.5 0.7 collective-permute-start.8
  3.2 0.7 collective-permute-start.9
  3.9 0.9 pad_maximum_fusion.refs_0_
  4.8 0.7 collective-permute-start.14
  5.5 0.7 collective-permute-start.15
  6.1 0.0 collective-permute-done.10.refs_3_
  6.1 0.7 collective-permute-start.16
  6.8 0.0 collective-permute-done.8.refs_1_
  6.8 0.7 collective-permute-start.17
  7.5 0.0 collective-permute-done.9.refs_2_
  7.5 0.7 collective-permute-start.18
  8.2 0.1 branch_0_fun.6
  8.3 0.0 collective-permute-done.14.refs_1_
  8.3 2.0 %collective-permute-start.11 = (bf16[192,5184]{1,0:T(8,128)(2,1)}, bf16[192,5184]{1,0:T(8,128)(2,1)}, u32[]{:S(2)}, u32[]{:S(2)}) collective-permute-start(bf16[192,5184]{1,0:T(8,128)(2,1)} %get-tuple-element.90), channel_id=1, source_target_pairs={{16,24},{17,25},{18,26},{19,27}} | collective-permute-start | bytes 5971976 | tf_op jit(solution)/shard_map/cond/branch_0_fun/ppermute | solution.py:306
  10.2 0.0 collective-permute-done.15.refs_2_
  10.2 1.5 %collective-permute-start.12 = (bf16[96,3456]{1,0:T(8,128)(2,1)}, bf16[96,3456]{1,0:T(8,128)(2,1)}, u32[]{:S(2)}, u32[]{:S(2)}) collective-permute-start(bf16[96,3456]{1,0:T(8,128)(2,1)} %get-tuple-element.91), channel_id=1, source_target_pairs={{24,16},{25,17},{26,18},{27,19}} | collective-permute-start | bytes 1990664 | tf_op jit(solution)/shard_map/cond/branch_0_fun/ppermute | solution.py:306
  11.8 0.0 collective-permute-done.16.refs_3_
  11.8 1.6 %collective-permute-start.13 = (bf16[192,1152]{1,0:T(8,128)(2,1)}, bf16[192,1152]{1,0:T(8,128)(2,1)}, u32[]{:S(2)}, u32[]{:S(2)}) collective-permute-start(bf16[192,1152]{1,0:T(8,128)(2,1)} %get-tuple-element.92), channel_id=1, source_target_pairs={{16,24},{17,25},{18,26},{19,27},{24,16},{25,17},{26,18},{27,19}} | collective-permute-start | bytes 1327112 | tf_op jit(solution)/shard_map/cond/branch_0_fun/ppermute | solution.py:306
  13.3 0.0 collective-permute-done.17.refs_4_
  13.3 0.0 collective-permute-done.18.refs_5_
  13.3 0.1 branch_0_fun.7
  13.4 1.4 %collective-permute-start.19 = (bf16[640,192]{1,0:T(8,128)(2,1)}, bf16[640,192]{1,0:T(8,128)(2,1)}, u32[]{:S(2)}, u32[]{:S(2)}) collective-permute-start(bf16[640,192]{1,0:T(8,128)(2,1)} %get-tuple-element.96), channel_id=1, source_target_pairs={{16,24},{17,25},{18,26},{19,27}} | collective-permute-start | bytes 737288 | tf_op jit(solution)/shard_map/cond/branch_0_fun/ppermute | solution.py:306
  14.8 0.0 copy-done.8
  14.8 0.0 collective-permute-done.19
  14.8 0.0 collective-permute-done.13
  14.8 0.0 collective-permute-done.12
  14.9 0.0 collective-permute-done.11
  15.1 0.7 collective-permute-start.20
  15.8 0.7 collective-permute-start.21
  16.5 0.7 collective-permute-start.22
  17.1 0.7 collective-permute-start.23
  17.8 0.0 collective-permute-done.20.same2
  17.8 0.0 collective-permute-done.21.same3
  17.9 0.0 collective-permute-done.22.other2
  17.9 0.0 collective-permute-done.23.other3
  17.9 0.1 shard_map.78
  18.0 0.7 collective-permute-start.24
  18.7 0.7 collective-permute-start.25
  19.3 0.7 collective-permute-start.26
  20.0 1.3 %collective-permute-start.27 = (bf16[32,3072]{1,0:T(8,128)(2,1)S(1)}, bf16[32,3072]{1,0:T(8,128)(2,1)S(1)}, u32[]{:S(2)}, u32[]{:S(2)}) collective-permute-start(bf16[32,3072]{1,0:T(8,128)(2,1)S(1)} %get-tuple-element.78), channel_id=1, source_target_pairs={{16,3},{17,11},{18,7},{19,15},{24,19},{25,27},{26,23},{27,31}} | collective-permute-start | bytes 589832 | tf_op jit(solution)/shard_map/ppermute | solution.py:306
  21.3 0.0 collective-permute-done.24
  21.3 0.0 collective-permute-done.25
  21.4 0.0 collective-permute-done.26
  21.4 83.2 %collective-permute-done.27 = bf16[32,3072]{1,0:T(8,128)(2,1)S(1)} collective-permute-done((bf16[32,3072]{1,0:T(8,128)(2,1)S(1)}, bf16[32,3072]{1,0:T(8,128)(2,1)S(1)}, u32[]{:S(2)}, u32[]{:S(2)}) %collective-permute-start.27) | collective-permute-done | bytes 196640 | tf_op jit(solution)/shard_map/ppermute | solution.py:306
  104.5 0.7 select_bitcast_fusion
  (2 shorter events, 0.0 us)
Async XLA Ops:
  1.7 4.4 %collective-permute-start.10 = (bf16[96,3200]{1,0:T(8,128)(2,1)S(1)}, bf16[96,3200]{1,0:T(8,128)(2,1)S(1)}, u32[]{:S(2)}, u32[]{:S(2)}) collective-permute-start(bf16[96,3200]{1,0:T(8,128)(2,1)S(1)} %branch_0_fun.5.refs_0_), channel_id=1, source_target_pairs={{16,19},{17,18},{18,17},{19,16},{24,27},{25,26},{26,25},{27,24}} | collective-permute-start | bytes 1843208 | tf_op jit(solution)/shard_map/cond/branch_0_fun/ppermute | solution.py:306
  2.5 4.4 %collective-permute-start.8 = (bf16[96,3200]{1,0:T(8,128)(2,1)S(1)}, bf16[96,3200]{1,0:T(8,128)(2,1)S(1)}, u32[]{:S(2)}, u32[]{:S(2)}) collective-permute-start(bf16[96,3200]{1,0:T(8,128)(2,1)S(1)} %branch_0_fun.5.refs_0_), channel_id=1, source_target_pairs={{16,18},{17,19},{18,16},{19,17},{24,26},{25,27},{26,24},{27,25}} | collective-permute-start | bytes 1843208 | tf_op jit(solution)/shard_map/cond/branch_0_fun/ppermute | solution.py:306
  3.2 4.4 %collective-permute-start.9 = (bf16[96,3200]{1,0:T(8,128)(2,1)S(1)}, bf16[96,3200]{1,0:T(8,128)(2,1)S(1)}, u32[]{:S(2)}, u32[]{:S(2)}) collective-permute-start(bf16[96,3200]{1,0:T(8,128)(2,1)S(1)} %branch_0_fun.5.refs_0_), channel_id=1, source_target_pairs={{16,17},{17,16},{18,19},{19,18},{24,25},{25,24},{26,27},{27,26}} | collective-permute-start | bytes 1843208 | tf_op jit(solution)/shard_map/cond/branch_0_fun/ppermute | solution.py:306
  4.8 3.5 %collective-permute-start.14 = (bf16[48,1536]{1,0:T(8,128)(2,1)S(1)}, bf16[48,1536]{1,0:T(8,128)(2,1)S(1)}, u32[]{:S(2)}, u32[]{:S(2)}) collective-permute-start(bf16[48,1536]{1,0:T(8,128)(2,1)S(1)} %pad_maximum_fusion.refs_0_), channel_id=1, source_target_pairs={{17,16},{16,17},{19,18},{18,19}} | collective-permute-start | bytes 442376 | tf_op jit(solution)/shard_map/cond/branch_0_fun/ppermute | solution.py:306
  5.5 4.8 %collective-permute-start.15 = (bf16[48,1536]{1,0:T(8,128)(2,1)S(1)}, bf16[48,1536]{1,0:T(8,128)(2,1)S(1)}, u32[]{:S(2)}, u32[]{:S(2)}) collective-permute-start(bf16[48,1536]{1,0:T(8,128)(2,1)S(1)} %pad_maximum_fusion.refs_0_), channel_id=1, source_target_pairs={{18,16},{19,17},{20,18},{21,19}} | collective-permute-start | bytes 442376 | tf_op jit(solution)/shard_map/cond/branch_0_fun/ppermute | solution.py:306
  6.1 5.6 %collective-permute-start.16 = (bf16[48,1536]{1,0:T(8,128)(2,1)S(1)}, bf16[48,1536]{1,0:T(8,128)(2,1)S(1)}, u32[]{:S(2)}, u32[]{:S(2)}) collective-permute-start(bf16[48,1536]{1,0:T(8,128)(2,1)S(1)} %pad_maximum_fusion.refs_0_), channel_id=1, source_target_pairs={{19,16},{18,17},{21,18},{20,19}} | collective-permute-start | bytes 442376 | tf_op jit(solution)/shard_map/cond/branch_0_fun/ppermute | solution.py:306
  6.8 6.5 %collective-permute-start.17 = (bf16[48,1536]{1,0:T(8,128)(2,1)S(1)}, bf16[48,1536]{1,0:T(8,128)(2,1)S(1)}, u32[]{:S(2)}, u32[]{:S(2)}) collective-permute-start(bf16[48,1536]{1,0:T(8,128)(2,1)S(1)} %pad_maximum_fusion.refs_0_), channel_id=1, source_target_pairs={{20,16},{21,17},{22,18},{23,19}} | collective-permute-start | bytes 442376 | tf_op jit(solution)/shard_map/cond/branch_0_fun/ppermute | solution.py:306
  7.5 5.8 %collective-permute-start.18 = (bf16[48,1536]{1,0:T(8,128)(2,1)S(1)}, bf16[48,1536]{1,0:T(8,128)(2,1)S(1)}, u32[]{:S(2)}, u32[]{:S(2)}) collective-permute-start(bf16[48,1536]{1,0:T(8,128)(2,1)S(1)} %pad_maximum_fusion.refs_0_), channel_id=1, source_target_pairs={{21,16},{20,17},{23,18},{22,19}} | collective-permute-start | bytes 442376 | tf_op jit(solution)/shard_map/cond/branch_0_fun/ppermute | solution.py:306
  8.3 6.6 %collective-permute-start.11 = (bf16[192,5184]{1,0:T(8,128)(2,1)}, bf16[192,5184]{1,0:T(8,128)(2,1)}, u32[]{:S(2)}, u32[]{:S(2)}) collective-permute-start(bf16[192,5184]{1,0:T(8,128)(2,1)} %get-tuple-element.90), channel_id=1, source_target_pairs={{16,24},{17,25},{18,26},{19,27}} | collective-permute-start | bytes 5971976 | tf_op jit(solution)/shard_map/cond/branch_0_fun/ppermute | solution.py:306
  10.2 4.6 %collective-permute-start.12 = (bf16[96,3456]{1,0:T(8,128)(2,1)}, bf16[96,3456]{1,0:T(8,128)(2,1)}, u32[]{:S(2)}, u32[]{:S(2)}) collective-permute-start(bf16[96,3456]{1,0:T(8,128)(2,1)} %get-tuple-element.91), channel_id=1, source_target_pairs={{24,16},{25,17},{26,18},{27,19}} | collective-permute-start | bytes 1990664 | tf_op jit(solution)/shard_map/cond/branch_0_fun/ppermute | solution.py:306
  11.8 3.0 %copy-start.8 = (bf16[192,2592]{1,0:T(8,128)(2,1)S(1)}, bf16[192,2592]{1,0:T(8,128)(2,1)}, u32[]{:S(2)}) copy-start(bf16[192,2592]{1,0:T(8,128)(2,1)} %get-tuple-element.23.refs_0_.k_any) | copy-start | bytes 2985988 | tf_op jit(solution)/shard_map/cond
  11.8 3.1 %collective-permute-start.13 = (bf16[192,1152]{1,0:T(8,128)(2,1)}, bf16[192,1152]{1,0:T(8,128)(2,1)}, u32[]{:S(2)}, u32[]{:S(2)}) collective-permute-start(bf16[192,1152]{1,0:T(8,128)(2,1)} %get-tuple-element.92), channel_id=1, source_target_pairs={{16,24},{17,25},{18,26},{19,27},{24,16},{25,17},{26,18},{27,19}} | collective-permute-start | bytes 1327112 | tf_op jit(solution)/shard_map/cond/branch_0_fun/ppermute | solution.py:306
  13.4 1.4 %collective-permute-start.19 = (bf16[640,192]{1,0:T(8,128)(2,1)}, bf16[640,192]{1,0:T(8,128)(2,1)}, u32[]{:S(2)}, u32[]{:S(2)}) collective-permute-start(bf16[640,192]{1,0:T(8,128)(2,1)} %get-tuple-element.96), channel_id=1, source_target_pairs={{16,24},{17,25},{18,26},{19,27}} | collective-permute-start | bytes 737288 | tf_op jit(solution)/shard_map/cond/branch_0_fun/ppermute | solution.py:306
  15.1 2.7 %collective-permute-start.20 = (bf16[320,384]{1,0:T(8,128)(2,1)}, bf16[320,384]{1,0:T(8,128)(2,1)S(1)}, u32[]{:S(2)}, u32[]{:S(2)}) collective-permute-start(bf16[320,384]{1,0:T(8,128)(2,1)} %get-tuple-element.65), channel_id=1, source_target_pairs={{8,16},{10,18}} | collective-permute-start | bytes 737288 | tf_op jit(solution)/shard_map/ppermute | solution.py:306
  15.8 2.1 %collective-permute-start.21 = (bf16[320,384]{1,0:T(8,128)(2,1)}, bf16[320,384]{1,0:T(8,128)(2,1)S(1)}, u32[]{:S(2)}, u32[]{:S(2)}) collective-permute-start(bf16[320,384]{1,0:T(8,128)(2,1)} %get-tuple-element.65), channel_id=1, source_target_pairs={{8,24},{9,25},{10,26},{11,27}} | collective-permute-start | bytes 737288 | tf_op jit(solution)/shard_map/ppermute | solution.py:306
  16.5 1.4 %collective-permute-start.22 = (bf16[320,384]{1,0:T(8,128)(2,1)}, bf16[320,384]{1,0:T(8,128)(2,1)S(1)}, u32[]{:S(2)}, u32[]{:S(2)}) collective-permute-start(bf16[320,384]{1,0:T(8,128)(2,1)} %get-tuple-element.65), channel_id=1, source_target_pairs={{8,17},{10,19}} | collective-permute-start | bytes 737288 | tf_op jit(solution)/shard_map/ppermute | solution.py:306
  17.1 0.7 collective-permute-start.23
  18.0 3.4 %collective-permute-start.24 = (bf16[32,3072]{1,0:T(8,128)(2,1)S(1)}, bf16[32,3072]{1,0:T(8,128)(2,1)S(1)}, u32[]{:S(2)}, u32[]{:S(2)}) collective-permute-start(bf16[32,3072]{1,0:T(8,128)(2,1)S(1)} %get-tuple-element.75), channel_id=1, source_target_pairs={{16,0},{17,8},{18,4},{19,12},{24,16},{25,24},{26,20},{27,28}} | collective-permute-start | bytes 589832 | tf_op jit(solution)/shard_map/ppermute | solution.py:306
  18.7 2.7 %collective-permute-start.25 = (bf16[32,3072]{1,0:T(8,128)(2,1)S(1)}, bf16[32,3072]{1,0:T(8,128)(2,1)S(1)}, u32[]{:S(2)}, u32[]{:S(2)}) collective-permute-start(bf16[32,3072]{1,0:T(8,128)(2,1)S(1)} %get-tuple-element.76), channel_id=1, source_target_pairs={{16,1},{17,9},{18,5},{19,13},{24,17},{25,25},{26,21},{27,29}} | collective-permute-start | bytes 589832 | tf_op jit(solution)/shard_map/ppermute | solution.py:306
  19.3 2.0 %collective-permute-start.26 = (bf16[32,3072]{1,0:T(8,128)(2,1)S(1)}, bf16[32,3072]{1,0:T(8,128)(2,1)S(1)}, u32[]{:S(2)}, u32[]{:S(2)}) collective-permute-start(bf16[32,3072]{1,0:T(8,128)(2,1)S(1)} %get-tuple-element.77), channel_id=1, source_target_pairs={{16,2},{17,10},{18,6},{19,14},{24,18},{25,26},{26,22},{27,30}} | collective-permute-start | bytes 589832 | tf_op jit(solution)/shard_map/ppermute | solution.py:306
  20.0 84.5 %collective-permute-start.27 = (bf16[32,3072]{1,0:T(8,128)(2,1)S(1)}, bf16[32,3072]{1,0:T(8,128)(2,1)S(1)}, u32[]{:S(2)}, u32[]{:S(2)}) collective-permute-start(bf16[32,3072]{1,0:T(8,128)(2,1)S(1)} %get-tuple-element.78), channel_id=1, source_target_pairs={{16,3},{17,11},{18,7},{19,15},{24,19},{25,27},{26,23},{27,31}} | collective-permute-start | bytes 589832 | tf_op jit(solution)/shard_map/ppermute | solution.py:306

commit v5 on v4

--- a/solution.py
+++ b/solution.py
@@ -528,7 +528,7 @@
         [pltpu.VMEM((192, 1728), bf16), pltpu.VMEM((2, 192, 2304), bf16)],
         *pieces,
         copies=2,
-        vmem=8,
+        vmem=62,
         cost=20 * 10**6,
         place=pltpu.VMEM,
     )
@@ -599,6 +599,7 @@
         ],
         partials, *ups,
         copies=3,
+        vmem=62,
     )
 
 
@@ -712,7 +713,7 @@
         ],
         frames, gathered, *kernels, *ups,
         copies=8,
-        vmem=26,
+        vmem=62,
     )
 
 
@@ -1058,7 +1059,6 @@
     ups = beside(u, u_far)
     u_z, u_x, u_d = (send(ups, square((0, 1), dh, dw)) for dh, dw in ((1, 0), (0, 1), (1, 1)))
     partial_sums = conv0(gathered, k)
-    partial_sums, k_x, k_z = lax.optimization_barrier((partial_sums, k_x, k_z))
     k_d = send(k_z, square((1,), 0, 1))
     partials = lax.all_to_all(partial_sums, ("ha", "wa"), split_axis=0, concat_axis=0, tiled=True)
     taps = join((ups, u_z, u_x, u_d))

time: 106 us -> 103 us (0.972)
  waiting for transfers between devices: 83.2 us -> 80 us
    ppermute x20, waiting for transfers between devices: 83.2 us -> 80 us  [send(): return lax.ppermute(value, AXES, [(place(*a), place(*b)) for a, b in pairs])]
where the time goes in v5:
time: 103 us; the launch traced here: 102 us
  waiting for transfers between devices  80 us (78%)
  starting transfers between devices  18 us (17%)
  Pallas kernels  1.95 us (2%)
  other arithmetic  1.62 us (2%)
    ppermute x20, waiting for transfers between devices, send(): return lax.ppermute(value, AXES, [(place(*a), place(*b)) for a, b in pairs])  80 us
    ppermute x20, starting transfers between devices, send(): return lax.ppermute(value, AXES, [(place(*a), place(*b)) for a, b in pairs])  18 us
  transfers between devices with their start and end apart: 20, of which 1 were waited for; matrix products, arithmetic and copies ran while one was open for 1% of the time, Pallas kernels for 0%

profile of v5, /device:TPU:31, one launch (start us, length us, event | category | flops | bytes accessed | tf_op | source)
XLA Modules:
  0.0 102.1 jit_solution(11912260806746566168)
XLA Ops:
  0.0 15.1 %conditional.1 = (bf16[320,384]{1,0:T(8,128)(2,1)S(1)}, bf16[192,5184]{1,0:T(8,128)(2,1)}, bf16[96,3456]{1,0:T(8,128)(2,1)}, bf16[192,1152]{1,0:T(8,128)(2,1)}, ...) conditional(s32[]{:T(128)} %convert_element_type.3, ...), branch_computations={%region_0.0_spmd, %region_1.0_spmd} | conditional | flops 60003295232 | bytes 30801388 | solution.py:1092
  0.0 1.7 %branch_0_fun.5.refs_0_ = bf16[96,3200]{1,0:T(8,128)(2,1)S(1)} custom-call(bf16[192,2592]{1,0:T(8,128)(2,1)} %get-tuple-element.23.refs_0_.k_any, bf16[192,432]{1,0:T(8,128)(2,1)} %get-tuple-element.24.u_any), custom_call_target="tpu_custom_call" | custom-call | flops 1000000 | bytes 1000 | tf_op jit(solution)/shard_map/cond/branch_0_fun/pallas_call | solution.py:316
  1.7 0.7 collective-permute-start.10
  2.5 0.7 collective-permute-start.8
  3.2 0.7 collective-permute-start.9
  3.9 0.9 pad_maximum_fusion.refs_0_
  4.8 0.7 collective-permute-start.14
  5.5 0.7 collective-permute-start.15
  6.1 0.0 collective-permute-done.10.refs_3_
  6.1 0.7 collective-permute-start.16
  6.8 0.0 collective-permute-done.8.refs_1_
  6.8 0.7 collective-permute-start.17
  7.5 0.0 collective-permute-done.9.refs_2_
  7.5 0.7 collective-permute-start.18
  8.2 0.1 branch_0_fun.6
  8.3 0.0 collective-permute-done.14.refs_1_
  8.3 2.0 %collective-permute-start.11 = (bf16[192,5184]{1,0:T(8,128)(2,1)}, bf16[192,5184]{1,0:T(8,128)(2,1)}, u32[]{:S(2)}, u32[]{:S(2)}) collective-permute-start(bf16[192,5184]{1,0:T(8,128)(2,1)} %get-tuple-element.87), channel_id=1, source_target_pairs={{16,24},{17,25},{18,26},{19,27}} | collective-permute-start | bytes 5971976 | tf_op jit(solution)/shard_map/cond/branch_0_fun/ppermute | solution.py:306
  10.3 0.0 collective-permute-done.15.refs_2_
  10.3 1.5 %collective-permute-start.12 = (bf16[96,3456]{1,0:T(8,128)(2,1)}, bf16[96,3456]{1,0:T(8,128)(2,1)}, u32[]{:S(2)}, u32[]{:S(2)}) collective-permute-start(bf16[96,3456]{1,0:T(8,128)(2,1)} %get-tuple-element.88), channel_id=1, source_target_pairs={{24,16},{25,17},{26,18},{27,19}} | collective-permute-start | bytes 1990664 | tf_op jit(solution)/shard_map/cond/branch_0_fun/ppermute | solution.py:306
  11.8 0.0 collective-permute-done.16.refs_3_
  11.8 1.6 %collective-permute-start.13 = (bf16[192,1152]{1,0:T(8,128)(2,1)}, bf16[192,1152]{1,0:T(8,128)(2,1)}, u32[]{:S(2)}, u32[]{:S(2)}) collective-permute-start(bf16[192,1152]{1,0:T(8,128)(2,1)} %get-tuple-element.89), channel_id=1, source_target_pairs={{16,24},{17,25},{18,26},{19,27},{24,16},{25,17},{26,18},{27,19}} | collective-permute-start | bytes 1327112 | tf_op jit(solution)/shard_map/cond/branch_0_fun/ppermute | solution.py:306
  13.4 0.0 collective-permute-done.17.refs_4_
  13.4 0.0 collective-permute-done.18.refs_5_
  13.4 0.1 branch_0_fun.7
  13.4 1.4 %collective-permute-start.19 = (bf16[640,192]{1,0:T(8,128)(2,1)S(1)}, bf16[640,192]{1,0:T(8,128)(2,1)}, u32[]{:S(2)}, u32[]{:S(2)}) collective-permute-start(bf16[640,192]{1,0:T(8,128)(2,1)S(1)} %get-tuple-element.93), channel_id=1, source_target_pairs={{16,24},{17,25},{18,26},{19,27}} | collective-permute-start | bytes 737288 | tf_op jit(solution)/shard_map/cond/branch_0_fun/ppermute | solution.py:306
  14.8 0.0 copy-done.2
  14.9 0.0 collective-permute-done.19
  14.9 0.0 collective-permute-done.13
  14.9 0.0 collective-permute-done.12
  14.9 0.0 collective-permute-done.11
  15.1 0.7 collective-permute-start.20
  15.8 0.7 collective-permute-start.21
  16.5 0.7 collective-permute-start.22
  17.2 0.7 collective-permute-start.23
  17.9 0.0 collective-permute-done.20.same2
  17.9 0.0 collective-permute-done.21.same3
  17.9 0.0 collective-permute-done.22.other2
  17.9 0.0 collective-permute-done.23.other3
  17.9 0.1 shard_map.78
  18.0 0.7 collective-permute-start.24
  18.7 0.7 collective-permute-start.25
  19.4 0.7 collective-permute-start.26
  20.1 1.3 %collective-permute-start.27 = (bf16[32,3072]{1,0:T(8,128)(2,1)S(1)}, bf16[32,3072]{1,0:T(8,128)(2,1)S(1)}, u32[]{:S(2)}, u32[]{:S(2)}) collective-permute-start(bf16[32,3072]{1,0:T(8,128)(2,1)S(1)} %get-tuple-element.75), channel_id=1, source_target_pairs={{16,3},{17,11},{18,7},{19,15},{24,19},{25,27},{26,23},{27,31}} | collective-permute-start | bytes 589832 | tf_op jit(solution)/shard_map/ppermute | solution.py:306
  21.4 0.0 collective-permute-done.24
  21.4 0.0 collective-permute-done.25
  21.4 0.0 collective-permute-done.26
  21.4 80.0 %collective-permute-done.27 = bf16[32,3072]{1,0:T(8,128)(2,1)S(1)} collective-permute-done((bf16[32,3072]{1,0:T(8,128)(2,1)S(1)}, bf16[32,3072]{1,0:T(8,128)(2,1)S(1)}, u32[]{:S(2)}, u32[]{:S(2)}) %collective-permute-start.27) | collective-permute-done | bytes 196640 | tf_op jit(solution)/shard_map/ppermute | solution.py:306
  101.4 0.7 select_bitcast_fusion
  (2 shorter events, 0.0 us)
Async XLA Ops:
  1.7 4.4 %collective-permute-start.10 = (bf16[96,3200]{1,0:T(8,128)(2,1)S(1)}, bf16[96,3200]{1,0:T(8,128)(2,1)S(1)}, u32[]{:S(2)}, u32[]{:S(2)}) collective-permute-start(bf16[96,3200]{1,0:T(8,128)(2,1)S(1)} %branch_0_fun.5.refs_0_), channel_id=1, source_target_pairs={{16,19},{17,18},{18,17},{19,16},{24,27},{25,26},{26,25},{27,24}} | collective-permute-start | bytes 1843208 | tf_op jit(solution)/shard_map/cond/branch_0_fun/ppermute | solution.py:306
  2.5 4.4 %collective-permute-start.8 = (bf16[96,3200]{1,0:T(8,128)(2,1)S(1)}, bf16[96,3200]{1,0:T(8,128)(2,1)S(1)}, u32[]{:S(2)}, u32[]{:S(2)}) collective-permute-start(bf16[96,3200]{1,0:T(8,128)(2,1)S(1)} %branch_0_fun.5.refs_0_), channel_id=1, source_target_pairs={{16,18},{17,19},{18,16},{19,17},{24,26},{25,27},{26,24},{27,25}} | collective-permute-start | bytes 1843208 | tf_op jit(solution)/shard_map/cond/branch_0_fun/ppermute | solution.py:306
  3.2 4.4 %collective-permute-start.9 = (bf16[96,3200]{1,0:T(8,128)(2,1)S(1)}, bf16[96,3200]{1,0:T(8,128)(2,1)S(1)}, u32[]{:S(2)}, u32[]{:S(2)}) collective-permute-start(bf16[96,3200]{1,0:T(8,128)(2,1)S(1)} %branch_0_fun.5.refs_0_), channel_id=1, source_target_pairs={{16,17},{17,16},{18,19},{19,18},{24,25},{25,24},{26,27},{27,26}} | collective-permute-start | bytes 1843208 | tf_op jit(solution)/shard_map/cond/branch_0_fun/ppermute | solution.py:306
  4.8 3.5 %collective-permute-start.14 = (bf16[48,1536]{1,0:T(8,128)(2,1)S(1)}, bf16[48,1536]{1,0:T(8,128)(2,1)S(1)}, u32[]{:S(2)}, u32[]{:S(2)}) collective-permute-start(bf16[48,1536]{1,0:T(8,128)(2,1)S(1)} %pad_maximum_fusion.refs_0_), channel_id=1, source_target_pairs={{17,16},{16,17},{19,18},{18,19}} | collective-permute-start | bytes 442376 | tf_op jit(solution)/shard_map/cond/branch_0_fun/ppermute | solution.py:306
  5.5 4.8 %collective-permute-start.15 = (bf16[48,1536]{1,0:T(8,128)(2,1)S(1)}, bf16[48,1536]{1,0:T(8,128)(2,1)S(1)}, u32[]{:S(2)}, u32[]{:S(2)}) collective-permute-start(bf16[48,1536]{1,0:T(8,128)(2,1)S(1)} %pad_maximum_fusion.refs_0_), channel_id=1, source_target_pairs={{18,16},{19,17},{20,18},{21,19}} | collective-permute-start | bytes 442376 | tf_op jit(solution)/shard_map/cond/branch_0_fun/ppermute | solution.py:306
  6.1 5.7 %collective-permute-start.16 = (bf16[48,1536]{1,0:T(8,128)(2,1)S(1)}, bf16[48,1536]{1,0:T(8,128)(2,1)S(1)}, u32[]{:S(2)}, u32[]{:S(2)}) collective-permute-start(bf16[48,1536]{1,0:T(8,128)(2,1)S(1)} %pad_maximum_fusion.refs_0_), channel_id=1, source_target_pairs={{19,16},{18,17},{21,18},{20,19}} | collective-permute-start | bytes 442376 | tf_op jit(solution)/shard_map/cond/branch_0_fun/ppermute | solution.py:306
  6.8 6.5 %collective-permute-start.17 = (bf16[48,1536]{1,0:T(8,128)(2,1)S(1)}, bf16[48,1536]{1,0:T(8,128)(2,1)S(1)}, u32[]{:S(2)}, u32[]{:S(2)}) collective-permute-start(bf16[48,1536]{1,0:T(8,128)(2,1)S(1)} %pad_maximum_fusion.refs_0_), channel_id=1, source_target_pairs={{20,16},{21,17},{22,18},{23,19}} | collective-permute-start | bytes 442376 | tf_op jit(solution)/shard_map/cond/branch_0_fun/ppermute | solution.py:306
  7.5 5.8 %collective-permute-start.18 = (bf16[48,1536]{1,0:T(8,128)(2,1)S(1)}, bf16[48,1536]{1,0:T(8,128)(2,1)S(1)}, u32[]{:S(2)}, u32[]{:S(2)}) collective-permute-start(bf16[48,1536]{1,0:T(8,128)(2,1)S(1)} %pad_maximum_fusion.refs_0_), channel_id=1, source_target_pairs={{21,16},{20,17},{23,18},{22,19}} | collective-permute-start | bytes 442376 | tf_op jit(solution)/shard_map/cond/branch_0_fun/ppermute | solution.py:306
  8.3 6.6 %collective-permute-start.11 = (bf16[192,5184]{1,0:T(8,128)(2,1)}, bf16[192,5184]{1,0:T(8,128)(2,1)}, u32[]{:S(2)}, u32[]{:S(2)}) collective-permute-start(bf16[192,5184]{1,0:T(8,128)(2,1)} %get-tuple-element.87), channel_id=1, source_target_pairs={{16,24},{17,25},{18,26},{19,27}} | collective-permute-start | bytes 5971976 | tf_op jit(solution)/shard_map/cond/branch_0_fun/ppermute | solution.py:306
  10.3 4.6 %collective-permute-start.12 = (bf16[96,3456]{1,0:T(8,128)(2,1)}, bf16[96,3456]{1,0:T(8,128)(2,1)}, u32[]{:S(2)}, u32[]{:S(2)}) collective-permute-start(bf16[96,3456]{1,0:T(8,128)(2,1)} %get-tuple-element.88), channel_id=1, source_target_pairs={{24,16},{25,17},{26,18},{27,19}} | collective-permute-start | bytes 1990664 | tf_op jit(solution)/shard_map/cond/branch_0_fun/ppermute | solution.py:306
  11.8 3.0 %copy-start.2 = (bf16[192,2592]{1,0:T(8,128)(2,1)S(1)}, bf16[192,2592]{1,0:T(8,128)(2,1)}, u32[]{:S(2)}) copy-start(bf16[192,2592]{1,0:T(8,128)(2,1)} %get-tuple-element.23.refs_0_.k_any) | copy-start | bytes 2985988 | tf_op jit(solution)/shard_map/cond
  11.8 3.1 %collective-permute-start.13 = (bf16[192,1152]{1,0:T(8,128)(2,1)}, bf16[192,1152]{1,0:T(8,128)(2,1)}, u32[]{:S(2)}, u32[]{:S(2)}) collective-permute-start(bf16[192,1152]{1,0:T(8,128)(2,1)} %get-tuple-element.89), channel_id=1, source_target_pairs={{16,24},{17,25},{18,26},{19,27},{24,16},{25,17},{26,18},{27,19}} | collective-permute-start | bytes 1327112 | tf_op jit(solution)/shard_map/cond/branch_0_fun/ppermute | solution.py:306
  13.4 1.4 %collective-permute-start.19 = (bf16[640,192]{1,0:T(8,128)(2,1)S(1)}, bf16[640,192]{1,0:T(8,128)(2,1)}, u32[]{:S(2)}, u32[]{:S(2)}) collective-permute-start(bf16[640,192]{1,0:T(8,128)(2,1)S(1)} %get-tuple-element.93), channel_id=1, source_target_pairs={{16,24},{17,25},{18,26},{19,27}} | collective-permute-start | bytes 737288 | tf_op jit(solution)/shard_map/cond/branch_0_fun/ppermute | solution.py:306
  15.1 2.7 %collective-permute-start.20 = (bf16[320,384]{1,0:T(8,128)(2,1)S(1)}, bf16[320,384]{1,0:T(8,128)(2,1)S(1)}, u32[]{:S(2)}, u32[]{:S(2)}) collective-permute-start(bf16[320,384]{1,0:T(8,128)(2,1)S(1)} %get-tuple-element.62), channel_id=1, source_target_pairs={{8,16},{10,18}} | collective-permute-start | bytes 737288 | tf_op jit(solution)/shard_map/ppermute | solution.py:306
  15.8 2.1 %collective-permute-start.21 = (bf16[320,384]{1,0:T(8,128)(2,1)S(1)}, bf16[320,384]{1,0:T(8,128)(2,1)S(1)}, u32[]{:S(2)}, u32[]{:S(2)}) collective-permute-start(bf16[320,384]{1,0:T(8,128)(2,1)S(1)} %get-tuple-element.62), channel_id=1, source_target_pairs={{8,24},{9,25},{10,26},{11,27}} | collective-permute-start | bytes 737288 | tf_op jit(solution)/shard_map/ppermute | solution.py:306
  16.5 1.4 %collective-permute-start.22 = (bf16[320,384]{1,0:T(8,128)(2,1)S(1)}, bf16[320,384]{1,0:T(8,128)(2,1)S(1)}, u32[]{:S(2)}, u32[]{:S(2)}) collective-permute-start(bf16[320,384]{1,0:T(8,128)(2,1)S(1)} %get-tuple-element.62), channel_id=1, source_target_pairs={{8,17},{10,19}} | collective-permute-start | bytes 737288 | tf_op jit(solution)/shard_map/ppermute | solution.py:306
  17.2 0.7 collective-permute-start.23
  18.0 3.4 %collective-permute-start.24 = (bf16[32,3072]{1,0:T(8,128)(2,1)S(1)}, bf16[32,3072]{1,0:T(8,128)(2,1)S(1)}, u32[]{:S(2)}, u32[]{:S(2)}) collective-permute-start(bf16[32,3072]{1,0:T(8,128)(2,1)S(1)} %get-tuple-element.72), channel_id=1, source_target_pairs={{16,0},{17,8},{18,4},{19,12},{24,16},{25,24},{26,20},{27,28}} | collective-permute-start | bytes 589832 | tf_op jit(solution)/shard_map/ppermute | solution.py:306
  18.7 2.7 %collective-permute-start.25 = (bf16[32,3072]{1,0:T(8,128)(2,1)S(1)}, bf16[32,3072]{1,0:T(8,128)(2,1)S(1)}, u32[]{:S(2)}, u32[]{:S(2)}) collective-permute-start(bf16[32,3072]{1,0:T(8,128)(2,1)S(1)} %get-tuple-element.73), channel_id=1, source_target_pairs={{16,1},{17,9},{18,5},{19,13},{24,17},{25,25},{26,21},{27,29}} | collective-permute-start | bytes 589832 | tf_op jit(solution)/shard_map/ppermute | solution.py:306
  19.4 2.0 %collective-permute-start.26 = (bf16[32,3072]{1,0:T(8,128)(2,1)S(1)}, bf16[32,3072]{1,0:T(8,128)(2,1)S(1)}, u32[]{:S(2)}, u32[]{:S(2)}) collective-permute-start(bf16[32,3072]{1,0:T(8,128)(2,1)S(1)} %get-tuple-element.74), channel_id=1, source_target_pairs={{16,2},{17,10},{18,6},{19,14},{24,18},{25,26},{26,22},{27,30}} | collective-permute-start | bytes 589832 | tf_op jit(solution)/shard_map/ppermute | solution.py:306
  20.1 81.3 %collective-permute-start.27 = (bf16[32,3072]{1,0:T(8,128)(2,1)S(1)}, bf16[32,3072]{1,0:T(8,128)(2,1)S(1)}, u32[]{:S(2)}, u32[]{:S(2)}) collective-permute-start(bf16[32,3072]{1,0:T(8,128)(2,1)S(1)} %get-tuple-element.75), channel_id=1, source_target_pairs={{16,3},{17,11},{18,7},{19,15},{24,19},{25,27},{26,23},{27,31}} | collective-permute-start | bytes 589832 | tf_op jit(solution)/shard_map/ppermute | solution.py:306

commit v6 on v5

--- a/solution.py
+++ b/solution.py
@@ -453,18 +453,19 @@
 
             @pl.when(h == part)
             def _():
-                total = None
-                at, end = part * 2592, part * 2592 + 2592
-                while at < end:
-                    tap, c0 = divmod(at, 384)
-                    c1 = min(384, c0 + end - at)
-                    dt, dy, dx = tap // 9, tap // 3 % 3, tap % 3
-                    start = dt * 160 + dy * 16
-                    k0 = at - part * 2592
-                    term = dot_t(xx[dx, start : start + 608, c0:c1], k_ref[:, k0 : k0 + c1 - c0])
-                    total = term if total is None else total + term
-                    at += c1 - c0
-                acc[...] = total
+                for pair in range(2):
+                    total = None
+                    at, end = part * 2592, part * 2592 + 2592
+                    while at < end:
+                        tap, c0 = divmod(at, 384)
+                        c1 = min(384, c0 + end - at)
+                        dt, dy, dx = tap // 9, tap // 3 % 3, tap % 3
+                        start = (dt + 2 * pair) * 160 + dy * 16
+                        k0 = at - part * 2592
+                        term = dot_t(xx[dx, start : start + 288, c0:c1], k_ref[:, k0 : k0 + c1 - c0])
+                        total = term if total is None else total + term
+                        at += c1 - c0
+                    acc[pair * 320 : pair * 320 + 288] = total
 
         for frame in range(4):
             for r in range(8):

time: 103 us -> 103 us (level)
  no operation moved by 1% of the time
where the time goes in v6:
time: 103 us; the launch traced here: 102 us
  waiting for transfers between devices  79.9 us (78%)
  starting transfers between devices  18 us (17%)
  Pallas kernels  1.95 us (2%)
  other arithmetic  1.62 us (2%)
    ppermute x20, waiting for transfers between devices, send(): return lax.ppermute(value, AXES, [(place(*a), place(*b)) for a, b in pairs])  79.9 us
    ppermute x20, starting transfers between devices, send(): return lax.ppermute(value, AXES, [(place(*a), place(*b)) for a, b in pairs])  18 us
  transfers between devices with their start and end apart: 20, of which 1 were waited for; matrix products, arithmetic and copies ran while one was open for 1% of the time, Pallas kernels for 0%

profile of v6, /device:TPU:31, one launch (start us, length us, event | category | flops | bytes accessed | tf_op | source)
XLA Modules:
  0.0 101.9 jit_solution(11058687167822385687)
XLA Ops:
  0.0 15.1 %conditional.1 = (bf16[320,384]{1,0:T(8,128)(2,1)S(1)}, bf16[192,5184]{1,0:T(8,128)(2,1)}, bf16[96,3456]{1,0:T(8,128)(2,1)}, bf16[192,1152]{1,0:T(8,128)(2,1)}, ...) conditional(s32[]{:T(128)} %convert_element_type.3, ...), branch_computations={%region_0.0_spmd, %region_1.0_spmd} | conditional | flops 60003295232 | bytes 30801388 | solution.py:1093
  0.0 1.7 %branch_0_fun.5.refs_0_ = bf16[96,3200]{1,0:T(8,128)(2,1)S(1)} custom-call(bf16[192,2592]{1,0:T(8,128)(2,1)} %get-tuple-element.23.refs_0_.k_any, bf16[192,432]{1,0:T(8,128)(2,1)} %get-tuple-element.24.u_any), custom_call_target="tpu_custom_call" | custom-call | flops 1000000 | bytes 1000 | tf_op jit(solution)/shard_map/cond/branch_0_fun/pallas_call | solution.py:316
  1.7 0.7 collective-permute-start.10
  2.5 0.7 collective-permute-start.8
  3.2 0.7 collective-permute-start.9
  3.9 0.9 pad_maximum_fusion.refs_0_
  4.8 0.7 collective-permute-start.14
  5.5 0.7 collective-permute-start.15
  6.1 0.0 collective-permute-done.10.refs_3_
  6.1 0.7 collective-permute-start.16
  6.8 0.0 collective-permute-done.8.refs_1_
  6.8 0.7 collective-permute-start.17
  7.5 0.0 collective-permute-done.9.refs_2_
  7.5 0.7 collective-permute-start.18
  8.2 0.1 branch_0_fun.6
  8.3 0.0 collective-permute-done.14.refs_1_
  8.3 2.0 %collective-permute-start.11 = (bf16[192,5184]{1,0:T(8,128)(2,1)}, bf16[192,5184]{1,0:T(8,128)(2,1)}, u32[]{:S(2)}, u32[]{:S(2)}) collective-permute-start(bf16[192,5184]{1,0:T(8,128)(2,1)} %get-tuple-element.87), channel_id=1, source_target_pairs={{16,24},{17,25},{18,26},{19,27}} | collective-permute-start | bytes 5971976 | tf_op jit(solution)/shard_map/cond/branch_0_fun/ppermute | solution.py:306
  10.3 0.0 collective-permute-done.15.refs_2_
  10.3 1.5 %collective-permute-start.12 = (bf16[96,3456]{1,0:T(8,128)(2,1)}, bf16[96,3456]{1,0:T(8,128)(2,1)}, u32[]{:S(2)}, u32[]{:S(2)}) collective-permute-start(bf16[96,3456]{1,0:T(8,128)(2,1)} %get-tuple-element.88), channel_id=1, source_target_pairs={{24,16},{25,17},{26,18},{27,19}} | collective-permute-start | bytes 1990664 | tf_op jit(solution)/shard_map/cond/branch_0_fun/ppermute | solution.py:306
  11.8 0.0 collective-permute-done.16.refs_3_
  11.8 1.6 %collective-permute-start.13 = (bf16[192,1152]{1,0:T(8,128)(2,1)}, bf16[192,1152]{1,0:T(8,128)(2,1)}, u32[]{:S(2)}, u32[]{:S(2)}) collective-permute-start(bf16[192,1152]{1,0:T(8,128)(2,1)} %get-tuple-element.89), channel_id=1, source_target_pairs={{16,24},{17,25},{18,26},{19,27},{24,16},{25,17},{26,18},{27,19}} | collective-permute-start | bytes 1327112 | tf_op jit(solution)/shard_map/cond/branch_0_fun/ppermute | solution.py:306
  13.4 0.0 collective-permute-done.17.refs_4_
  13.4 0.0 collective-permute-done.18.refs_5_
  13.4 0.1 branch_0_fun.7
  13.4 1.4 %collective-permute-start.19 = (bf16[640,192]{1,0:T(8,128)(2,1)S(1)}, bf16[640,192]{1,0:T(8,128)(2,1)}, u32[]{:S(2)}, u32[]{:S(2)}) collective-permute-start(bf16[640,192]{1,0:T(8,128)(2,1)S(1)} %get-tuple-element.93), channel_id=1, source_target_pairs={{16,24},{17,25},{18,26},{19,27}} | collective-permute-start | bytes 737288 | tf_op jit(solution)/shard_map/cond/branch_0_fun/ppermute | solution.py:306
  14.8 0.0 copy-done.2
  14.9 0.0 collective-permute-done.19
  14.9 0.0 collective-permute-done.13
  14.9 0.0 collective-permute-done.12
  14.9 0.0 collective-permute-done.11
  15.1 0.7 collective-permute-start.20
  15.8 0.7 collective-permute-start.21
  16.5 0.7 collective-permute-start.22
  17.2 0.7 collective-permute-start.23
  17.9 0.0 collective-permute-done.20.same2
  17.9 0.0 collective-permute-done.21.same3
  17.9 0.0 collective-permute-done.22.other2
  17.9 0.0 collective-permute-done.23.other3
  17.9 0.1 shard_map.78
  18.0 0.7 collective-permute-start.24
  18.7 0.7 collective-permute-start.25
  19.4 0.7 collective-permute-start.26
  20.1 1.3 %collective-permute-start.27 = (bf16[32,3072]{1,0:T(8,128)(2,1)S(1)}, bf16[32,3072]{1,0:T(8,128)(2,1)S(1)}, u32[]{:S(2)}, u32[]{:S(2)}) collective-permute-start(bf16[32,3072]{1,0:T(8,128)(2,1)S(1)} %get-tuple-element.75), channel_id=1, source_target_pairs={{16,3},{17,11},{18,7},{19,15},{24,19},{25,27},{26,23},{27,31}} | collective-permute-start | bytes 589832 | tf_op jit(solution)/shard_map/ppermute | solution.py:306
  21.4 0.0 collective-permute-done.24
  21.4 0.0 collective-permute-done.25
  21.4 0.0 collective-permute-done.26
  21.4 79.8 %collective-permute-done.27 = bf16[32,3072]{1,0:T(8,128)(2,1)S(1)} collective-permute-done((bf16[32,3072]{1,0:T(8,128)(2,1)S(1)}, bf16[32,3072]{1,0:T(8,128)(2,1)S(1)}, u32[]{:S(2)}, u32[]{:S(2)}) %collective-permute-start.27) | collective-permute-done | bytes 196640 | tf_op jit(solution)/shard_map/ppermute | solution.py:306
  101.2 0.7 select_bitcast_fusion
  (2 shorter events, 0.0 us)
Async XLA Ops:
  1.7 4.4 %collective-permute-start.10 = (bf16[96,3200]{1,0:T(8,128)(2,1)S(1)}, bf16[96,3200]{1,0:T(8,128)(2,1)S(1)}, u32[]{:S(2)}, u32[]{:S(2)}) collective-permute-start(bf16[96,3200]{1,0:T(8,128)(2,1)S(1)} %branch_0_fun.5.refs_0_), channel_id=1, source_target_pairs={{16,19},{17,18},{18,17},{19,16},{24,27},{25,26},{26,25},{27,24}} | collective-permute-start | bytes 1843208 | tf_op jit(solution)/shard_map/cond/branch_0_fun/ppermute | solution.py:306
  2.5 4.4 %collective-permute-start.8 = (bf16[96,3200]{1,0:T(8,128)(2,1)S(1)}, bf16[96,3200]{1,0:T(8,128)(2,1)S(1)}, u32[]{:S(2)}, u32[]{:S(2)}) collective-permute-start(bf16[96,3200]{1,0:T(8,128)(2,1)S(1)} %branch_0_fun.5.refs_0_), channel_id=1, source_target_pairs={{16,18},{17,19},{18,16},{19,17},{24,26},{25,27},{26,24},{27,25}} | collective-permute-start | bytes 1843208 | tf_op jit(solution)/shard_map/cond/branch_0_fun/ppermute | solution.py:306
  3.2 4.4 %collective-permute-start.9 = (bf16[96,3200]{1,0:T(8,128)(2,1)S(1)}, bf16[96,3200]{1,0:T(8,128)(2,1)S(1)}, u32[]{:S(2)}, u32[]{:S(2)}) collective-permute-start(bf16[96,3200]{1,0:T(8,128)(2,1)S(1)} %branch_0_fun.5.refs_0_), channel_id=1, source_target_pairs={{16,17},{17,16},{18,19},{19,18},{24,25},{25,24},{26,27},{27,26}} | collective-permute-start | bytes 1843208 | tf_op jit(solution)/shard_map/cond/branch_0_fun/ppermute | solution.py:306
  4.8 3.5 %collective-permute-start.14 = (bf16[48,1536]{1,0:T(8,128)(2,1)S(1)}, bf16[48,1536]{1,0:T(8,128)(2,1)S(1)}, u32[]{:S(2)}, u32[]{:S(2)}) collective-permute-start(bf16[48,1536]{1,0:T(8,128)(2,1)S(1)} %pad_maximum_fusion.refs_0_), channel_id=1, source_target_pairs={{17,16},{16,17},{19,18},{18,19}} | collective-permute-start | bytes 442376 | tf_op jit(solution)/shard_map/cond/branch_0_fun/ppermute | solution.py:306
  5.5 4.8 %collective-permute-start.15 = (bf16[48,1536]{1,0:T(8,128)(2,1)S(1)}, bf16[48,1536]{1,0:T(8,128)(2,1)S(1)}, u32[]{:S(2)}, u32[]{:S(2)}) collective-permute-start(bf16[48,1536]{1,0:T(8,128)(2,1)S(1)} %pad_maximum_fusion.refs_0_), channel_id=1, source_target_pairs={{18,16},{19,17},{20,18},{21,19}} | collective-permute-start | bytes 442376 | tf_op jit(solution)/shard_map/cond/branch_0_fun/ppermute | solution.py:306
  6.1 5.7 %collective-permute-start.16 = (bf16[48,1536]{1,0:T(8,128)(2,1)S(1)}, bf16[48,1536]{1,0:T(8,128)(2,1)S(1)}, u32[]{:S(2)}, u32[]{:S(2)}) collective-permute-start(bf16[48,1536]{1,0:T(8,128)(2,1)S(1)} %pad_maximum_fusion.refs_0_), channel_id=1, source_target_pairs={{19,16},{18,17},{21,18},{20,19}} | collective-permute-start | bytes 442376 | tf_op jit(solution)/shard_map/cond/branch_0_fun/ppermute | solution.py:306
  6.8 6.5 %collective-permute-start.17 = (bf16[48,1536]{1,0:T(8,128)(2,1)S(1)}, bf16[48,1536]{1,0:T(8,128)(2,1)S(1)}, u32[]{:S(2)}, u32[]{:S(2)}) collective-permute-start(bf16[48,1536]{1,0:T(8,128)(2,1)S(1)} %pad_maximum_fusion.refs_0_), channel_id=1, source_target_pairs={{20,16},{21,17},{22,18},{23,19}} | collective-permute-start | bytes 442376 | tf_op jit(solution)/shard_map/cond/branch_0_fun/ppermute | solution.py:306
  7.5 5.8 %collective-permute-start.18 = (bf16[48,1536]{1,0:T(8,128)(2,1)S(1)}, bf16[48,1536]{1,0:T(8,128)(2,1)S(1)}, u32[]{:S(2)}, u32[]{:S(2)}) collective-permute-start(bf16[48,1536]{1,0:T(8,128)(2,1)S(1)} %pad_maximum_fusion.refs_0_), channel_id=1, source_target_pairs={{21,16},{20,17},{23,18},{22,19}} | collective-permute-start | bytes 442376 | tf_op jit(solution)/shard_map/cond/branch_0_fun/ppermute | solution.py:306
  8.3 6.6 %collective-permute-start.11 = (bf16[192,5184]{1,0:T(8,128)(2,1)}, bf16[192,5184]{1,0:T(8,128)(2,1)}, u32[]{:S(2)}, u32[]{:S(2)}) collective-permute-start(bf16[192,5184]{1,0:T(8,128)(2,1)} %get-tuple-element.87), channel_id=1, source_target_pairs={{16,24},{17,25},{18,26},{19,27}} | collective-permute-start | bytes 5971976 | tf_op jit(solution)/shard_map/cond/branch_0_fun/ppermute | solution.py:306
  10.3 4.6 %collective-permute-start.12 = (bf16[96,3456]{1,0:T(8,128)(2,1)}, bf16[96,3456]{1,0:T(8,128)(2,1)}, u32[]{:S(2)}, u32[]{:S(2)}) collective-permute-start(bf16[96,3456]{1,0:T(8,128)(2,1)} %get-tuple-element.88), channel_id=1, source_target_pairs={{24,16},{25,17},{26,18},{27,19}} | collective-permute-start | bytes 1990664 | tf_op jit(solution)/shard_map/cond/branch_0_fun/ppermute | solution.py:306
  11.8 3.0 %copy-start.2 = (bf16[192,2592]{1,0:T(8,128)(2,1)S(1)}, bf16[192,2592]{1,0:T(8,128)(2,1)}, u32[]{:S(2)}) copy-start(bf16[192,2592]{1,0:T(8,128)(2,1)} %get-tuple-element.23.refs_0_.k_any) | copy-start | bytes 2985988 | tf_op jit(solution)/shard_map/cond
  11.8 3.1 %collective-permute-start.13 = (bf16[192,1152]{1,0:T(8,128)(2,1)}, bf16[192,1152]{1,0:T(8,128)(2,1)}, u32[]{:S(2)}, u32[]{:S(2)}) collective-permute-start(bf16[192,1152]{1,0:T(8,128)(2,1)} %get-tuple-element.89), channel_id=1, source_target_pairs={{16,24},{17,25},{18,26},{19,27},{24,16},{25,17},{26,18},{27,19}} | collective-permute-start | bytes 1327112 | tf_op jit(solution)/shard_map/cond/branch_0_fun/ppermute | solution.py:306
  13.4 1.4 %collective-permute-start.19 = (bf16[640,192]{1,0:T(8,128)(2,1)S(1)}, bf16[640,192]{1,0:T(8,128)(2,1)}, u32[]{:S(2)}, u32[]{:S(2)}) collective-permute-start(bf16[640,192]{1,0:T(8,128)(2,1)S(1)} %get-tuple-element.93), channel_id=1, source_target_pairs={{16,24},{17,25},{18,26},{19,27}} | collective-permute-start | bytes 737288 | tf_op jit(solution)/shard_map/cond/branch_0_fun/ppermute | solution.py:306
  15.1 2.7 %collective-permute-start.20 = (bf16[320,384]{1,0:T(8,128)(2,1)S(1)}, bf16[320,384]{1,0:T(8,128)(2,1)S(1)}, u32[]{:S(2)}, u32[]{:S(2)}) collective-permute-start(bf16[320,384]{1,0:T(8,128)(2,1)S(1)} %get-tuple-element.62), channel_id=1, source_target_pairs={{8,16},{10,18}} | collective-permute-start | bytes 737288 | tf_op jit(solution)/shard_map/ppermute | solution.py:306
  15.8 2.1 %collective-permute-start.21 = (bf16[320,384]{1,0:T(8,128)(2,1)S(1)}, bf16[320,384]{1,0:T(8,128)(2,1)S(1)}, u32[]{:S(2)}, u32[]{:S(2)}) collective-permute-start(bf16[320,384]{1,0:T(8,128)(2,1)S(1)} %get-tuple-element.62), channel_id=1, source_target_pairs={{8,24},{9,25},{10,26},{11,27}} | collective-permute-start | bytes 737288 | tf_op jit(solution)/shard_map/ppermute | solution.py:306
  16.5 1.4 %collective-permute-start.22 = (bf16[320,384]{1,0:T(8,128)(2,1)S(1)}, bf16[320,384]{1,0:T(8,128)(2,1)S(1)}, u32[]{:S(2)}, u32[]{:S(2)}) collective-permute-start(bf16[320,384]{1,0:T(8,128)(2,1)S(1)} %get-tuple-element.62), channel_id=1, source_target_pairs={{8,17},{10,19}} | collective-permute-start | bytes 737288 | tf_op jit(solution)/shard_map/ppermute | solution.py:306
  17.2 0.7 collective-permute-start.23
  18.0 3.4 %collective-permute-start.24 = (bf16[32,3072]{1,0:T(8,128)(2,1)S(1)}, bf16[32,3072]{1,0:T(8,128)(2,1)S(1)}, u32[]{:S(2)}, u32[]{:S(2)}) collective-permute-start(bf16[32,3072]{1,0:T(8,128)(2,1)S(1)} %get-tuple-element.72), channel_id=1, source_target_pairs={{16,0},{17,8},{18,4},{19,12},{24,16},{25,24},{26,20},{27,28}} | collective-permute-start | bytes 589832 | tf_op jit(solution)/shard_map/ppermute | solution.py:306
  18.7 2.7 %collective-permute-start.25 = (bf16[32,3072]{1,0:T(8,128)(2,1)S(1)}, bf16[32,3072]{1,0:T(8,128)(2,1)S(1)}, u32[]{:S(2)}, u32[]{:S(2)}) collective-permute-start(bf16[32,3072]{1,0:T(8,128)(2,1)S(1)} %get-tuple-element.73), channel_id=1, source_target_pairs={{16,1},{17,9},{18,5},{19,13},{24,17},{25,25},{26,21},{27,29}} | collective-permute-start | bytes 589832 | tf_op jit(solution)/shard_map/ppermute | solution.py:306
  19.4 2.0 %collective-permute-start.26 = (bf16[32,3072]{1,0:T(8,128)(2,1)S(1)}, bf16[32,3072]{1,0:T(8,128)(2,1)S(1)}, u32[]{:S(2)}, u32[]{:S(2)}) collective-permute-start(bf16[32,3072]{1,0:T(8,128)(2,1)S(1)} %get-tuple-element.74), channel_id=1, source_target_pairs={{16,2},{17,10},{18,6},{19,14},{24,18},{25,26},{26,22},{27,30}} | collective-permute-start | bytes 589832 | tf_op jit(solution)/shard_map/ppermute | solution.py:306
  20.1 81.2 %collective-permute-start.27 = (bf16[32,3072]{1,0:T(8,128)(2,1)S(1)}, bf16[32,3072]{1,0:T(8,128)(2,1)S(1)}, u32[]{:S(2)}, u32[]{:S(2)}) collective-permute-start(bf16[32,3072]{1,0:T(8,128)(2,1)S(1)} %get-tuple-element.75), channel_id=1, source_target_pairs={{16,3},{17,11},{18,7},{19,15},{24,19},{25,27},{26,23},{27,31}} | collective-permute-start | bytes 589832 | tf_op jit(solution)/shard_map/ppermute | solution.py:306
